TPU v7x, 256 devices: a whole 4x4x8 slice. The times are simulated.
256 devices in a mesh: dp: 32 (over y, x, core), mp: 8 (over z).
Axes of the slice: x: 4, y: 4, z: 8, core: 2. Of those that a mesh axis runs over, the one named last changes fastest.
Arguments:
- hidden: bfloat16 [16384, 28672], P('dp', 'mp'), may hold values from -6 to 6
- grad_out: bfloat16 [16384, 8192], P('dp', 'mp'), may hold values from -6 to 6
- basis: bfloat16 [28672, 512], P('mp'), may hold values from -0.03125 to 0.03125
- owners: int32 [256, 1], P('mp'), may hold values from 0 to 31; in each aligned block of 32 rows (0 to 31, 32 to 63, ...) at most 4 rows name the same one
- first_moment: float32 [32768, 512], P(('dp', 'mp')), may hold values from -6 to 6
- second_moment: float32 [32768, 512], P(('dp', 'mp')), may hold values from 0.25 to 4
Outputs:
- update: bfloat16 [28672, 8192], P('mp', 'dp')
- new_first: float32 [32768, 512], P(('dp', 'mp'))
- new_second: float32 [32768, 512], P(('dp', 'mp'))
Inputs may be any that keep to these rules, and one draw needn't show every extreme that they name: `owners`: among the 32 fragments of one index of mp no owner is named more than 4 times; in some of them an owner is named exactly 4 times; every owner is named somewhere.
All inputs are finite; a program needn't handle non-finite values.
Results may differ from a plain program's by a relative error of at most 0.0049.
Values may be sent and summed in bfloat16 or wider, within the bound.
No kernel may reach another device: no remote copies, remote signals or barrier semaphores. Data moves between devices by JAX's collectives and lax.ppermute only.
A program may use at most 64 MiB of HBM per device.

v0:
```python
import math

import jax
import jax.numpy as jnp
from jax import lax
from jax.sharding import PartitionSpec as P

FF = 28672
RANK = 512
FC = 32


first_keep = 0.9
first_take = 0.1
second_keep = 0.95
second_take = 0.05
adam_eps = 1e-08


def broadcast(value, axis, root):
    mine = lax.axis_index(axis) == root
    return lax.psum(jnp.where(mine, value, jnp.zeros_like(value)), axis)


def lookup(table, keys, table_size):
    match = keys[:, None] == jnp.arange(table_size, dtype=jnp.int32)[None, :]
    return jnp.sum(jnp.where(match, table[None, :], 0), axis=1)


def slot_tables(owner_ids, slots, owner_count):
    frag_count = owner_ids.shape[0]
    frag_index = jnp.arange(frag_count, dtype=jnp.int32)
    same = owner_ids[None, :] == owner_ids[:, None]
    before = frag_index[None, :] < frag_index[:, None]
    slot_of = jnp.sum((same & before).astype(jnp.int32), axis=1)
    key_of = owner_ids * slots + slot_of
    key_index = jnp.arange(owner_count * slots, dtype=jnp.int32)
    match = key_of[:, None] == key_index[None, :]
    source = jnp.sum(jnp.where(match, frag_index[:, None], 0), axis=0)
    filled = jnp.sum(match.astype(jnp.int32), axis=0)
    return (key_of, source, filled)


def body(hidden, grad_out, basis, owners, first_moment, second_moment):
    tok_rows = hidden.shape[0]
    owner_count = lax.axis_size("dp")
    shard_count = lax.axis_size("mp")
    col_rows = grad_out.shape[1]
    slots = first_moment.shape[0] // FC
    scale = 1.0 / math.sqrt(tok_rows * owner_count)
    owner_ids = owners[:, 0]
    key_of, source, filled = slot_tables(owner_ids, slots, owner_count)
    my_owner = lax.axis_index("dp")
    my_filled = lax.dynamic_slice_in_dim(filled, my_owner * slots, slots)
    within = jnp.arange(FC, dtype=jnp.int32)
    partial_value = jnp.dot(hidden, basis, preferred_element_type=jnp.float32)
    coeffs = lax.psum(partial_value, "mp").astype(jnp.bfloat16)
    local_proj = (
        lax.dot_general(
            grad_out, coeffs, (((0,), (0,)), ((), ())), preferred_element_type=jnp.float32
        )
        * scale
    )
    key_total = owner_count * slots
    buffer_rows = jnp.arange(slots * FC * lax.axis_size("dp"), dtype=jnp.int32)
    keys = buffer_rows // FC
    source_rows = lookup(source, keys, key_total) * FC + buffer_rows % FC
    live = lookup(filled, keys, key_total) > 0
    picked = jnp.take(local_proj, source_rows, axis=0)
    totals = lax.psum_scatter(
        jnp.where(live[:, None], picked, 0.0), "dp", scatter_dimension=0, tiled=True
    )
    live_rows = (jnp.repeat(my_filled, FC) > 0)[:, None]
    blend_first = first_keep * first_moment + first_take * totals
    blend_second = second_keep * second_moment + second_take * totals * totals
    new_first = jnp.where(live_rows, blend_first, first_moment)
    new_second = jnp.where(live_rows, blend_second, second_moment)
    factor = jnp.where(live_rows, new_first / (jnp.sqrt(new_second) + adam_eps), 0.0).astype(
        jnp.bfloat16
    )
    everyone = lax.all_gather(factor, "dp", axis=0, tiled=True)
    frag_rows = (key_of[:, None] * FC + within[None, :]).reshape(-1)
    ordered = jnp.take(everyone, frag_rows, axis=0)
    block_rows = col_rows * shard_count // owner_count
    first_row = my_owner * block_rows
    root_shard = first_row // col_rows
    candidate = lax.dynamic_slice_in_dim(ordered, first_row % col_rows, block_rows, 0)
    chosen = broadcast(candidate, "mp", root_shard)
    update = lax.dot_general(
        basis, chosen, (((1,), (1,)), ((), ())), preferred_element_type=jnp.float32
    )
    update = (update * math.sqrt(FF / RANK)).astype(jnp.bfloat16)
    return (update, new_first, new_second)


def solution(mesh):
    placed = (
        P("dp", "mp"),
        P("dp", "mp"),
        P("mp", None),
        P("mp", None),
        P(("dp", "mp"), None),
        P(("dp", "mp"), None),
    )
    return jax.shard_map(
        body,
        mesh=mesh,
        in_specs=placed,
        out_specs=(P("mp", "dp"), P(("dp", "mp"), None), P(("dp", "mp"), None)),
        check_vma=False,
    )
```

profile of v0, /device:TPU:1, one launch (start us, length us, event | category | flops | bytes accessed | tf_op | source)
XLA Modules:
  0.0 348.5 jit_solution(18415024637539920597)
XLA Ops:
  7.2 0.0 copy-start
  7.2 0.0 reduce-scatter.2.cloned.1.call-start
  7.2 0.9 convert_reduce_fusion.1
  8.2 0.7 multiply_bitcast_fusion.1
  8.8 0.1 convert_reduce_fusion
  8.9 1.8 select_reduce_fusion.1
  10.8 5.2 %fusion.18 = f32[512,512]{1,0:T(8,128)S(1)} fusion(bf16[512,3584]{1,0:T(8,128)(2,1)} %param.6, bf16[3584,512]{1,0:T(8,128)(2,1)} %param.8), kind=kOutput, calls=%fused_computation.53 | convolution fusion | flops 1879048192 | bytes 8388608 | tf_op jit(solution)/shard_map/dot_general | solution.py:56
  16.1 52.7 %all-reduce.4 = bf16[512,512]{1,0:T(8,128)(2,1)S(1)} all-reduce(f32[512,512]{1,0:T(8,128)S(1)} %fusion.18), channel_id=1, replica_groups=mesh['dp'=32,'mp'=8] {'mp'}, use_global_device_ids=true, to_apply=%region_5.6 | all-reduce | flops 262144 | bytes 1572864 | tf_op jit(solution)/shard_map/psum | solution.py:57
  68.7 2.1 multiply_bitcast_fusion
  70.8 1.9 copy.13
  72.8 16.8 %gather_fusion = f32[4096,512]{1,0:T(8,128)} fusion(f32[1024,512]{1,0:T(8,128)S(1)} %copy.13, s32[4096]{0:T(1024)S(1)} %broadcast_clamp_fusion), kind=kCustom, calls=%fused_computation | custom fusion | bytes 16793600 | tf_op jit(solution)/shard_map/jit(_take)/gather | solution.py:69
  89.5 7.4 %select_select_fusion = f32[4096,512]{1,0:T(8,128)} fusion(f32[4096,512]{1,0:T(8,128)} %gather_fusion, pred[4096]{0:T(1024)(128)(4,1)S(1)} %get-tuple-element.21, pred[4096]{0:T(1024)(128)(4,1)S(1)} %get-tuple-element.22), kind=kLoop, calls=%fused_computation.2 | loop fusion | flops 4194304 | bytes 16785408 | tf_op jit(solution)/shard_map/jit(_where)/select_n | solution.py:71
  97.0 0.0 reduce-scatter.2.cloned.1.call-update
  97.0 0.0 all-gather.2.cloned.1.call-start
  97.1 0.1 dynamic-slice_compare_fusion
  97.1 0.1 broadcast_in_dim.105
  97.2 0.1 gt.24
  97.3 108.3 %reduce-scatter.2.cloned.1.call-done = f32[128,512]{1,0:T(8,128)} async-done(((f32[4096,512]{1,0:T(8,128)}), f32[128,512]{1,0:T(8,128)}) %reduce-scatter.2.cloned.1.call-update) | async-done | bytes 262160 | tf_op jit(solution)/shard_map/reduce_scatter | solution.py:70
  205.7 2.0 select_convert_fusion
  207.6 0.0 all-gather.2.cloned.1.call-update
  207.7 0.0 all-reduce.3.cloned.1.call-start
  207.7 0.1 iota_add_fusion
  207.8 0.1 add.161
  207.9 0.1 add.145
  208.0 0.1 dynamic-slice
  208.1 53.6 %all-gather.2.cloned.1.call-done = bf16[4096,512]{1,0:T(8,128)(2,1)} async-done(((bf16[128,512]{1,0:T(8,128)(2,1)}), bf16[4096,512]{1,0:T(8,128)(2,1)}) %all-gather.2.cloned.1.call-update) | async-done | bytes 4194320 | tf_op jit(solution)/shard_map/all_gather | solution.py:81
  261.7 6.7 %gather_fusion.1 = bf16[1024,512]{1,0:T(8,128)(2,1)S(1)} fusion(bf16[4096,512]{1,0:T(8,128)(2,1)} %all-gather.2.cloned.1.call-done, s32[1024]{0:T(1024)S(1)} %broadcast_clamp_fusion.1), kind=kCustom, calls=%fused_computation.1 | custom fusion | bytes 2101248 | tf_op jit(solution)/shard_map/jit(_take)/gather | solution.py:83
  268.4 0.8 fusion.5
  269.3 0.0 all-reduce.3.cloned.1.call-update
  269.3 67.1 %all-reduce.3.cloned.1.call-done = bf16[256,512]{1,0:T(8,128)(2,1)} async-done(((bf16[256,512]{1,0:T(8,128)(2,1)}), bf16[256,512]{1,0:T(8,128)(2,1)}) %all-reduce.3.cloned.1.call-update) | async-done | bytes 262160 | tf_op jit(solution)/shard_map/psum | solution.py:22
  336.4 3.3 fusion.1
  339.7 2.3 copy.14
  (13 shorter events, 0.1 us)
Async XLA Ops:
  7.2 61.6 %copy-start = (bf16[512,1024]{1,0:T(8,128)(2,1)S(1)}, bf16[512,1024]{1,0:T(8,128)(2,1)}, u32[]{:S(2)}) copy-start(bf16[512,1024]{1,0:T(8,128)(2,1)} %param.7) | copy-start | bytes 3145732
  7.2 198.5 %reduce-scatter.2.cloned.1.call-start = ((), (), s32[]{:S(2)}) async-start(), calls=%async_computation.1 | async-start | bytes 8650752 | tf_op jit(solution)/shard_map/reduce_scatter | solution.py:70
  97.0 108.7 %copy-start.1 = (f32[128,512]{1,0:T(8,128)S(1)}, f32[128,512]{1,0:T(8,128)}, u32[]{:S(2)}) copy-start(f32[128,512]{1,0:T(8,128)} %param.11) | copy-start | bytes 786436
  97.0 108.7 %copy-start.2 = (f32[128,512]{1,0:T(8,128)S(1)}, f32[128,512]{1,0:T(8,128)}, u32[]{:S(2)}) copy-start(f32[128,512]{1,0:T(8,128)} %param.10) | copy-start | bytes 786436
  97.0 164.7 %all-gather.2.cloned.1.call-start = ((), (), s32[]{:S(2)}) async-start(), calls=%async_computation.2 | async-start | bytes 4325376 | tf_op jit(solution)/shard_map/all_gather | solution.py:81
  207.7 128.7 %all-reduce.3.cloned.1.call-start = ((), (), s32[]{:S(2)}) async-start(), calls=%async_computation.3 | async-start | bytes 524288 | tf_op jit(solution)/shard_map/psum | solution.py:22
Sparse Core Ops, SparseCore 0:
  97.1 108.4 reduce-scatter.1
  209.1 52.5 all-gather.1
  269.4 66.9 all-reduce.2
where the time goes:
time: 352 us; the launch traced here: 348 us
  waiting for transfers between devices  229 us (65%)
  blocking collectives  52.7 us (15%)
  local copies, waits for them, and re-layouts  28.1 us (8%)
  other arithmetic  14 us (4%)
  between operations  13.9 us (4%)
  matrix products  10.6 us (3%)
    reduce_scatter x1, waiting for transfers between devices, body(): lax.psum_scatter(jnp.where(live[:, None], picked, 0.0), 'dp', scatter_dim...  108 us
    psum x1, waiting for transfers between devices, broadcast(): return lax.psum(jnp.where(mine, value, jnp.zeros_like(value)), axis)  67.1 us
    all_gather x1, waiting for transfers between devices, body(): everyone = lax.all_gather(factor, 'dp', axis=0, tiled=True)  53.6 us
    psum x1, blocking collectives, body(): coeffs = lax.psum(partial_value, 'mp').astype(jnp.bfloat16)  52.7 us
    gather x1, local copies, waits for them, and re-layouts, body(): picked = jnp.take(local_proj, source_rows, axis=0)  16.8 us
    select_n x1, other arithmetic, body(): jnp.where(live[:, None], picked, 0.0)  7.43 us
  transfers between devices with their start and end apart: 3, of which 3 were waited for; matrix products, arithmetic and copies ran while one was open for 0% of the time, Pallas kernels for 0%

commit v1 on v0

v1 whole, which is shorter than its diff:
```python
import math

import jax
import jax.numpy as jnp
from jax import lax
from jax.sharding import PartitionSpec as P

FF = 28672
RANK = 512
FC = 32

first_keep = 0.9
first_take = 0.1
second_keep = 0.95
second_take = 0.05
adam_eps = 1e-08

bf16 = jnp.bfloat16
f32 = jnp.float32


def body(hidden, grad_out, basis, owners, first_moment, second_moment):
    owner_count = lax.axis_size("dp")
    planes = lax.axis_size("mp")
    chips = owner_count // 2
    tok, col = grad_out.shape
    slots = first_moment.shape[0] // FC
    frags = owners.shape[0]
    block = col * planes // owner_count
    per_block = block // FC
    piece = block // chips
    pairs = col // block // 2
    scale = 1.0 / math.sqrt(tok * owner_count)
    same_core = [[2 * k + c for k in range(chips)] for c in range(2)]
    swap = [(i, i ^ 1) for i in range(owner_count)]

    def other_core(x):
        return lax.ppermute(x, "dp", swap)

    def over_chips(x):
        return lax.all_to_all(x, "dp", 0, 0, axis_index_groups=same_core, tiled=True)

    def over_planes(x):
        return lax.all_to_all(x, "mp", 0, 0, tiled=True)

    me = lax.axis_index("dp")
    core = me % 2
    chip = me // 2

    raw = jnp.concatenate([first_moment.astype(bf16), second_moment.astype(bf16)], axis=1)
    raw = jnp.concatenate([raw, other_core(raw)], axis=0)

    go = grad_out.reshape(tok, pairs, 2, block)
    go_mine = lax.dynamic_slice_in_dim(go, core, 1, 2).reshape(tok, pairs * block)
    go_theirs = lax.dynamic_slice_in_dim(go, 1 - core, 1, 2).reshape(tok, pairs * block)
    go_both = jnp.concatenate([go_mine, other_core(go_theirs)], axis=0)

    ids = owners[:, 0]
    order = jnp.arange(frags, dtype=jnp.int32)
    same = ids[None, :] == ids[:, None]
    slot_of = jnp.sum((same & (order[None, :] < order[:, None])).astype(jnp.int32), axis=1)

    k_of = jnp.arange(chips, dtype=jnp.int32)[:, None]
    p_of = jnp.arange(pairs, dtype=jnp.int32)[None, :]
    parts = FC // piece
    half = chips // per_block
    frag = (core + 2 * p_of) * per_block + k_of // half
    base = (ids % 2 != core).astype(jnp.int32) * slots * FC + slot_of * FC
    pick = (frag.reshape(-1)[:, None] == order[None, :]).astype(jnp.int32)
    start = jnp.sum(pick * base[None, :], axis=1).reshape(chips, pairs) + (k_of % half) * piece
    rows = (start[:, :, None] + jnp.arange(piece, dtype=jnp.int32)).reshape(-1)
    hot = (rows[:, None] == jnp.arange(raw.shape[0], dtype=jnp.int32)[None, :]).astype(bf16)
    moments = jnp.dot(hot, raw, preferred_element_type=f32).astype(bf16)
    moments = moments.reshape(chips, pairs * piece, 2 * RANK)

    part = jnp.dot(hidden, basis, preferred_element_type=f32).astype(bf16)
    part = over_planes(part).reshape(planes, tok // planes, RANK)
    mine = jnp.sum(part.astype(f32), axis=0).astype(bf16)
    coeffs = over_planes(jnp.broadcast_to(mine[None], part.shape).reshape(tok, RANK))
    both = jnp.concatenate([coeffs, other_core(coeffs)], axis=0)

    proj = lax.dot_general(go_both, both, (((0,), (0,)), ((), ())), preferred_element_type=f32)
    proj = (proj * scale).astype(bf16).reshape(pairs, chips, piece, RANK)
    proj = proj.transpose(1, 0, 2, 3).reshape(chips, pairs * piece, RANK)
    got = over_chips(jnp.concatenate([proj, moments], axis=2))
    grad = jnp.sum(got[:, :, :RANK].astype(f32), axis=0)
    old = []
    for p in range(pairs):
        q = (core + 2 * p) * per_block + chip // half
        from_chip = jnp.sum(jnp.where(order == q, ids, 0)) // 2
        old.append(
            lax.dynamic_slice(
                got, (from_chip, p * piece, RANK), (1, piece, 2 * RANK)
            )[0]
        )
    old = jnp.concatenate(old, axis=0).astype(f32)
    blend_first = first_keep * old[:, :RANK] + first_take * grad
    blend_second = second_keep * old[:, RANK:] + second_take * grad * grad
    factor = (blend_first / (jnp.sqrt(blend_second) + adam_eps)).astype(bf16)

    spread = over_planes(jnp.broadcast_to(factor[None], (planes, pairs * piece, RANK)))
    spread = spread.reshape(chips, piece, RANK)
    grad_bf = jnp.broadcast_to(grad.astype(bf16)[None], (chips, pairs * piece, RANK))
    last = over_chips(jnp.concatenate([spread, grad_bf], axis=1))
    chosen = last[:, :piece].reshape(block, RANK)
    update = lax.dot_general(basis, chosen, (((1,), (1,)), ((), ())), preferred_element_type=f32)
    update = (update * math.sqrt(FF / RANK)).astype(bf16)

    sums = last[:, piece:].reshape(chips * pairs * piece, RANK)
    sums = jnp.concatenate([sums, other_core(sums)], axis=0)
    key = jnp.arange(slots, dtype=jnp.int32)
    mine_slot = (ids[None, :] == me) & (slot_of[None, :] == key[:, None])
    filled = jnp.any(mine_slot, axis=1)
    source = jnp.sum(jnp.where(mine_slot, order[None, :], 0), axis=1)
    b = source // per_block
    within = jnp.arange(FC, dtype=jnp.int32)
    k = ((source % per_block) * half)[:, None] + (within // piece)[None, :]
    row = k * (pairs * piece) + ((b // 2) * piece)[:, None] + (within % piece)[None, :]
    row = row + ((b % 2 != core).astype(jnp.int32) * chips * pairs * piece)[:, None]
    row = jnp.where(filled[:, None], row, -1).reshape(-1)
    hot2 = (row[:, None] == jnp.arange(sums.shape[0], dtype=jnp.int32)[None, :]).astype(bf16)
    totals = jnp.dot(hot2, sums, preferred_element_type=f32)
    live = jnp.repeat(filled, FC)[:, None]
    new_first = jnp.where(live, first_keep * first_moment + first_take * totals, first_moment)
    new_second = jnp.where(
        live, second_keep * second_moment + second_take * totals * totals, second_moment
    )
    return (update, new_first, new_second)


def solution(mesh):
    placed = (
        P("dp", "mp"),
        P("dp", "mp"),
        P("mp", None),
        P("mp", None),
        P(("dp", "mp"), None),
        P(("dp", "mp"), None),
    )
    return jax.shard_map(
        body,
        mesh=mesh,
        in_specs=placed,
        out_specs=(P("mp", "dp"), P(("dp", "mp"), None), P(("dp", "mp"), None)),
        check_vma=False,
    )
```

time: 352 us -> 137 us (0.39)
  waiting for transfers between devices: 229 us -> 73.7 us
  blocking collectives: 52.7 us -> 0 us
  starting transfers between devices: 0.12 us -> 33.8 us
  local copies, waits for them, and re-layouts: 28.1 us -> 5.12 us
  other arithmetic: 14 us -> 4.08 us
  between operations: 13.9 us -> 6.09 us
    reduce_scatter x1 -> x0, waiting for transfers between devices: 108 us -> none  [body(): lax.psum_scatter(jnp.where(live[:, None], picked, 0.0), 'dp', scatter_dim...]
    all_to_all x0 -> x5, waiting for transfers between devices: none -> 72.8 us  [the longest x3 41.5 us: over_planes(): return lax.all_to_all(x, 'mp', 0, 0, tiled=True)]
    psum x1 -> x0, waiting for transfers between devices: 67.1 us -> none  [broadcast(): return lax.psum(jnp.where(mine, value, jnp.zeros_like(value)), axis)]
    all_gather x1 -> x0, waiting for transfers between devices: 53.6 us -> none  [body(): everyone = lax.all_gather(factor, 'dp', axis=0, tiled=True)]
    psum x1 -> x0, blocking collectives: 52.7 us -> none  [body(): coeffs = lax.psum(partial_value, 'mp').astype(jnp.bfloat16)]
    all_to_all x0 -> x5, starting transfers between devices: none -> 29.3 us  [the longest x3 15.9 us: over_planes(): return lax.all_to_all(x, 'mp', 0, 0, tiled=True)]
    gather x2 -> x0, local copies, waits for them, and re-layouts: 23.5 us -> none  [the longest x1 16.8 us: body(): picked = jnp.take(local_proj, source_rows, axis=0)]
    select_n x5 -> x3, other arithmetic: 8.32 us -> 0.01 us  [the longest x1 0.01 us: body(): frag = (core + 2 * p_of) * per_block + k_of // half]
  transfers between devices with their start and end apart: 3 -> 9, of which waited for: 3 -> 6; matrix products, arithmetic and copies ran while one was open for 0% -> 7% of each run, Pallas kernels for 0% -> 0%
where the time goes in v1:
time: 137 us
  waiting for transfers between devices  73.7 us (54%)
  starting transfers between devices  33.8 us (25%)
  matrix products  13.9 us (10%)
  between operations  6.09 us (4%)
  local copies, waits for them, and re-layouts  5.12 us (4%)
  other arithmetic  4.08 us (3%)
    all_to_all x3, waiting for transfers between devices, over_planes(): return lax.all_to_all(x, 'mp', 0, 0, tiled=True)  41.5 us
    all_to_all x2, waiting for transfers between devices, over_chips(): lax.all_to_all(x, 'dp', 0, 0, axis_index_groups=same_core, tiled=True)  31.3 us
    all_to_all x3, starting transfers between devices, over_planes(): return lax.all_to_all(x, 'mp', 0, 0, tiled=True)  15.9 us
    all_to_all x2, starting transfers between devices, over_chips(): lax.all_to_all(x, 'dp', 0, 0, axis_index_groups=same_core, tiled=True)  13.4 us
    dot_general x1, matrix products, body(): part = jnp.dot(hidden, basis, preferred_element_type=f32).astype(bf16)  6.08 us
    ppermute x4, starting transfers between devices, other_core(): return lax.ppermute(x, 'dp', swap)  4.55 us
    dot_general x1, matrix products, body(): lax.dot_general(basis, chosen, (((1,), (1,)), ((), ())), preferred_elemen...  3.19 us
    unnamed x10, local copies, waits for them, and re-layouts  2.84 us
  transfers between devices with their start and end apart: 9, of which 6 were waited for; matrix products, arithmetic and copies ran while one was open for 7% of the time, Pallas kernels for 0%

profile of v1, /device:TPU:1, one launch (start us, length us, event | category | flops | bytes accessed | tf_op | source)
XLA Modules:
  0.0 136.7 jit_solution(8471350400699682127)
XLA Ops:
  0.6 6.1 %convolution_convert_fusion.1 = bf16[512,512]{1,0:T(8,128)(2,1)} fusion(bf16[512,3584]{1,0:T(8,128)(2,1)} %param.6, bf16[3584,512]{1,0:T(8,128)(2,1)} %param.8), kind=kOutput, calls=%fused_computation.7 | convolution fusion | flops 1879310336 | bytes 7864320 | tf_op jit(solution)/shard_map/dot_general | solution.py:76
  6.7 9.0 %all-to-all-start = ((bf16[8,64,512]{2,1,0:T(8,128)(2,1)}), bf16[8,64,512]{2,1,0:T(8,128)(2,1)S(1)}, u32[]{:S(2)}, u32[]{:S(2)}) async-start(bf16[8,64,512]{2,1,0:T(8,128)(2,1)} %bitcast.3), calls=%async_computation | async-start | bytes 1048576 | tf_op jit(solution)/shard_map/all_to_all | solution.py:44
  15.8 0.5 copy.15
  16.4 1.0 collective-permute-start
  17.5 16.2 %all-to-all-done = bf16[8,64,512]{2,1,0:T(8,128)(2,1)S(1)} async-done(((bf16[8,64,512]{2,1,0:T(8,128)(2,1)}), bf16[8,64,512]{2,1,0:T(8,128)(2,1)S(1)}, u32[]{:S(2)}, u32[]{:S(2)}) %all-to-all-start) | async-done | bytes 524320 | tf_op jit(solution)/shard_map/all_to_all | solution.py:44
  33.8 0.8 broadcast_in_dim.39
  34.6 3.5 %all-to-all-start.1 = ((bf16[8,64,512]{2,1,0:T(8,128)(2,1)}), bf16[8,64,512]{2,1,0:T(8,128)(2,1)S(1)}, u32[]{:S(2)}, u32[]{:S(2)}) async-start(bf16[8,64,512]{2,1,0:T(8,128)(2,1)} %broadcast_in_dim.39), calls=%async_computation.1 | async-start | bytes 1048576 | tf_op jit(solution)/shard_map/all_to_all | solution.py:44
  38.1 0.6 collective-permute-start.2
  38.9 0.2 convert_reduce_fusion.1
  39.1 0.6 fusion.33
  39.7 0.2 select_reduce_fusion
  40.0 16.0 %all-to-all-done.1 = bf16[8,64,512]{2,1,0:T(8,128)(2,1)S(1)} async-done(((bf16[8,64,512]{2,1,0:T(8,128)(2,1)}), bf16[8,64,512]{2,1,0:T(8,128)(2,1)S(1)}, u32[]{:S(2)}, u32[]{:S(2)}) %all-to-all-start.1) | async-done | bytes 524320 | tf_op jit(solution)/shard_map/all_to_all | solution.py:44
  56.0 0.5 collective-permute-start.1
  56.6 0.1 add.265
  56.7 0.5 convolution_convert_fusion
  57.2 0.9 collective-permute-done.1
  58.1 1.9 %fusion.2 = bf16[512,512]{1,0:T(8,128)(2,1)S(1)} fusion(bf16[512,512]{0,1:T(8,128)(2,1)} %collective-permute-done, bf16[512,512]{0,1:T(8,128)(2,1)S(1)} %bitcast.37, bf16[512,512]{1,0:T(8,128)(2,1)} %collective-permute-done.1, bf16[512,512]{1,0:T(8,128)(2,1)S(1)} %bitcast.33), kind=kOutput, calls=%fused_computation.6 | convolution fusion | flops 541589504 | bytes 2621440 | tf_op jit(solution)/shard_map/dot_general | solution.py:82
  60.1 1.3 pad_maximum_fusion
  61.4 6.8 %all-to-all-start.2 = ((bf16[16,32,1536]{2,1,0:T(8,128)(2,1)}), bf16[16,32,1536]{2,1,0:T(8,128)(2,1)S(1)}, u32[]{:S(2)}, u32[]{:S(2)}) async-start(bf16[16,32,1536]{2,1,0:T(8,128)(2,1)} %pad_maximum_fusion), calls=%async_computation.2 | async-start | bytes 3145728 | tf_op jit(solution)/shard_map/all_to_all | solution.py:41
  73.3 18.7 %all-to-all-done.2 = bf16[16,32,1536]{2,1,0:T(8,128)(2,1)S(1)} async-done(((bf16[16,32,1536]{2,1,0:T(8,128)(2,1)}), bf16[16,32,1536]{2,1,0:T(8,128)(2,1)S(1)}, u32[]{:S(2)}, u32[]{:S(2)}) %all-to-all-start.2) | async-done | bytes 1572896 | tf_op jit(solution)/shard_map/all_to_all | solution.py:41
  92.2 0.7 broadcast_in_dim.40
  93.0 3.4 %all-to-all-start.3 = ((bf16[8,32,512]{2,1,0:T(8,128)(2,1)}), bf16[8,32,512]{2,1,0:T(8,128)(2,1)S(1)}, u32[]{:S(2)}, u32[]{:S(2)}) async-start(bf16[8,32,512]{2,1,0:T(8,128)(2,1)} %broadcast_in_dim.40), calls=%async_computation.3 | async-start | bytes 524288 | tf_op jit(solution)/shard_map/all_to_all | solution.py:44
  96.4 0.1 select_reduce_fusion.1
  96.5 9.3 %all-to-all-done.3 = bf16[8,32,512]{2,1,0:T(8,128)(2,1)S(1)} async-done(((bf16[8,32,512]{2,1,0:T(8,128)(2,1)}), bf16[8,32,512]{2,1,0:T(8,128)(2,1)S(1)}, u32[]{:S(2)}, u32[]{:S(2)}) %all-to-all-start.3) | async-done | bytes 262176 | tf_op jit(solution)/shard_map/all_to_all | solution.py:44
  105.9 0.9 pad_maximum_fusion.1
  106.8 6.6 %all-to-all-start.4 = ((bf16[16,48,512]{2,1,0:T(8,128)(2,1)}), bf16[16,48,512]{2,1,0:T(8,128)(2,1)S(1)}, u32[]{:S(2)}, u32[]{:S(2)}) async-start(bf16[16,48,512]{2,1,0:T(8,128)(2,1)} %pad_maximum_fusion.1), calls=%async_computation.4 | async-start | bytes 1572864 | tf_op jit(solution)/shard_map/all_to_all | solution.py:41
  113.7 0.1 fusion.30
  113.9 12.6 %all-to-all-done.4 = bf16[16,48,512]{2,1,0:T(8,128)(2,1)S(1)} async-done(((bf16[16,48,512]{2,1,0:T(8,128)(2,1)}), bf16[16,48,512]{2,1,0:T(8,128)(2,1)S(1)}, u32[]{:S(2)}, u32[]{:S(2)}) %all-to-all-start.4) | async-done | bytes 786464 | tf_op jit(solution)/shard_map/all_to_all | solution.py:41
  126.6 2.4 %collective-permute-start.3 = (bf16[512,512]{1,0:T(8,128)(2,1)S(1)}, bf16[512,512]{1,0:T(8,128)(2,1)}, u32[]{:S(2)}, u32[]{:S(2)}) collective-permute-start(bf16[512,512]{1,0:T(8,128)(2,1)S(1)} %bitcast.34), channel_id=1, source_target_pairs={{0,8},{8,0},{16,24},{24,16},{32,40},{40,32},{48,56},{56,48},{64,72... | collective-permute-start | bytes 1572872 | tf_op jit(solution)/shard_map/ppermute | solution.py:38
  129.0 3.2 %fusion.1 = bf16[3584,256]{0,1:T(8,128)(2,1)S(1)} fusion(bf16[256,512]{1,0:T(8,128)(2,1)S(1)} %bitcast.39, bf16[3584,512]{1,0:T(8,128)(2,1)} %param.8), kind=kOutput, calls=%fused_computation.2 | convolution fusion | flops 941359104 | bytes 5767168 | tf_op jit(solution)/shard_map/dot_general | solution.py:106
  132.2 2.3 %copy.17 = bf16[3584,256]{1,0:T(8,128)(2,1)} copy(bf16[3584,256]{0,1:T(8,128)(2,1)S(1)} %fusion.1) | data formatting | bytes 3670016
  134.5 2.2 %fusion.19 = (f32[128,512]{1,0:T(8,128)}, f32[128,512]{1,0:T(8,128)}) fusion(f32[128,512]{1,0:T(8,128)S(1)} %copy-done.1, pred[128]{0:T(512)(128)(4,1)S(1)} %broadcast_in_dim.43, f32[128,512]{1,0:T(8,128)S(1)} %copy-done.2, bf16[512,512]{1,0:T(8,128)(2,1)} %collective-permute-done.3, bf16[512,512]{1,0:T(8,128)(2,1)S(1)} %bitcast.35, ...), kind=kOutput, calls=%fused_computation.29 | convolution fusion | flops 137035776 | bytes 2097792 | tf_op jit(solution)/shard_map/dot_general | solution.py:122
  (40 shorter events, 1.3 us)
Async XLA Ops:
  0.6 15.1 %copy-start = (bf16[512,1024]{1,0:T(8,128)(2,1)S(1)}, bf16[512,1024]{1,0:T(8,128)(2,1)}, u32[]{:S(2)}) copy-start(bf16[512,1024]{1,0:T(8,128)(2,1)} %param.7) | copy-start | bytes 3145732
  6.7 27.0 %all-to-all-start = ((bf16[8,64,512]{2,1,0:T(8,128)(2,1)}), bf16[8,64,512]{2,1,0:T(8,128)(2,1)S(1)}, u32[]{:S(2)}, u32[]{:S(2)}) async-start(bf16[8,64,512]{2,1,0:T(8,128)(2,1)} %bitcast.3), calls=%async_computation | async-start | bytes 1048576 | tf_op jit(solution)/shard_map/all_to_all | solution.py:44
  15.7 1.7 %copy-start.2 = (f32[128,512]{1,0:T(8,128)S(1)}, f32[128,512]{1,0:T(8,128)}, u32[]{:S(2)}) copy-start(f32[128,512]{1,0:T(8,128)} %param.10) | copy-start | bytes 786436
  15.8 1.7 %copy-start.1 = (f32[128,512]{1,0:T(8,128)S(1)}, f32[128,512]{1,0:T(8,128)}, u32[]{:S(2)}) copy-start(f32[128,512]{1,0:T(8,128)} %param.11) | copy-start | bytes 786436
  16.4 22.5 %copy-start.3 = (s32[32,1]{0,1:T(1,128)S(1)}, s32[32,1]{0,1:T(1,128)}, u32[]{:S(2)}) copy-start(s32[32,1]{0,1:T(1,128)} %param.9) | copy-start | bytes 388
  16.4 40.8 %collective-permute-start = (bf16[512,512]{0,1:T(8,128)(2,1)S(1)}, bf16[512,512]{0,1:T(8,128)(2,1)}, u32[]{:S(2)}, u32[]{:S(2)}) collective-permute-start(bf16[512,512]{0,1:T(8,128)(2,1)S(1)} %bitcast.38), channel_id=1, source_target_pairs={{0,8},{8,0},{16,24},{24,16},{32,40},{40,32},{48,56},{56,48},{64,72... | collective-permute-start | bytes 1572872 | tf_op jit(solution)/shard_map/ppermute | solution.py:38
  34.6 21.4 %all-to-all-start.1 = ((bf16[8,64,512]{2,1,0:T(8,128)(2,1)}), bf16[8,64,512]{2,1,0:T(8,128)(2,1)S(1)}, u32[]{:S(2)}, u32[]{:S(2)}) async-start(bf16[8,64,512]{2,1,0:T(8,128)(2,1)} %broadcast_in_dim.39), calls=%async_computation.1 | async-start | bytes 1048576 | tf_op jit(solution)/shard_map/all_to_all | solution.py:44
  38.1 18.6 %collective-permute-start.2 = (bf16[128,1024]{1,0:T(8,128)(2,1)S(1)}, bf16[128,1024]{1,0:T(8,128)(2,1)S(1)}, u32[]{:S(2)}, u32[]{:S(2)}) collective-permute-start(bf16[128,1024]{1,0:T(8,128)(2,1)S(1)} %pad_maximum_fusion.2), channel_id=1, source_target_pairs={{0,8},{8,0},{16,24},{24,16},{32,40},{40,32},{48,56},{56,48},{64,72... | collective-permute-start | bytes 786440 | tf_op jit(solution)/shard_map/ppermute | solution.py:38
  56.0 2.2 %collective-permute-start.1 = (bf16[512,512]{1,0:T(8,128)(2,1)S(1)}, bf16[512,512]{1,0:T(8,128)(2,1)}, u32[]{:S(2)}, u32[]{:S(2)}) collective-permute-start(bf16[512,512]{1,0:T(8,128)(2,1)S(1)} %bitcast.32), channel_id=1, source_target_pairs={{0,8},{8,0},{16,24},{24,16},{32,40},{40,32},{48,56},{56,48},{64,72... | collective-permute-start | bytes 1572872 | tf_op jit(solution)/shard_map/ppermute | solution.py:38
  61.4 30.7 %all-to-all-start.2 = ((bf16[16,32,1536]{2,1,0:T(8,128)(2,1)}), bf16[16,32,1536]{2,1,0:T(8,128)(2,1)S(1)}, u32[]{:S(2)}, u32[]{:S(2)}) async-start(bf16[16,32,1536]{2,1,0:T(8,128)(2,1)} %pad_maximum_fusion), calls=%async_computation.2 | async-start | bytes 3145728 | tf_op jit(solution)/shard_map/all_to_all | solution.py:41
  93.0 12.9 %all-to-all-start.3 = ((bf16[8,32,512]{2,1,0:T(8,128)(2,1)}), bf16[8,32,512]{2,1,0:T(8,128)(2,1)S(1)}, u32[]{:S(2)}, u32[]{:S(2)}) async-start(bf16[8,32,512]{2,1,0:T(8,128)(2,1)} %broadcast_in_dim.40), calls=%async_computation.3 | async-start | bytes 524288 | tf_op jit(solution)/shard_map/all_to_all | solution.py:44
  106.8 19.7 %all-to-all-start.4 = ((bf16[16,48,512]{2,1,0:T(8,128)(2,1)}), bf16[16,48,512]{2,1,0:T(8,128)(2,1)S(1)}, u32[]{:S(2)}, u32[]{:S(2)}) async-start(bf16[16,48,512]{2,1,0:T(8,128)(2,1)} %pad_maximum_fusion.1), calls=%async_computation.4 | async-start | bytes 1572864 | tf_op jit(solution)/shard_map/all_to_all | solution.py:41
  126.6 7.9 %collective-permute-start.3 = (bf16[512,512]{1,0:T(8,128)(2,1)S(1)}, bf16[512,512]{1,0:T(8,128)(2,1)}, u32[]{:S(2)}, u32[]{:S(2)}) collective-permute-start(bf16[512,512]{1,0:T(8,128)(2,1)S(1)} %bitcast.34), channel_id=1, source_target_pairs={{0,8},{8,0},{16,24},{24,16},{32,40},{40,32},{48,56},{56,48},{64,72... | collective-permute-start | bytes 1572872 | tf_op jit(solution)/shard_map/ppermute | solution.py:38

commit v2 on v1

v2 whole, which is shorter than its diff:
```python
import math

import jax
import jax.numpy as jnp
from jax import lax
from jax.sharding import PartitionSpec as P

FF = 28672
RANK = 512
FC = 32

first_keep = 0.9
first_take = 0.1
second_keep = 0.95
second_take = 0.05
adam_eps = 1e-08

bf16 = jnp.bfloat16
f32 = jnp.float32


def over(exchange, x, *rest):
    x, rest = lax.optimization_barrier((x, rest))
    return lax.optimization_barrier((exchange(x), rest))


def body(hidden, grad_out, basis, owners, first_moment, second_moment):
    owner_count = lax.axis_size("dp")
    planes = lax.axis_size("mp")
    chips = owner_count // 2
    tok, col = grad_out.shape
    slots = first_moment.shape[0] // FC
    frags = owners.shape[0]
    block = col * planes // owner_count
    per_block = block // FC
    piece = block // chips
    pairs = col // block // 2
    half = chips // per_block
    share = pairs * piece
    scale = 1.0 / math.sqrt(tok * owner_count)
    same_core = [[2 * k + c for k in range(chips)] for c in range(2)]
    swap = [(i, i ^ 1) for i in range(owner_count)]

    def other_core(x):
        return lax.ppermute(x, "dp", swap)

    def over_chips(x):
        return lax.all_to_all(x, "dp", 0, 0, axis_index_groups=same_core, tiled=True)

    def over_planes(x):
        return lax.all_to_all(x, "mp", 0, 0, tiled=True)

    def iota(shape, dim):
        return lax.broadcasted_iota(jnp.int32, shape, dim)

    me = lax.axis_index("dp")
    core = me & 1

    raw = jnp.concatenate([first_moment.astype(bf16), second_moment.astype(bf16)], axis=1)
    raw_other = other_core(raw)

    go = grad_out.reshape(tok, pairs, 2, block)
    go_even, go_odd = (go[:, :, c].reshape(tok, pairs * block) for c in range(2))
    go_mine = jnp.where(core == 0, go_even, go_odd)
    go_other = other_core(jnp.where(core == 0, go_odd, go_even))

    part = jnp.dot(hidden, basis, preferred_element_type=f32).astype(bf16)
    part, (raw, raw_other, go_mine, go_other, owners, first_moment, second_moment, me) = over(
        over_planes, part, raw, raw_other, go_mine, go_other, owners, first_moment, second_moment, me
    )
    part = part.reshape(planes, tok // planes, RANK)
    mine = jnp.sum(part.astype(f32), axis=0).astype(bf16)
    mine = jnp.broadcast_to(mine[None], part.shape).reshape(tok, RANK)
    coeffs, (raw, raw_other, go_mine, go_other, owners, first_moment, second_moment, me) = over(
        over_planes, mine, raw, raw_other, go_mine, go_other, owners, first_moment, second_moment, me
    )
    coeffs_other = other_core(coeffs)

    core = me & 1
    chip = me >> 1
    ids = owners[:, 0]
    order = iota((frags,), 0)
    same = ids[None, :] == ids[:, None]
    slot_of = jnp.sum((same & (order[None, :] < order[:, None])).astype(jnp.int32), axis=1)

    at = iota((chips * share, 1), 0) + (me & owner_count)
    k_of, p_of, r_of = at // share, (at // piece) % pairs, at % piece
    frag = (core + 2 * p_of) * per_block + k_of // half
    base = ((ids & 1) != core).astype(jnp.int32) * (slots * FC) + slot_of * FC
    rows = jnp.sum(jnp.where(frag == order[None, :], base[None, :], 0), axis=1, keepdims=True)
    rows = rows + (k_of % half) * piece + r_of
    held = slots * FC
    hot = (rows == iota((1, 2 * held), 1)).astype(bf16)
    moments = (
        jnp.dot(hot[:, :held], raw, preferred_element_type=f32)
        + jnp.dot(hot[:, held:], raw_other, preferred_element_type=f32)
    ).astype(bf16)
    moments = moments.reshape(chips, share, 2 * RANK)

    over_tokens = (((0,), (0,)), ((), ()))
    proj = lax.dot_general(go_mine, coeffs, over_tokens, preferred_element_type=f32)
    proj = proj + lax.dot_general(go_other, coeffs_other, over_tokens, preferred_element_type=f32)
    proj = (proj * scale).astype(bf16).reshape(pairs, chips, piece, RANK)
    proj = proj.transpose(1, 0, 2, 3).reshape(chips, share, RANK)
    got, (owners, first_moment, second_moment, me) = over(
        over_chips,
        jnp.concatenate([proj, moments], axis=2),
        owners,
        first_moment,
        second_moment,
        me,
    )
    core = me & 1
    chip = me >> 1
    ids = owners[:, 0]
    order = iota((frags,), 0)
    grad = jnp.sum(got[:, :, :RANK].astype(f32), axis=0)
    at = iota((share, 1), 0) + (me & owner_count)
    frag = (core + 2 * (at // piece)) * per_block + chip // half
    sender = jnp.sum(jnp.where(frag == order[None, :], ids[None, :], 0), axis=1) >> 1
    sent = iota((chips, share, 1), 0) == sender[None, :, None]
    old = jnp.sum(jnp.where(sent, got[:, :, RANK:].astype(f32), 0.0), axis=0)
    blend_first = first_keep * old[:, :RANK] + first_take * grad
    blend_second = second_keep * old[:, RANK:] + second_take * grad * grad
    factor = (blend_first / (jnp.sqrt(blend_second) + adam_eps)).astype(bf16)

    spread, (grad, owners, first_moment, second_moment, me) = over(
        over_planes,
        jnp.broadcast_to(factor[None], (planes, share, RANK)),
        grad.astype(bf16),
        owners,
        first_moment,
        second_moment,
        me,
    )
    spread = spread.reshape(chips, piece, RANK)
    grad = jnp.broadcast_to(grad[None], (chips, share, RANK))
    last, (owners, first_moment, second_moment, me) = over(
        over_chips,
        jnp.concatenate([spread, grad], axis=1),
        owners,
        first_moment,
        second_moment,
        me,
    )
    sums = last[:, piece:].reshape(chips * share, RANK)
    sums_other = other_core(sums)
    chosen = last[:, :piece].reshape(block, RANK)
    update = lax.dot_general(basis, chosen, (((1,), (1,)), ((), ())), preferred_element_type=f32)
    update = (update * math.sqrt(FF / RANK)).astype(bf16)

    core = me & 1
    ids = owners[:, 0]
    order = iota((frags,), 0)
    same = ids[None, :] == ids[:, None]
    slot_of = jnp.sum((same & (order[None, :] < order[:, None])).astype(jnp.int32), axis=1)
    at = iota((held, 1), 0) + (me & owner_count)
    within = at % FC
    own = (ids[None, :] == me) & (slot_of[None, :] == at // FC)
    live = jnp.any(own, axis=1, keepdims=True)
    source = jnp.sum(jnp.where(own, order[None, :], 0), axis=1, keepdims=True)
    b = source // per_block
    row = ((source % per_block) * half + within // piece) * share + (b // 2) * piece + within % piece
    row = row + (b % 2 != core).astype(jnp.int32) * (chips * share)
    row = jnp.where(live, row, -1)
    hot = (row == iota((1, 2 * chips * share), 1)).astype(bf16)
    totals = jnp.dot(hot[:, : chips * share], sums, preferred_element_type=f32)
    totals = totals + jnp.dot(hot[:, chips * share :], sums_other, preferred_element_type=f32)
    new_first = jnp.where(live, first_keep * first_moment + first_take * totals, first_moment)
    new_second = jnp.where(
        live, second_keep * second_moment + second_take * totals * totals, second_moment
    )
    return (update, new_first, new_second)


def solution(mesh):
    placed = (
        P("dp", "mp"),
        P("dp", "mp"),
        P("mp", None),
        P("mp", None),
        P(("dp", "mp"), None),
        P(("dp", "mp"), None),
    )
    return jax.shard_map(
        body,
        mesh=mesh,
        in_specs=placed,
        out_specs=(P("mp", "dp"), P(("dp", "mp"), None), P(("dp", "mp"), None)),
        check_vma=False,
    )
```

time: 137 us -> 129 us (0.942)
  blocking collectives: 0 us -> 95.4 us
  waiting for transfers between devices: 73.7 us -> 0.24 us
  starting transfers between devices: 33.8 us -> 11.2 us
  between operations: 6.09 us -> 0.91 us
    all_to_all x0 -> x5, blocking collectives: none -> 95.4 us  [the longest x3 51.5 us: over_planes(): return lax.all_to_all(x, 'mp', 0, 0, tiled=True)]
    all_to_all x5 -> x0, waiting for transfers between devices: 72.8 us -> none  [the longest x3 41.5 us: over_planes(): return lax.all_to_all(x, 'mp', 0, 0, tiled=True)]
    all_to_all x5 -> x0, starting transfers between devices: 29.3 us -> none  [the longest x3 15.9 us: over_planes(): return lax.all_to_all(x, 'mp', 0, 0, tiled=True)]
    ppermute x4, starting transfers between devices: 4.55 us -> 11.2 us  [other_core(): return lax.ppermute(x, 'dp', swap)]
    concatenate x2, other arithmetic: 2.21 us -> 0.17 us  [the longest x1 0.11 us: body(): jnp.concatenate([proj, moments], axis=2)]
    broadcast_in_dim x5 -> x3, local copies, waits for them, and re-layouts: 1.77 us -> 0.1 us  [the longest x1 0.04 us: body(): grad = jnp.broadcast_to(grad[None], (chips, share, RANK))]
    unnamed x10 -> x8, local copies, waits for them, and re-layouts: 2.84 us -> 3.78 us
    dot_general x3 -> x6, matrix products: 4.62 us -> 4.12 us  [the longest x1 2.16 us: body(): jnp.dot(hot[:, chips * share:], sums_other, preferred_element_type=f32)]
  transfers between devices with their start and end apart: 9 -> 4, of which waited for: 6 -> 1; matrix products, arithmetic and copies ran while one was open for 7% -> 11% of each run, Pallas kernels for 0% -> 0%
where the time goes in v2:
time: 129 us; the launch traced here: 128 us
  blocking collectives  95.4 us (74%)
  matrix products  12.6 us (10%)
  starting transfers between devices  11.2 us (9%)
  local copies, waits for them, and re-layouts  3.97 us (3%)
  other arithmetic  3.93 us (3%)
    all_to_all x3, blocking collectives, over_planes(): return lax.all_to_all(x, 'mp', 0, 0, tiled=True)  51.5 us
    all_to_all x2, blocking collectives, over_chips(): lax.all_to_all(x, 'dp', 0, 0, axis_index_groups=same_core, tiled=True)  43.9 us
    ppermute x4, starting transfers between devices, other_core(): return lax.ppermute(x, 'dp', swap)  11.2 us
    dot_general x1, matrix products, body(): part = jnp.dot(hidden, basis, preferred_element_type=f32).astype(bf16)  5.21 us
    unnamed x8, local copies, waits for them, and re-layouts  3.78 us
    dot_general x1, matrix products, body(): lax.dot_general(basis, chosen, (((1,), (1,)), ((), ())), preferred_elemen...  3.25 us
  transfers between devices with their start and end apart: 4, of which 1 were waited for; matrix products, arithmetic and copies ran while one was open for 11% of the time, Pallas kernels for 0%

profile of v2, /device:TPU:1, one launch (start us, length us, event | category | flops | bytes accessed | tf_op | source)
XLA Modules:
  0.0 128.3 jit_solution(5415592504812275571)
XLA Ops:
  0.6 1.0 convert_element_type.46
  1.6 1.0 convert_element_type.47
  2.6 3.3 %collective-permute-start = (bf16[128,1024]{1,0:T(8,128)(2,1)S(1)}, bf16[128,1024]{1,0:T(8,128)(2,1)S(1)}, u32[]{:S(2)}, u32[]{:S(2)}) collective-permute-start(bf16[128,1024]{1,0:T(8,128)(2,1)S(1)} %pad_maximum_fusion.2), channel_id=1, source_target_pairs={{0,8},{8,0},{16,24},{24,16},{32,40},{40,32},{48,56},{56,48},{64,72... | collective-permute-start | bytes 786440 | tf_op jit(solution)/shard_map/ppermute | solution.py:45
  5.9 1.5 %copy.15 = bf16[512,1024]{0,1:T(8,128)(2,1)S(1)} copy(bf16[512,1024]{1,0:T(8,128)(2,1)} %param.7) | data formatting | bytes 2097152 | tf_op args[1]
  7.5 0.1 collective-permute-start.1
  7.6 5.2 %convolution_convert_fusion = bf16[512,512]{1,0:T(8,128)(2,1)S(1)} fusion(bf16[512,3584]{1,0:T(8,128)(2,1)} %param.6, bf16[3584,512]{1,0:T(8,128)(2,1)} %param.8), kind=kOutput, calls=%fused_computation.9 | convolution fusion | flops 1879310336 | bytes 7864320 | tf_op jit(solution)/shard_map/dot_general | solution.py:67
  12.9 22.6 %all_to_all.39 = bf16[8,64,512]{2,1,0:T(8,128)(2,1)S(1)} all-to-all(bf16[8,64,512]{2,1,0:T(8,128)(2,1)S(1)} %bitcast.47), channel_id=1, replica_groups=mesh['dp'=32,'mp'=8] {'mp'}, dimensions={0} | all-to-all | bytes 1048576 | tf_op jit(solution)/shard_map/all_to_all | solution.py:51
  35.6 17.0 %all_to_all.40 = bf16[8,64,512]{2,1,0:T(8,128)(2,1)S(1)} all-to-all(bf16[8,64,512]{2,1,0:T(8,128)(2,1)S(1)} %broadcast_in_dim.94), channel_id=1, replica_groups=mesh['dp'=32,'mp'=8] {'mp'}, dimensions={0} | all-to-all | bytes 1048576 | tf_op jit(solution)/shard_map/all_to_all | solution.py:51
  52.6 0.2 convert_reduce_fusion.2
  52.8 0.1 select_reduce_fusion.1
  52.9 0.1 iota_compare_fusion.1
  53.1 4.0 %collective-permute-start.2 = (bf16[512,512]{1,0:T(8,128)(2,1)S(1)}, bf16[512,512]{1,0:T(8,128)(2,1)S(1)}, u32[]{:S(2)}, u32[]{:S(2)}) collective-permute-start(bf16[512,512]{1,0:T(8,128)(2,1)S(1)} %bitcast.42), channel_id=1, source_target_pairs={{0,8},{8,0},{16,24},{24,16},{32,40},{40,32},{48,56},{56,48},{64,72... | collective-permute-start | bytes 1572872 | tf_op jit(solution)/shard_map/ppermute | solution.py:45
  57.0 0.4 fusion.10
  57.5 0.4 fusion.41
  57.9 0.4 add_convert_fusion
  58.3 0.2 collective-permute-done.2
  58.6 0.4 fusion.3
  59.1 0.1 pad_maximum_fusion
  59.2 28.5 %all_to_all.41 = bf16[16,32,1536]{2,1,0:T(8,128)(2,1)S(1)} all-to-all(bf16[16,32,1536]{2,1,0:T(8,128)(2,1)S(1)} %pad_maximum_fusion), channel_id=1, replica_groups={{0,16,32,48,64,80,96,112,128,144,160,176,192,208,224,240},{8,24,40,56,7..., dimensions={0} | all-to-all | bytes 3145728 | tf_op jit(solution)/shard_map/all_to_all | solution.py:48
  87.7 0.2 select_reduce_fusion.3
  88.0 0.3 select_reduce_fusion
  88.4 11.9 %all_to_all.42 = bf16[8,32,512]{2,1,0:T(8,128)(2,1)S(1)} all-to-all(bf16[8,32,512]{2,1,0:T(8,128)(2,1)S(1)} %broadcast_in_dim.102), channel_id=1, replica_groups=mesh['dp'=32,'mp'=8] {'mp'}, dimensions={0} | all-to-all | bytes 524288 | tf_op jit(solution)/shard_map/all_to_all | solution.py:51
  100.4 15.4 %all_to_all.43 = bf16[16,48,512]{2,1,0:T(8,128)(2,1)S(1)} all-to-all(bf16[16,48,512]{2,1,0:T(8,128)(2,1)S(1)} %pad_maximum_fusion.1), channel_id=1, replica_groups={{0,16,32,48,64,80,96,112,128,144,160,176,192,208,224,240},{8,24,40,56,7..., dimensions={0} | all-to-all | bytes 1572864 | tf_op jit(solution)/shard_map/all_to_all | solution.py:48
  115.9 0.2 convert_reduce_fusion.1
  116.1 0.1 fusion.20
  116.2 0.1 select_reduce_fusion.2
  116.3 3.8 %collective-permute-start.3 = (bf16[512,512]{1,0:T(8,128)(2,1)S(1)}, bf16[512,512]{1,0:T(8,128)(2,1)}, u32[]{:S(2)}, u32[]{:S(2)}) collective-permute-start(bf16[512,512]{1,0:T(8,128)(2,1)S(1)} %bitcast.40), channel_id=1, source_target_pairs={{0,8},{8,0},{16,24},{24,16},{32,40},{40,32},{48,56},{56,48},{64,72... | collective-permute-start | bytes 1572872 | tf_op jit(solution)/shard_map/ppermute | solution.py:45
  120.1 3.2 %fusion.1 = bf16[3584,256]{0,1:T(8,128)(2,1)S(1)} fusion(bf16[256,512]{1,0:T(8,128)(2,1)S(1)} %bitcast.48, bf16[3584,512]{1,0:T(8,128)(2,1)} %param.8), kind=kOutput, calls=%fused_computation.2 | convolution fusion | flops 941359104 | bytes 5767168 | tf_op jit(solution)/shard_map/dot_general | solution.py:149
  123.5 2.3 %copy.17 = bf16[3584,256]{1,0:T(8,128)(2,1)} copy(bf16[3584,256]{0,1:T(8,128)(2,1)S(1)} %fusion.1) | data formatting | bytes 3670016
  125.7 0.1 iota_compare_fusion
  125.9 0.2 fusion.7
  126.1 2.2 %fusion.5 = (f32[128,512]{1,0:T(8,128)}, f32[128,512]{1,0:T(8,128)}) fusion(f32[128,512]{1,0:T(8,128)S(1)} %copy-done, pred[128]{0:T(512)(128)(4,1)S(1)} %fusion.20, f32[128,512]{1,0:T(8,128)S(1)} %copy-done.1, f32[128,512]{1,0:T(8,128)S(1)} %fusion.7, bf16[512,512]{1,0:T(8,128)(2,1)} %collective-permute-done.3, pred[128,1024]{1,0:T(32,128)(4,1)S(1)} %iota_compare_fusion), kind=kOutput, calls=%fused_computation.19 | convolution fusion | flops 67764224 | bytes 1901056 | tf_op jit(solution)/shard_map/dot_general | solution.py:168
  (30 shorter events, 0.7 us)
Async XLA Ops:
  2.6 10.3 %collective-permute-start = (bf16[128,1024]{1,0:T(8,128)(2,1)S(1)}, bf16[128,1024]{1,0:T(8,128)(2,1)S(1)}, u32[]{:S(2)}, u32[]{:S(2)}) collective-permute-start(bf16[128,1024]{1,0:T(8,128)(2,1)S(1)} %pad_maximum_fusion.2), channel_id=1, source_target_pairs={{0,8},{8,0},{16,24},{24,16},{32,40},{40,32},{48,56},{56,48},{64,72... | collective-permute-start | bytes 786440 | tf_op jit(solution)/shard_map/ppermute | solution.py:45
  7.5 5.3 %collective-permute-start.1 = (bf16[512,512]{0,1:T(8,128)(2,1)S(1)}, bf16[512,512]{0,1:T(8,128)(2,1)S(1)}, u32[]{:S(2)}, u32[]{:S(2)}) collective-permute-start(bf16[512,512]{0,1:T(8,128)(2,1)S(1)} %bitcast.46), channel_id=1, source_target_pairs={{0,8},{8,0},{16,24},{24,16},{32,40},{40,32},{48,56},{56,48},{64,72... | collective-permute-start | bytes 1572872 | tf_op jit(solution)/shard_map/ppermute | solution.py:45
  12.8 39.7 %copy-start.2 = (s32[32,1]{0,1:T(1,128)S(1)}, s32[32,1]{0,1:T(1,128)}, u32[]{:S(2)}) copy-start(s32[32,1]{0,1:T(1,128)} %param.9) | copy-start | bytes 388
  53.1 5.5 %collective-permute-start.2 = (bf16[512,512]{1,0:T(8,128)(2,1)S(1)}, bf16[512,512]{1,0:T(8,128)(2,1)S(1)}, u32[]{:S(2)}, u32[]{:S(2)}) collective-permute-start(bf16[512,512]{1,0:T(8,128)(2,1)S(1)} %bitcast.42), channel_id=1, source_target_pairs={{0,8},{8,0},{16,24},{24,16},{32,40},{40,32},{48,56},{56,48},{64,72... | collective-permute-start | bytes 1572872 | tf_op jit(solution)/shard_map/ppermute | solution.py:45
  116.3 9.8 %collective-permute-start.3 = (bf16[512,512]{1,0:T(8,128)(2,1)S(1)}, bf16[512,512]{1,0:T(8,128)(2,1)}, u32[]{:S(2)}, u32[]{:S(2)}) collective-permute-start(bf16[512,512]{1,0:T(8,128)(2,1)S(1)} %bitcast.40), channel_id=1, source_target_pairs={{0,8},{8,0},{16,24},{24,16},{32,40},{40,32},{48,56},{56,48},{64,72... | collective-permute-start | bytes 1572872 | tf_op jit(solution)/shard_map/ppermute | solution.py:45
  123.4 2.7 %copy-start = (f32[128,512]{1,0:T(8,128)S(1)}, f32[128,512]{1,0:T(8,128)}, u32[]{:S(2)}) copy-start(f32[128,512]{1,0:T(8,128)} %param.11) | copy-start | bytes 786436
  123.4 2.7 %copy-start.1 = (f32[128,512]{1,0:T(8,128)S(1)}, f32[128,512]{1,0:T(8,128)}, u32[]{:S(2)}) copy-start(f32[128,512]{1,0:T(8,128)} %param.10) | copy-start | bytes 786436

commit v3 on v1

v3 whole, which is shorter than its diff:
```python
import functools
import math

import jax
import jax.numpy as jnp
from jax import lax
from jax.experimental import pallas as pl
from jax.experimental.pallas import tpu as pltpu
from jax.sharding import PartitionSpec as P

FF = 28672
RANK = 512
FC = 32
STEPS = 7

first_keep = 0.9
first_take = 0.1
second_keep = 0.95
second_take = 0.05
adam_eps = 1e-08

bf16 = jnp.bfloat16
f32 = jnp.float32
VMEM = pl.BlockSpec(memory_space=pltpu.VMEM)
SMEM = pl.BlockSpec(memory_space=pltpu.SMEM)


def iota(shape, dim):
    return lax.broadcasted_iota(jnp.int32, shape, dim)


def kernel_params(mib=16):
    return pltpu.CompilerParams(vmem_limit_bytes=mib * 2**20)


def plane_slots(ids_row):
    n = ids_row.shape[1]
    f0, f1 = iota((n, n), 0), iota((n, n), 1)
    ids_col = jnp.sum(jnp.where(f0 == f1, ids_row, 0), axis=1, keepdims=True)
    same = ids_col == ids_row
    return jnp.sum((same & (f0 < f1)).astype(jnp.int32), axis=0, keepdims=True)


def coeffs_kernel(
    me_ref, hidden_ref, basis_ref, go_ref, first_ref, second_ref,
    part_ref, mine_ref, other_ref, raw_ref, total,
):
    step = pl.program_id(0)

    @pl.when(step == 0)
    def _():
        total[...] = jnp.zeros_like(total)
        raw_ref[:, :RANK] = first_ref[...].astype(bf16)
        raw_ref[:, RANK:] = second_ref[...].astype(bf16)
        even = (me_ref[0] & 1) == 0
        width = go_ref.shape[1] // 4
        for p in range(2):
            low = go_ref[:, (2 * p) * width : (2 * p + 1) * width]
            high = go_ref[:, (2 * p + 1) * width : (2 * p + 2) * width]
            mine_ref[:, p * width : (p + 1) * width] = jnp.where(even, low, high)
            other_ref[:, p * width : (p + 1) * width] = jnp.where(even, high, low)

    total[...] += jnp.dot(hidden_ref[...], basis_ref[...], preferred_element_type=f32)

    @pl.when(step == STEPS - 1)
    def _():
        part_ref[...] = total[...].astype(bf16)


def coeffs_call(me, hidden, basis, go, first, second):
    tok, ff = hidden.shape
    step = ff // STEPS
    held = first.shape[0]
    whole = lambda shape: pl.BlockSpec(shape, lambda i: (0, 0))
    return pl.pallas_call(
        coeffs_kernel,
        grid=(STEPS,),
        in_specs=[
            SMEM,
            pl.BlockSpec((tok, step), lambda i: (0, i)),
            pl.BlockSpec((step, RANK), lambda i: (i, 0)),
            whole(go.shape),
            whole(first.shape),
            whole(second.shape),
        ],
        out_specs=[
            whole((tok, RANK)),
            whole((tok, go.shape[1] // 2)),
            whole((tok, go.shape[1] // 2)),
            whole((held, 2 * RANK)),
        ],
        out_shape=[
            jax.ShapeDtypeStruct((tok, RANK), bf16),
            jax.ShapeDtypeStruct((tok, go.shape[1] // 2), bf16),
            jax.ShapeDtypeStruct((tok, go.shape[1] // 2), bf16),
            jax.ShapeDtypeStruct((held, 2 * RANK), bf16),
        ],
        scratch_shapes=[pltpu.VMEM((tok, RANK), f32)],
        compiler_params=kernel_params(56),
    )(me, hidden, basis, go, first, second)


OVER_TOKENS = (((0,), (0,)), ((), ()))


def payload_kernel(
    dims, me_ref, owners_ref, raw_ref, raw_other_ref, mine_ref, co_ref, out_ref, proj_ref
):
    chips, pairs, piece, per_block, slots, _ = dims
    share = pairs * piece
    half = chips // per_block
    held = slots * FC
    core = me_ref[0] & 1
    ids_row = owners_ref[...]
    slot_row = plane_slots(ids_row)
    frags = ids_row.shape[1]
    at = iota((chips * share, 1), 0)
    k_of, p_of, r_of = at // share, (at // piece) % pairs, at % piece
    frag = (core + 2 * p_of) * per_block + k_of // half
    base = ((ids_row & 1) != core).astype(jnp.int32) * held + slot_row * FC
    rows = jnp.sum(jnp.where(frag == iota((1, frags), 1), base, 0), axis=1, keepdims=True)
    rows = rows + (k_of % half) * piece + r_of
    cols = iota((1, held), 1)
    hot = jnp.where(rows == cols, 1.0, 0.0).astype(bf16)
    hot_other = jnp.where(rows == cols + held, 1.0, 0.0).astype(bf16)
    for n in range(2):
        at_n = slice(n * RANK, (n + 1) * RANK)
        old = jnp.dot(hot, raw_ref[:, at_n], preferred_element_type=f32)
        old += jnp.dot(hot_other, raw_other_ref[:, at_n], preferred_element_type=f32)
        old = old.astype(bf16).reshape(chips, share, RANK)
        out_ref[:, (n + 1) * share : (n + 2) * share, :] = old
    proj_ref[...] = lax.dot_general(
        mine_ref[...], co_ref[...], OVER_TOKENS, preferred_element_type=f32
    )


def project_kernel(dims, other_ref, co_other_ref, proj_ref, part_ref, out_ref):
    chips, pairs, piece, _, _, scale = dims
    proj = proj_ref[...] + lax.dot_general(
        other_ref[...], co_other_ref[...], OVER_TOKENS, preferred_element_type=f32
    )
    proj = (proj * scale).astype(bf16).reshape(pairs, chips, piece, RANK)
    for p in range(pairs):
        out_ref[:, p * piece : (p + 1) * piece, :] = proj[p]


def factor_kernel(dims, me_ref, owners_ref, got_ref, factor_ref, grad_ref):
    chips, pairs, piece, per_block, _, _ = dims
    share = pairs * piece
    core = me_ref[0] & 1
    chip = me_ref[0] >> 1
    ids_row = owners_ref[...]
    at = iota((share, 1), 0)
    frag = (core + 2 * (at // piece)) * per_block + chip // (chips // per_block)
    sender = jnp.where(frag == iota((1, ids_row.shape[1]), 1), ids_row, 0)
    sender = jnp.sum(sender, axis=1, keepdims=True) >> 1
    grad = jnp.zeros((share, RANK), f32)
    first = jnp.zeros((share, RANK), f32)
    second = jnp.zeros((share, RANK), f32)
    for k in range(chips):
        sent = sender == k
        grad += got_ref[k, :share, :].astype(f32)
        first = jnp.where(sent, got_ref[k, share : 2 * share, :].astype(f32), first)
        second = jnp.where(sent, got_ref[k, 2 * share :, :].astype(f32), second)
    first = first_keep * first + first_take * grad
    second = second_keep * second + second_take * grad * grad
    factor = (first / (jnp.sqrt(second) + adam_eps)).astype(bf16)
    for m in range(factor_ref.shape[0]):
        factor_ref[m] = factor
    grad_ref[...] = grad.astype(bf16)


def update_kernel(block, piece, basis_ref, last_ref, out_ref):
    chosen = last_ref[:, :piece, :].reshape(block, RANK)
    update = lax.dot_general(
        basis_ref[...], chosen, (((1,), (1,)), ((), ())), preferred_element_type=f32
    )
    out_ref[...] = (update * math.sqrt(FF / RANK)).astype(bf16)


def update_call(basis, last, block, piece):
    rows = basis.shape[0]
    step = rows // STEPS
    return pl.pallas_call(
        functools.partial(update_kernel, block, piece),
        grid=(STEPS,),
        in_specs=[
            pl.BlockSpec((step, RANK), lambda i: (i, 0)),
            pl.BlockSpec(last.shape, lambda i: (0, 0, 0)),
        ],
        out_specs=pl.BlockSpec((step, block), lambda i: (i, 0)),
        out_shape=jax.ShapeDtypeStruct((rows, block), bf16),
        compiler_params=kernel_params(),
    )(basis, last)


def owner_kernel(
    dims, me_ref, owners_ref, first_ref, second_ref, sums_ref, sums_other_ref, first_out, second_out
):
    chips, pairs, piece, per_block, slots = dims
    share = pairs * piece
    half = chips // per_block
    me = me_ref[0]
    ids_row = owners_ref[...]
    slot_row = plane_slots(ids_row)
    frags = ids_row.shape[1]
    at = iota((slots * FC, 1), 0)
    within = at % FC
    own = (ids_row == me) & (slot_row == at // FC)
    live = jnp.sum(own.astype(jnp.int32), axis=1, keepdims=True) > 0
    source = jnp.sum(jnp.where(own, iota((1, frags), 1), 0), axis=1, keepdims=True)
    b = source // per_block
    row = ((source % per_block) * half + within // piece) * share + (b // 2) * piece + within % piece
    row = jnp.where(live, row + (b % 2 != (me & 1)).astype(jnp.int32) * (chips * share), -1)
    cols = iota((1, chips * share), 1)
    hot = jnp.where(row == cols, 1.0, 0.0).astype(bf16)
    hot_other = jnp.where(row == cols + chips * share, 1.0, 0.0).astype(bf16)
    g = jnp.dot(hot, sums_ref[...], preferred_element_type=f32)
    g += jnp.dot(hot_other, sums_other_ref[...], preferred_element_type=f32)
    first, second = first_ref[...], second_ref[...]
    first_out[...] = jnp.where(live, first_keep * first + first_take * g, first)
    second_out[...] = jnp.where(live, second_keep * second + second_take * g * g, second)


def over(exchange, x, *rest):
    x, rest = lax.optimization_barrier((x, rest))
    return lax.optimization_barrier((exchange(x), rest))


def body(hidden, grad_out, basis, owners, first_moment, second_moment):
    owner_count = lax.axis_size("dp")
    planes = lax.axis_size("mp")
    chips = owner_count // 2
    tok, col = grad_out.shape
    slots = first_moment.shape[0] // FC
    frags = owners.shape[0]
    block = col * planes // owner_count
    per_block = block // FC
    piece = block // chips
    pairs = col // block // 2
    share = pairs * piece
    scale = 1.0 / math.sqrt(tok * owner_count)
    same_core = [[2 * k + c for k in range(chips)] for c in range(2)]
    swap = [(i, i ^ 1) for i in range(owner_count)]

    def other_core(x):
        return lax.ppermute(x, "dp", swap)

    def over_chips(x):
        return lax.all_to_all(x, "dp", 0, 0, axis_index_groups=same_core, tiled=True)

    def over_planes(x):
        return lax.all_to_all(x, "mp", 0, 0, tiled=True)

    me = lax.axis_index("dp").reshape(1)
    owners = owners.reshape(1, frags)

    part, go_mine, go_theirs, raw = coeffs_call(
        me, hidden, basis, grad_out, first_moment, second_moment
    )
    raw_other = other_core(raw)
    go_other = other_core(go_theirs)

    part, (raw_other, go_other) = over(over_planes, part, raw_other, go_other)
    part = part.reshape(planes, tok // planes, RANK)
    mine = jnp.sum(part.astype(f32), axis=0).astype(bf16)
    mine = jnp.broadcast_to(mine[None], part.shape).reshape(tok, RANK)
    coeffs, (me, owners) = over(over_planes, mine, me, owners)
    coeffs_other = other_core(coeffs)

    dims = (chips, pairs, piece, per_block, slots, scale)
    payload_shape = jax.ShapeDtypeStruct((chips, 3 * share, RANK), bf16)
    payload, proj = pl.pallas_call(
        functools.partial(payload_kernel, dims),
        in_specs=[SMEM] + [VMEM] * 5,
        out_specs=[VMEM, VMEM],
        out_shape=[payload_shape, jax.ShapeDtypeStruct((pairs * block, RANK), f32)],
        compiler_params=kernel_params(),
    )(me, owners, raw, raw_other, go_mine, coeffs)
    payload = pl.pallas_call(
        functools.partial(project_kernel, dims),
        in_specs=[VMEM] * 4,
        out_specs=VMEM,
        out_shape=payload_shape,
        input_output_aliases={3: 0},
        compiler_params=kernel_params(),
    )(go_other, coeffs_other, proj, payload)
    got, (me, owners) = over(over_chips, payload, me, owners)
    factor, grad = pl.pallas_call(
        functools.partial(factor_kernel, dims),
        in_specs=[SMEM] + [VMEM] * 2,
        out_specs=[VMEM, VMEM],
        out_shape=[
            jax.ShapeDtypeStruct((planes, share, RANK), bf16),
            jax.ShapeDtypeStruct((share, RANK), bf16),
        ],
        compiler_params=kernel_params(),
    )(me, owners, got)

    spread, (grad,) = over(over_planes, factor, grad)
    spread = spread.reshape(chips, piece, RANK)
    grad = jnp.broadcast_to(grad[None], (chips, share, RANK))
    last, (me, owners, first_moment, second_moment) = over(
        over_chips,
        jnp.concatenate([spread, grad], axis=1),
        me,
        owners,
        first_moment,
        second_moment,
    )
    sums = last[:, piece:].reshape(chips * share, RANK)
    sums_other = other_core(sums)
    update = update_call(basis, last, block, piece)

    like = jax.ShapeDtypeStruct(first_moment.shape, f32)
    new_first, new_second = pl.pallas_call(
        functools.partial(owner_kernel, dims[:5]),
        in_specs=[SMEM] + [VMEM] * 5,
        out_specs=[VMEM, VMEM],
        out_shape=[like, like],
        compiler_params=kernel_params(),
    )(me, owners, first_moment, second_moment, sums, sums_other)
    return (update, new_first, new_second)


def solution(mesh):
    placed = (
        P("dp", "mp"),
        P("dp", "mp"),
        P("mp", None),
        P("mp", None),
        P(("dp", "mp"), None),
        P(("dp", "mp"), None),
    )
    return jax.shard_map(
        body,
        mesh=mesh,
        in_specs=placed,
        out_specs=(P("mp", "dp"), P(("dp", "mp"), None), P(("dp", "mp"), None)),
        check_vma=False,
    )
```

time: 137 us -> 127 us (0.927)
  blocking collectives: 0 us -> 96.6 us
  waiting for transfers between devices: 73.7 us -> 2.43 us
  starting transfers between devices: 33.8 us -> 10.8 us
  Pallas kernels: 0 us -> 16.1 us
  matrix products: 13.9 us -> 0 us
  between operations: 6.09 us -> 0.72 us
  local copies, waits for them, and re-layouts: 5.12 us -> 0.14 us
  other arithmetic: 4.08 us -> 0.13 us
    all_to_all x0 -> x5, blocking collectives: none -> 96.6 us  [the longest x3 52.4 us: over_planes(): return lax.all_to_all(x, 'mp', 0, 0, tiled=True)]
    all_to_all x5 -> x0, waiting for transfers between devices: 72.8 us -> none  [the longest x3 41.5 us: over_planes(): return lax.all_to_all(x, 'mp', 0, 0, tiled=True)]
    all_to_all x5 -> x0, starting transfers between devices: 29.3 us -> none  [the longest x3 15.9 us: over_planes(): return lax.all_to_all(x, 'mp', 0, 0, tiled=True)]
    pallas_call x0 -> x6, Pallas kernels: none -> 16.1 us  [the longest x1 8.62 us: coeffs_call(): pl.pallas_call(coeffs_kernel, grid=(STEPS,), in_specs=[SMEM, pl.BlockSpec...]
    dot_general x5 -> x0, matrix products: 13.9 us -> none  [the longest x1 6.08 us: body(): part = jnp.dot(hidden, basis, preferred_element_type=f32).astype(bf16)]
    ppermute x4, starting transfers between devices: 4.55 us -> 10.8 us  [other_core(): return lax.ppermute(x, 'dp', swap)]
    unnamed x10 -> x12, local copies, waits for them, and re-layouts: 2.84 us -> 0.03 us
    concatenate x3 -> x1, other arithmetic: 2.23 us -> 0.06 us  [body(): jnp.concatenate([spread, grad], axis=1)]
  transfers between devices with their start and end apart: 9 -> 4, of which waited for: 6 -> 2; matrix products, arithmetic and copies ran while one was open for 7% -> 0% of each run, Pallas kernels for 0% -> 4%
where the time goes in v3:
time: 127 us
  blocking collectives  96.6 us (76%)
  Pallas kernels  16.1 us (13%)
  starting transfers between devices  10.8 us (9%)
  waiting for transfers between devices  2.43 us (2%)
    all_to_all x3, blocking collectives, over_planes(): return lax.all_to_all(x, 'mp', 0, 0, tiled=True)  52.4 us
    all_to_all x2, blocking collectives, over_chips(): lax.all_to_all(x, 'dp', 0, 0, axis_index_groups=same_core, tiled=True)  44.2 us
    ppermute x4, starting transfers between devices, other_core(): return lax.ppermute(x, 'dp', swap)  10.8 us
    pallas_call x1, Pallas kernels, coeffs_call(): pl.pallas_call(coeffs_kernel, grid=(STEPS,), in_specs=[SMEM, pl.BlockSpec...  8.62 us
    pallas_call x1, Pallas kernels, update_call(): pl.pallas_call(functools.partial(update_kernel, block, piece), grid=(STEP...  4.12 us
  transfers between devices with their start and end apart: 4, of which 2 were waited for; matrix products, arithmetic and copies ran while one was open for 0% of the time, Pallas kernels for 4%

profile of v3, /device:TPU:1, one launch (start us, length us, event | category | flops | bytes accessed | tf_op | source)
XLA Modules:
  0.0 127.0 jit_solution(10426765173047298796)
XLA Ops:
  0.6 8.6 %shard_map.85 = (bf16[512,512]{1,0:T(8,128)(2,1)}, bf16[512,512]{1,0:T(8,128)(2,1)}, bf16[512,512]{1,0:T(8,128)(2,1)}, bf16[128,1024]{1,0:T(8,128)(2,1)}) custom-call(s32[1]{0:T(128)} %bitcast.me_ref, bf16[512,3584]{1,0:T(8,128)(2,1)} %hidden_ref.1, bf16[3584,512]{1,0:T(8,128)(2,1)} %basis_ref.3, bf16[512,1024]{1,0:T(8,128)(2,1)} %go_ref.1, ...), custom_call_target="tpu_custom_call" | custom-call | tf_op jit(solution)/shard_map/pallas_call | solution.py:75
  9.3 3.2 %collective-permute-start.1 = (bf16[512,512]{1,0:T(8,128)(2,1)}, bf16[512,512]{1,0:T(8,128)(2,1)S(1)}, u32[]{:S(2)}, u32[]{:S(2)}) collective-permute-start(bf16[512,512]{1,0:T(8,128)(2,1)} %get-tuple-element.45), channel_id=1, source_target_pairs={{0,8},{8,0},{16,24},{24,16},{32,40},{40,32},{48,56},{56,48},{64,72... | collective-permute-start | bytes 1572872 | tf_op jit(solution)/shard_map/ppermute | solution.py:247
  12.5 0.1 collective-permute-start
  12.6 2.1 %collective-permute-done.raw_other_ref = bf16[128,1024]{1,0:T(8,128)(2,1)S(1)} collective-permute-done((bf16[128,1024]{1,0:T(8,128)(2,1)}, bf16[128,1024]{1,0:T(8,128)(2,1)S(1)}, u32[]{:S(2)}, u32[]{:S(2)}) %collective-permute-start) | collective-permute-done | bytes 262176 | tf_op jit(solution)/shard_map/ppermute | solution.py:247
  14.6 0.0 collective-permute-done.1.other_ref
  14.6 0.0 copy-start.3
  14.6 0.0 copy-start.5
  14.6 23.3 %all_to_all.39 = bf16[8,64,512]{2,1,0:T(8,128)(2,1)S(1)} all-to-all(bf16[8,64,512]{2,1,0:T(8,128)(2,1)} %bitcast.18), channel_id=1, replica_groups=mesh['dp'=32,'mp'=8] {'mp'}, dimensions={0} | all-to-all | bytes 1048576 | tf_op jit(solution)/shard_map/all_to_all | solution.py:253
  37.9 0.1 reduce_sum.12
  38.0 17.2 %all_to_all.40 = bf16[8,64,512]{2,1,0:T(8,128)(2,1)S(1)} all-to-all(bf16[8,64,512]{2,1,0:T(8,128)(2,1)S(1)} %broadcast_in_dim.4), channel_id=1, replica_groups=mesh['dp'=32,'mp'=8] {'mp'}, dimensions={0} | all-to-all | bytes 1048576 | tf_op jit(solution)/shard_map/all_to_all | solution.py:253
  55.2 3.6 %collective-permute-start.2 = (bf16[512,512]{1,0:T(8,128)(2,1)S(1)}, bf16[512,512]{1,0:T(8,128)(2,1)S(1)}, u32[]{:S(2)}, u32[]{:S(2)}) collective-permute-start(bf16[512,512]{1,0:T(8,128)(2,1)S(1)} %bitcast.12), channel_id=1, source_target_pairs={{0,8},{8,0},{16,24},{24,16},{32,40},{40,32},{48,56},{56,48},{64,72... | collective-permute-start | bytes 1572872 | tf_op jit(solution)/shard_map/ppermute | solution.py:247
  58.9 0.0 copy-done.3
  58.9 0.0 copy-done.4
  58.9 0.0 copy-done.5
  58.9 1.2 shard_map.86
  60.0 0.4 collective-permute-done.2.co_other_ref
  60.4 0.5 shard_map.87
  60.9 28.5 %all_to_all.41.got_ref = bf16[16,96,512]{2,1,0:T(8,128)(2,1)S(1)} all-to-all(bf16[16,96,512]{2,1,0:T(8,128)(2,1)S(1)} %shard_map.87), channel_id=1, replica_groups={{0,16,32,48,64,80,96,112,128,144,160,176,192,208,224,240},{8,24,40,56,7..., dimensions={0} | all-to-all | bytes 3145728 | tf_op jit(solution)/shard_map/all_to_all | solution.py:250
  89.4 0.3 shard_map.88
  89.7 11.9 %all_to_all.42 = bf16[8,32,512]{2,1,0:T(8,128)(2,1)S(1)} all-to-all(bf16[8,32,512]{2,1,0:T(8,128)(2,1)S(1)} %get-tuple-element.67), channel_id=1, replica_groups=mesh['dp'=32,'mp'=8] {'mp'}, dimensions={0} | all-to-all | bytes 524288 | tf_op jit(solution)/shard_map/all_to_all | solution.py:253
  101.7 0.0 copy-start
  101.7 0.1 pad_maximum_fusion
  101.8 15.7 %all_to_all.43.last_ref = bf16[16,48,512]{2,1,0:T(8,128)(2,1)S(1)} all-to-all(bf16[16,48,512]{2,1,0:T(8,128)(2,1)S(1)} %pad_maximum_fusion), channel_id=1, replica_groups={{0,16,32,48,64,80,96,112,128,144,160,176,192,208,224,240},{8,24,40,56,7..., dimensions={0} | all-to-all | bytes 1572864 | tf_op jit(solution)/shard_map/all_to_all | solution.py:250
  117.5 0.0 copy-start.1
  117.6 0.0 copy-start.2
  117.6 3.8 %collective-permute-start.3 = (bf16[512,512]{1,0:T(8,128)(2,1)S(1)}, bf16[512,512]{1,0:T(8,128)(2,1)S(1)}, u32[]{:S(2)}, u32[]{:S(2)}) collective-permute-start(bf16[512,512]{1,0:T(8,128)(2,1)S(1)} %bitcast.10), channel_id=1, source_target_pairs={{0,8},{8,0},{16,24},{24,16},{32,40},{40,32},{48,56},{56,48},{64,72... | collective-permute-start | bytes 1572872 | tf_op jit(solution)/shard_map/ppermute | solution.py:247
  121.4 0.0 copy-done
  121.4 4.1 %shard_map.89 = bf16[3584,256]{1,0:T(8,128)(2,1)} custom-call(bf16[3584,512]{1,0:T(8,128)(2,1)S(1)} %copy-done, bf16[16,48,512]{2,1,0:T(8,128)(2,1)S(1)} %all_to_all.43.last_ref), custom_call_target="tpu_custom_call" | custom-call | tf_op jit(solution)/shard_map/pallas_call | solution.py:184
  125.5 0.0 collective-permute-done.3.sums_other_ref
  125.5 0.0 copy-done.1
  125.5 0.0 copy-done.2
  125.5 1.4 %shard_map.90 = (f32[128,512]{1,0:T(8,128)}, f32[128,512]{1,0:T(8,128)}) custom-call(s32[1]{0:T(128)} %bitcast.me_ref, s32[1,32]{1,0:T(1,128)S(1)} %bitcast.16, f32[128,512]{1,0:T(8,128)S(1)} %copy-done.1, f32[128,512]{1,0:T(8,128)S(1)} %copy-done.2, bf16[512,512]{1,0:T(8,128)(2,1)S(1)} %bitcast.11, bf16[512,512]{1,0:T(8,128)(2,1)S(1)} %collective-permute-done.3.sums_other_ref), custom_call_target="tpu_custom_call" | custom-call | tf_op jit(solution)/shard_map/pallas_call | solution.py:316
  (4 shorter events, 0.1 us)
Async XLA Ops:
  9.3 5.4 %collective-permute-start.1 = (bf16[512,512]{1,0:T(8,128)(2,1)}, bf16[512,512]{1,0:T(8,128)(2,1)S(1)}, u32[]{:S(2)}, u32[]{:S(2)}) collective-permute-start(bf16[512,512]{1,0:T(8,128)(2,1)} %get-tuple-element.45), channel_id=1, source_target_pairs={{0,8},{8,0},{16,24},{24,16},{32,40},{40,32},{48,56},{56,48},{64,72... | collective-permute-start | bytes 1572872 | tf_op jit(solution)/shard_map/ppermute | solution.py:247
  12.5 2.1 %collective-permute-start = (bf16[128,1024]{1,0:T(8,128)(2,1)}, bf16[128,1024]{1,0:T(8,128)(2,1)S(1)}, u32[]{:S(2)}, u32[]{:S(2)}) collective-permute-start(bf16[128,1024]{1,0:T(8,128)(2,1)} %get-tuple-element.44.raw_ref), channel_id=1, source_target_pairs={{0,8},{8,0},{16,24},{24,16},{32,40},{40,32},{48,56},{56,48},{64,72... | collective-permute-start | bytes 786440 | tf_op jit(solution)/shard_map/ppermute | solution.py:247
  14.6 44.2 %copy-start.3 = (bf16[512,512]{1,0:T(8,128)(2,1)S(1)}, bf16[512,512]{1,0:T(8,128)(2,1)}, u32[]{:S(2)}) copy-start(bf16[512,512]{1,0:T(8,128)(2,1)} %get-tuple-element.58.mine_ref) | copy-start | bytes 1572868
  14.6 44.2 %copy-start.4 = (bf16[128,1024]{1,0:T(8,128)(2,1)S(1)}, bf16[128,1024]{1,0:T(8,128)(2,1)}, u32[]{:S(2)}) copy-start(bf16[128,1024]{1,0:T(8,128)(2,1)} %get-tuple-element.44.raw_ref) | copy-start | bytes 786436
  14.6 44.2 %copy-start.5 = (s32[32,1]{0,1:T(1,128)S(1)}, s32[32,1]{0,1:T(1,128)}, u32[]{:S(2)}) copy-start(s32[32,1]{0,1:T(1,128)} %param.9) | copy-start | bytes 388
  55.2 5.2 %collective-permute-start.2 = (bf16[512,512]{1,0:T(8,128)(2,1)S(1)}, bf16[512,512]{1,0:T(8,128)(2,1)S(1)}, u32[]{:S(2)}, u32[]{:S(2)}) collective-permute-start(bf16[512,512]{1,0:T(8,128)(2,1)S(1)} %bitcast.12), channel_id=1, source_target_pairs={{0,8},{8,0},{16,24},{24,16},{32,40},{40,32},{48,56},{56,48},{64,72... | collective-permute-start | bytes 1572872 | tf_op jit(solution)/shard_map/ppermute | solution.py:247
  101.7 19.7 %copy-start = (bf16[3584,512]{1,0:T(8,128)(2,1)S(1)}, bf16[3584,512]{1,0:T(8,128)(2,1)}, u32[]{:S(2)}) copy-start(bf16[3584,512]{1,0:T(8,128)(2,1)} %basis_ref.3) | copy-start | bytes 11010052
  117.5 8.0 %copy-start.1 = (f32[128,512]{1,0:T(8,128)S(1)}, f32[128,512]{1,0:T(8,128)}, u32[]{:S(2)}) copy-start(f32[128,512]{1,0:T(8,128)} %first_ref.2) | copy-start | bytes 786436
  117.6 8.0 %copy-start.2 = (f32[128,512]{1,0:T(8,128)S(1)}, f32[128,512]{1,0:T(8,128)}, u32[]{:S(2)}) copy-start(f32[128,512]{1,0:T(8,128)} %second_ref.2) | copy-start | bytes 786436
  117.6 8.0 %collective-permute-start.3 = (bf16[512,512]{1,0:T(8,128)(2,1)S(1)}, bf16[512,512]{1,0:T(8,128)(2,1)S(1)}, u32[]{:S(2)}, u32[]{:S(2)}) collective-permute-start(bf16[512,512]{1,0:T(8,128)(2,1)S(1)} %bitcast.10), channel_id=1, source_target_pairs={{0,8},{8,0},{16,24},{24,16},{32,40},{40,32},{48,56},{56,48},{64,72... | collective-permute-start | bytes 1572872 | tf_op jit(solution)/shard_map/ppermute | solution.py:247

commit v4 on v3

--- a/solution.py
+++ b/solution.py
@@ -43,59 +43,73 @@
 
 def coeffs_kernel(
     me_ref, hidden_ref, basis_ref, go_ref, first_ref, second_ref,
-    part_ref, mine_ref, other_ref, raw_ref, total,
+    part_ref, mine_ref, other_ref, raw_ref,
+    hidden, basis, go, first, second, total, sems,
 ):
-    step = pl.program_id(0)
-
-    @pl.when(step == 0)
-    def _():
-        total[...] = jnp.zeros_like(total)
-        raw_ref[:, :RANK] = first_ref[...].astype(bf16)
-        raw_ref[:, RANK:] = second_ref[...].astype(bf16)
-        even = (me_ref[0] & 1) == 0
-        width = go_ref.shape[1] // 4
-        for p in range(2):
-            low = go_ref[:, (2 * p) * width : (2 * p + 1) * width]
-            high = go_ref[:, (2 * p + 1) * width : (2 * p + 2) * width]
-            mine_ref[:, p * width : (p + 1) * width] = jnp.where(even, low, high)
-            other_ref[:, p * width : (p + 1) * width] = jnp.where(even, high, low)
-
-    total[...] += jnp.dot(hidden_ref[...], basis_ref[...], preferred_element_type=f32)
-
-    @pl.when(step == STEPS - 1)
-    def _():
-        part_ref[...] = total[...].astype(bf16)
+    step = hidden.shape[2]
+
+    def chunk(j):
+        at = slice(j * step, (j + 1) * step)
+        return (
+            pltpu.make_async_copy(hidden_ref.at[:, at], hidden.at[j], sems.at[2 * j]),
+            pltpu.make_async_copy(basis_ref.at[at, :], basis.at[j], sems.at[2 * j + 1]),
+        )
+
+    chunks = [chunk(j) for j in range(STEPS)]
+    extra = [
+        pltpu.make_async_copy(first_ref, first, sems.at[2 * STEPS]),
+        pltpu.make_async_copy(second_ref, second, sems.at[2 * STEPS + 1]),
+        pltpu.make_async_copy(go_ref, go, sems.at[2 * STEPS + 2]),
+    ]
+    for copy in [c for pair in chunks for c in pair] + extra:
+        copy.start()
+    for j in range(STEPS):
+        for copy in chunks[j]:
+            copy.wait()
+        term = jnp.dot(hidden[j], basis[j], preferred_element_type=f32)
+        if j == 0:
+            total[...] = term
+        elif j < STEPS - 1:
+            total[...] += term
+        else:
+            part_ref[...] = (total[...] + term).astype(bf16)
+    for copy in extra:
+        copy.wait()
+    raw_ref[:, :RANK] = first[...].astype(bf16)
+    raw_ref[:, RANK:] = second[...].astype(bf16)
+    even = (me_ref[0] & 1) == 0
+    width = go.shape[1] // 4
+    for p in range(2):
+        low = go[:, (2 * p) * width : (2 * p + 1) * width]
+        high = go[:, (2 * p + 1) * width : (2 * p + 2) * width]
+        mine_ref[:, p * width : (p + 1) * width] = jnp.where(even, low, high)
+        other_ref[:, p * width : (p + 1) * width] = jnp.where(even, high, low)
 
 
 def coeffs_call(me, hidden, basis, go, first, second):
     tok, ff = hidden.shape
     step = ff // STEPS
     held = first.shape[0]
-    whole = lambda shape: pl.BlockSpec(shape, lambda i: (0, 0))
+    like = lambda *shape: jax.ShapeDtypeStruct(shape, bf16)
     return pl.pallas_call(
         coeffs_kernel,
-        grid=(STEPS,),
-        in_specs=[
-            SMEM,
-            pl.BlockSpec((tok, step), lambda i: (0, i)),
-            pl.BlockSpec((step, RANK), lambda i: (i, 0)),
-            whole(go.shape),
-            whole(first.shape),
-            whole(second.shape),
+        in_specs=[SMEM] + [pl.BlockSpec(memory_space=pl.ANY)] * 5,
+        out_specs=[VMEM] * 4,
+        out_shape=[
+            like(tok, RANK),
+            like(tok, go.shape[1] // 2),
+            like(tok, go.shape[1] // 2),
+            like(held, 2 * RANK),
         ],
-        out_specs=[
-            whole((tok, RANK)),
-            whole((tok, go.shape[1] // 2)),
-            whole((tok, go.shape[1] // 2)),
-            whole((held, 2 * RANK)),
+        scratch_shapes=[
+            pltpu.VMEM((STEPS, tok, step), bf16),
+            pltpu.VMEM((STEPS, step, RANK), bf16),
+            pltpu.VMEM(go.shape, bf16),
+            pltpu.VMEM(first.shape, f32),
+            pltpu.VMEM(second.shape, f32),
+            pltpu.VMEM((tok, RANK), f32),
+            pltpu.SemaphoreType.DMA((2 * STEPS + 3,)),
         ],
-        out_shape=[
-            jax.ShapeDtypeStruct((tok, RANK), bf16),
-            jax.ShapeDtypeStruct((tok, go.shape[1] // 2), bf16),
-            jax.ShapeDtypeStruct((tok, go.shape[1] // 2), bf16),
-            jax.ShapeDtypeStruct((held, 2 * RANK), bf16),
-        ],
-        scratch_shapes=[pltpu.VMEM((tok, RANK), f32)],
         compiler_params=kernel_params(56),
     )(me, hidden, basis, go, first, second)
 
@@ -104,31 +118,42 @@
 
 
 def payload_kernel(
-    dims, me_ref, owners_ref, raw_ref, raw_other_ref, mine_ref, co_ref, out_ref, proj_ref
+    dims, me_ref, owners_ref, near_ref, far_ref, mine_ref, co_ref, out_ref, proj_ref
 ):
     chips, pairs, piece, per_block, slots, _ = dims
     share = pairs * piece
     half = chips // per_block
     held = slots * FC
     core = me_ref[0] & 1
+    chip = me_ref[0] >> 1
     ids_row = owners_ref[...]
     slot_row = plane_slots(ids_row)
     frags = ids_row.shape[1]
     at = iota((chips * share, 1), 0)
     k_of, p_of, r_of = at // share, (at // piece) % pairs, at % piece
     frag = (core + 2 * p_of) * per_block + k_of // half
-    base = ((ids_row & 1) != core).astype(jnp.int32) * held + slot_row * FC
+    base = ((ids_row & 1) != core).astype(jnp.int32) * (2 * held) + slot_row * FC
+    base += ((ids_row >> 1) != chip).astype(jnp.int32) * held
     rows = jnp.sum(jnp.where(frag == iota((1, frags), 1), base, 0), axis=1, keepdims=True)
     rows = rows + (k_of % half) * piece + r_of
-    cols = iota((1, held), 1)
+    cols = iota((1, 2 * held), 1)
     hot = jnp.where(rows == cols, 1.0, 0.0).astype(bf16)
-    hot_other = jnp.where(rows == cols + held, 1.0, 0.0).astype(bf16)
+    hot_far = jnp.where(rows == cols + 2 * held, 1.0, 0.0).astype(bf16)
+    width = RANK // 2
+    low = (chip & 1) == 0
     for n in range(2):
-        at_n = slice(n * RANK, (n + 1) * RANK)
-        old = jnp.dot(hot, raw_ref[:, at_n], preferred_element_type=f32)
-        old += jnp.dot(hot_other, raw_other_ref[:, at_n], preferred_element_type=f32)
-        old = old.astype(bf16).reshape(chips, share, RANK)
-        out_ref[:, (n + 1) * share : (n + 2) * share, :] = old
+        near, far = (
+            jnp.where(
+                low,
+                ref[:, 2 * n * width : (2 * n + 1) * width],
+                ref[:, (2 * n + 1) * width : (2 * n + 2) * width],
+            )
+            for ref in (near_ref, far_ref)
+        )
+        old = jnp.dot(hot, near, preferred_element_type=f32)
+        old += jnp.dot(hot_far, far, preferred_element_type=f32)
+        old = old.astype(bf16).reshape(chips, share, width)
+        out_ref[:, share:, n * width : (n + 1) * width] = old
     proj_ref[...] = lax.dot_general(
         mine_ref[...], co_ref[...], OVER_TOKENS, preferred_element_type=f32
     )
@@ -154,14 +179,15 @@
     frag = (core + 2 * (at // piece)) * per_block + chip // (chips // per_block)
     sender = jnp.where(frag == iota((1, ids_row.shape[1]), 1), ids_row, 0)
     sender = jnp.sum(sender, axis=1, keepdims=True) >> 1
+    width = RANK // 2
     grad = jnp.zeros((share, RANK), f32)
-    first = jnp.zeros((share, RANK), f32)
-    second = jnp.zeros((share, RANK), f32)
+    old = [jnp.zeros((share, 2 * width), f32) for _ in range(2)]
     for k in range(chips):
-        sent = sender == k
         grad += got_ref[k, :share, :].astype(f32)
-        first = jnp.where(sent, got_ref[k, share : 2 * share, :].astype(f32), first)
-        second = jnp.where(sent, got_ref[k, 2 * share :, :].astype(f32), second)
+        sent = (sender >> 1) == (k >> 1)
+        old[k & 1] = jnp.where(sent, got_ref[k, share:, :].astype(f32), old[k & 1])
+    first = jnp.concatenate([old[0][:, :width], old[1][:, :width]], axis=1)
+    second = jnp.concatenate([old[0][:, width:], old[1][:, width:]], axis=1)
     first = first_keep * first + first_take * grad
     second = second_keep * second + second_take * grad * grad
     factor = (first / (jnp.sqrt(second) + adam_eps)).astype(bf16)
@@ -170,26 +196,33 @@
     grad_ref[...] = grad.astype(bf16)
 
 
-def update_kernel(block, piece, basis_ref, last_ref, out_ref):
+def update_kernel(piece, basis_ref, last_ref, out_ref, done, sems):
+    step, block = done.shape[1:]
     chosen = last_ref[:, :piece, :].reshape(block, RANK)
-    update = lax.dot_general(
-        basis_ref[...], chosen, (((1,), (1,)), ((), ())), preferred_element_type=f32
-    )
-    out_ref[...] = (update * math.sqrt(FF / RANK)).astype(bf16)
+    copies = []
+    for j in range(STEPS):
+        at = slice(j * step, (j + 1) * step)
+        update = lax.dot_general(
+            basis_ref[at, :], chosen, (((1,), (1,)), ((), ())), preferred_element_type=f32
+        )
+        done[j] = (update * math.sqrt(FF / RANK)).astype(bf16)
+        copies.append(pltpu.make_async_copy(done.at[j], out_ref.at[at, :], sems.at[j]))
+        copies[-1].start()
+    for copy in copies:
+        copy.wait()
 
 
 def update_call(basis, last, block, piece):
     rows = basis.shape[0]
-    step = rows // STEPS
     return pl.pallas_call(
-        functools.partial(update_kernel, block, piece),
-        grid=(STEPS,),
-        in_specs=[
-            pl.BlockSpec((step, RANK), lambda i: (i, 0)),
-            pl.BlockSpec(last.shape, lambda i: (0, 0, 0)),
+        functools.partial(update_kernel, piece),
+        in_specs=[VMEM, VMEM],
+        out_specs=pl.BlockSpec(memory_space=pl.ANY),
+        out_shape=jax.ShapeDtypeStruct((rows, block), bf16),
+        scratch_shapes=[
+            pltpu.VMEM((STEPS, rows // STEPS, block), bf16),
+            pltpu.SemaphoreType.DMA((STEPS,)),
         ],
-        out_specs=pl.BlockSpec((step, block), lambda i: (i, 0)),
-        out_shape=jax.ShapeDtypeStruct((rows, block), bf16),
         compiler_params=kernel_params(),
     )(basis, last)
 
@@ -242,6 +275,7 @@
     scale = 1.0 / math.sqrt(tok * owner_count)
     same_core = [[2 * k + c for k in range(chips)] for c in range(2)]
     swap = [(i, i ^ 1) for i in range(owner_count)]
+    next_chip = [(i, i ^ 2) for i in range(owner_count)]
 
     def other_core(x):
         return lax.ppermute(x, "dp", swap)
@@ -258,25 +292,26 @@
     part, go_mine, go_theirs, raw = coeffs_call(
         me, hidden, basis, grad_out, first_moment, second_moment
     )
-    raw_other = other_core(raw)
     go_other = other_core(go_theirs)
-
-    part, (raw_other, go_other) = over(over_planes, part, raw_other, go_other)
+    near = jnp.concatenate([raw, lax.ppermute(raw, "dp", next_chip)], axis=0)
+
+    part, _ = over(over_planes, part)
     part = part.reshape(planes, tok // planes, RANK)
     mine = jnp.sum(part.astype(f32), axis=0).astype(bf16)
+    far = other_core(near)
     mine = jnp.broadcast_to(mine[None], part.shape).reshape(tok, RANK)
     coeffs, (me, owners) = over(over_planes, mine, me, owners)
     coeffs_other = other_core(coeffs)
 
     dims = (chips, pairs, piece, per_block, slots, scale)
-    payload_shape = jax.ShapeDtypeStruct((chips, 3 * share, RANK), bf16)
+    payload_shape = jax.ShapeDtypeStruct((chips, 2 * share, RANK), bf16)
     payload, proj = pl.pallas_call(
         functools.partial(payload_kernel, dims),
         in_specs=[SMEM] + [VMEM] * 5,
         out_specs=[VMEM, VMEM],
         out_shape=[payload_shape, jax.ShapeDtypeStruct((pairs * block, RANK), f32)],
         compiler_params=kernel_params(),
-    )(me, owners, raw, raw_other, go_mine, coeffs)
+    )(me, owners, near, far, go_mine, coeffs)
     payload = pl.pallas_call(
         functools.partial(project_kernel, dims),
         in_specs=[VMEM] * 4,

time: 127 us -> 114 us (0.90)
  blocking collectives: 96.6 us -> 75.7 us
  starting transfers between devices: 10.8 us -> 18.5 us
  Pallas kernels: 16.1 us -> 10 us
  waiting for transfers between devices: 2.43 us -> 7.79 us
    all_to_all x3 -> x2, blocking collectives: 52.4 us -> 37.1 us  [over_planes(): return lax.all_to_all(x, 'mp', 0, 0, tiled=True)]
    all_to_all x0 -> x1, waiting for transfers between devices: none -> 5.91 us  [over_planes(): return lax.all_to_all(x, 'mp', 0, 0, tiled=True)]
    pallas_call x2, Pallas kernels: 12.7 us -> 6.98 us  [the longest x1 4.97 us: coeffs_call(): pl.pallas_call(coeffs_kernel, in_specs=[SMEM] + [pl.BlockSpec(memory_spac...]
    all_to_all x2, blocking collectives: 44.2 us -> 38.6 us  [over_chips(): lax.all_to_all(x, 'dp', 0, 0, axis_index_groups=same_core, tiled=True)]
    all_to_all x0 -> x1, starting transfers between devices: none -> 3.49 us  [over_planes(): return lax.all_to_all(x, 'mp', 0, 0, tiled=True)]
    ppermute x4, starting transfers between devices: 10.8 us -> 13.7 us  [other_core(): return lax.ppermute(x, 'dp', swap)]
    ppermute x4, waiting for transfers between devices: 2.43 us -> 0.63 us  [other_core(): return lax.ppermute(x, 'dp', swap)]
    ppermute x0 -> x1, starting transfers between devices: none -> 1.3 us  [body(): near = jnp.concatenate([raw, lax.ppermute(raw, 'dp', next_chip)], axis=0)]
  transfers between devices with their start and end apart: 4 -> 6, of which waited for: 2 -> 3; matrix products, arithmetic and copies ran while one was open for 0% -> 0% of each run, Pallas kernels for 4% -> 3%
where the time goes in v4:
time: 114 us
  blocking collectives  75.7 us (66%)
  starting transfers between devices  18.5 us (16%)
  Pallas kernels  10 us (9%)
  waiting for transfers between devices  7.79 us (7%)
    all_to_all x2, blocking collectives, over_chips(): lax.all_to_all(x, 'dp', 0, 0, axis_index_groups=same_core, tiled=True)  38.6 us
    all_to_all x2, blocking collectives, over_planes(): return lax.all_to_all(x, 'mp', 0, 0, tiled=True)  37.1 us
    ppermute x4, starting transfers between devices, other_core(): return lax.ppermute(x, 'dp', swap)  13.7 us
    all_to_all x1, waiting for transfers between devices, over_planes(): return lax.all_to_all(x, 'mp', 0, 0, tiled=True)  5.91 us
    pallas_call x1, Pallas kernels, coeffs_call(): pl.pallas_call(coeffs_kernel, in_specs=[SMEM] + [pl.BlockSpec(memory_spac...  4.97 us
    all_to_all x1, starting transfers between devices, over_planes(): return lax.all_to_all(x, 'mp', 0, 0, tiled=True)  3.49 us
  transfers between devices with their start and end apart: 6, of which 3 were waited for; matrix products, arithmetic and copies ran while one was open for 0% of the time, Pallas kernels for 3%

profile of v4, /device:TPU:1, one launch (start us, length us, event | category | flops | bytes accessed | tf_op | source)
XLA Modules:
  0.0 113.9 jit_solution(17619555809580142873)
XLA Ops:
  0.6 5.0 %shard_map.85 = (bf16[512,512]{1,0:T(8,128)(2,1)}, bf16[512,512]{1,0:T(8,128)(2,1)}, bf16[512,512]{1,0:T(8,128)(2,1)}, bf16[128,1024]{1,0:T(8,128)(2,1)}) custom-call(s32[1]{0:T(128)} %bitcast.me_ref, bf16[512,3584]{1,0:T(8,128)(2,1)} %hidden_ref.1, bf16[3584,512]{1,0:T(8,128)(2,1)} %basis_ref.3, bf16[512,1024]{1,0:T(8,128)(2,1)} %go_ref.1, ...), custom_call_target="tpu_custom_call" | custom-call | tf_op jit(solution)/shard_map/pallas_call | solution.py:94
  5.6 0.0 copy-start.5
  5.6 0.0 copy-start.6
  5.6 25.1 %all_to_all.39 = bf16[8,64,512]{2,1,0:T(8,128)(2,1)S(1)} all-to-all(bf16[8,64,512]{2,1,0:T(8,128)(2,1)} %bitcast.18), channel_id=1, replica_groups=mesh['dp'=32,'mp'=8] {'mp'}, dimensions={0} | all-to-all | bytes 1048576 | tf_op jit(solution)/shard_map/all_to_all | solution.py:287
  30.8 0.1 reduce_sum.12
  30.9 0.8 broadcast_in_dim.4
  31.7 3.5 %all-to-all-start.1 = ((bf16[8,64,512]{2,1,0:T(8,128)(2,1)}), bf16[8,64,512]{2,1,0:T(8,128)(2,1)S(1)}, u32[]{:S(2)}, u32[]{:S(2)}) async-start(bf16[8,64,512]{2,1,0:T(8,128)(2,1)} %bitcast.6), calls=%async_computation.1 | async-start | bytes 1048576 | tf_op jit(solution)/shard_map/all_to_all | solution.py:287
  35.2 1.3 %collective-permute-start.2 = (bf16[128,1024]{1,0:T(8,128)(2,1)S(1)}, bf16[128,1024]{1,0:T(8,128)(2,1)S(1)}, u32[]{:S(2)}, u32[]{:S(2)}) collective-permute-start(bf16[128,1024]{1,0:T(8,128)(2,1)S(1)} %copy-done.5), channel_id=1, source_target_pairs={{0,16},{8,24},{16,0},{24,8},{32,48},{40,56},{48,32},{56,40},{64,80... | collective-permute-start | bytes 786440 | tf_op jit(solution)/shard_map/ppermute | solution.py:296
  36.5 2.7 %collective-permute-start = (bf16[512,512]{1,0:T(8,128)(2,1)S(1)}, bf16[512,512]{1,0:T(8,128)(2,1)S(1)}, u32[]{:S(2)}, u32[]{:S(2)}) collective-permute-start(bf16[512,512]{1,0:T(8,128)(2,1)S(1)} %copy-done.6), channel_id=1, source_target_pairs={{0,8},{8,0},{16,24},{24,16},{32,40},{40,32},{48,56},{56,48},{64,72... | collective-permute-start | bytes 1572872 | tf_op jit(solution)/shard_map/ppermute | solution.py:281
  39.3 1.3 %collective-permute-done.2 = bf16[128,1024]{1,0:T(8,128)(2,1)S(1)} collective-permute-done((bf16[128,1024]{1,0:T(8,128)(2,1)S(1)}, bf16[128,1024]{1,0:T(8,128)(2,1)S(1)}, u32[]{:S(2)}, u32[]{:S(2)}) %collective-permute-start.2) | collective-permute-done | bytes 262176 | tf_op jit(solution)/shard_map/ppermute | solution.py:296
  40.5 3.7 %collective-permute-start.3 = (bf16[256,1024]{1,0:T(8,128)(2,1)S(1)}, bf16[256,1024]{1,0:T(8,128)(2,1)S(1)}, u32[]{:S(2)}, u32[]{:S(2)}) collective-permute-start(bf16[256,1024]{1,0:T(8,128)(2,1)S(1)} %constant_dynamic-update-slice_fusion.near_ref), channel_id=1, source_target_pairs={{0,8},{8,0},{16,24},{24,16},{32,40},{40,32},{48,56},{56,48},{64,72... | collective-permute-start | bytes 1572872 | tf_op jit(solution)/shard_map/ppermute | solution.py:281
  44.2 5.9 %all-to-all-done.1 = bf16[8,64,512]{2,1,0:T(8,128)(2,1)S(1)} async-done(((bf16[8,64,512]{2,1,0:T(8,128)(2,1)}), bf16[8,64,512]{2,1,0:T(8,128)(2,1)S(1)}, u32[]{:S(2)}, u32[]{:S(2)}) %all-to-all-start.1) | async-done | bytes 524320 | tf_op jit(solution)/shard_map/all_to_all | solution.py:287
  50.1 3.4 %collective-permute-start.1 = (bf16[512,512]{1,0:T(8,128)(2,1)S(1)}, bf16[512,512]{1,0:T(8,128)(2,1)S(1)}, u32[]{:S(2)}, u32[]{:S(2)}) collective-permute-start(bf16[512,512]{1,0:T(8,128)(2,1)S(1)} %bitcast.10), channel_id=1, source_target_pairs={{0,8},{8,0},{16,24},{24,16},{32,40},{40,32},{48,56},{56,48},{64,72... | collective-permute-start | bytes 1572872 | tf_op jit(solution)/shard_map/ppermute | solution.py:281
  53.6 0.0 collective-permute-done.3.far_ref
  53.6 0.9 shard_map.86
  54.5 0.0 collective-permute-done.other_ref
  54.5 0.6 collective-permute-done.1.co_other_ref
  55.1 0.5 shard_map.87
  55.6 22.9 %all_to_all.40.got_ref = bf16[16,64,512]{2,1,0:T(8,128)(2,1)S(1)} all-to-all(bf16[16,64,512]{2,1,0:T(8,128)(2,1)S(1)} %shard_map.87), channel_id=1, replica_groups={{0,16,32,48,64,80,96,112,128,144,160,176,192,208,224,240},{8,24,40,56,7..., dimensions={0} | all-to-all | bytes 2097152 | tf_op jit(solution)/shard_map/all_to_all | solution.py:284
  78.5 0.2 shard_map.88
  78.7 12.0 %all_to_all.41 = bf16[8,32,512]{2,1,0:T(8,128)(2,1)S(1)} all-to-all(bf16[8,32,512]{2,1,0:T(8,128)(2,1)S(1)} %get-tuple-element.55), channel_id=1, replica_groups=mesh['dp'=32,'mp'=8] {'mp'}, dimensions={0} | all-to-all | bytes 524288 | tf_op jit(solution)/shard_map/all_to_all | solution.py:287
  90.7 0.0 copy-start
  90.7 0.1 pad_maximum_fusion
  90.8 15.7 %all_to_all.42.last_ref = bf16[16,48,512]{2,1,0:T(8,128)(2,1)S(1)} all-to-all(bf16[16,48,512]{2,1,0:T(8,128)(2,1)S(1)} %pad_maximum_fusion), channel_id=1, replica_groups={{0,16,32,48,64,80,96,112,128,144,160,176,192,208,224,240},{8,24,40,56,7..., dimensions={0} | all-to-all | bytes 1572864 | tf_op jit(solution)/shard_map/all_to_all | solution.py:284
  106.5 0.0 copy-start.1
  106.5 0.0 copy-start.2
  106.5 3.8 %collective-permute-start.4 = (bf16[512,512]{1,0:T(8,128)(2,1)S(1)}, bf16[512,512]{1,0:T(8,128)(2,1)S(1)}, u32[]{:S(2)}, u32[]{:S(2)}) collective-permute-start(bf16[512,512]{1,0:T(8,128)(2,1)S(1)} %bitcast.12), channel_id=1, source_target_pairs={{0,8},{8,0},{16,24},{24,16},{32,40},{40,32},{48,56},{56,48},{64,72... | collective-permute-start | bytes 1572872 | tf_op jit(solution)/shard_map/ppermute | solution.py:281
  110.4 2.0 %shard_map.89 = bf16[3584,256]{1,0:T(8,128)(2,1)} custom-call(bf16[3584,512]{1,0:T(8,128)(2,1)S(1)} %copy-done, bf16[16,48,512]{2,1,0:T(8,128)(2,1)S(1)} %all_to_all.42.last_ref), custom_call_target="tpu_custom_call" | custom-call | tf_op jit(solution)/shard_map/pallas_call | solution.py:217
  112.4 0.0 collective-permute-done.4.sums_other_ref
  112.4 0.0 copy-done.1
  112.4 0.0 copy-done.2
  112.4 1.4 %shard_map.90 = (f32[128,512]{1,0:T(8,128)}, f32[128,512]{1,0:T(8,128)}) custom-call(s32[1]{0:T(128)} %bitcast.me_ref, s32[1,32]{1,0:T(1,128)S(1)} %bitcast.16, f32[128,512]{1,0:T(8,128)S(1)} %copy-done.1, f32[128,512]{1,0:T(8,128)S(1)} %copy-done.2, bf16[512,512]{1,0:T(8,128)(2,1)S(1)} %bitcast.13, bf16[512,512]{1,0:T(8,128)(2,1)S(1)} %collective-permute-done.4.sums_other_ref), custom_call_target="tpu_custom_call" | custom-call | tf_op jit(solution)/shard_map/pallas_call | solution.py:351
  (11 shorter events, 0.1 us)
Async XLA Ops:
  5.6 29.6 %copy-start.5 = (bf16[128,1024]{1,0:T(8,128)(2,1)S(1)}, bf16[128,1024]{1,0:T(8,128)(2,1)}, u32[]{:S(2)}) copy-start(bf16[128,1024]{1,0:T(8,128)(2,1)} %get-tuple-element.45) | copy-start | bytes 786436
  5.6 30.9 %copy-start.6 = (bf16[512,512]{1,0:T(8,128)(2,1)S(1)}, bf16[512,512]{1,0:T(8,128)(2,1)}, u32[]{:S(2)}) copy-start(bf16[512,512]{1,0:T(8,128)(2,1)} %get-tuple-element.37) | copy-start | bytes 1572868
  30.8 22.8 %copy-start.3 = (bf16[512,512]{1,0:T(8,128)(2,1)S(1)}, bf16[512,512]{1,0:T(8,128)(2,1)}, u32[]{:S(2)}) copy-start(bf16[512,512]{1,0:T(8,128)(2,1)} %get-tuple-element.46.mine_ref) | copy-start | bytes 1572868
  30.8 22.8 %copy-start.4 = (s32[32,1]{0,1:T(1,128)S(1)}, s32[32,1]{0,1:T(1,128)}, u32[]{:S(2)}) copy-start(s32[32,1]{0,1:T(1,128)} %param.9) | copy-start | bytes 388
  31.7 18.4 %all-to-all-start.1 = ((bf16[8,64,512]{2,1,0:T(8,128)(2,1)}), bf16[8,64,512]{2,1,0:T(8,128)(2,1)S(1)}, u32[]{:S(2)}, u32[]{:S(2)}) async-start(bf16[8,64,512]{2,1,0:T(8,128)(2,1)} %bitcast.6), calls=%async_computation.1 | async-start | bytes 1048576 | tf_op jit(solution)/shard_map/all_to_all | solution.py:287
  35.2 5.3 %collective-permute-start.2 = (bf16[128,1024]{1,0:T(8,128)(2,1)S(1)}, bf16[128,1024]{1,0:T(8,128)(2,1)S(1)}, u32[]{:S(2)}, u32[]{:S(2)}) collective-permute-start(bf16[128,1024]{1,0:T(8,128)(2,1)S(1)} %copy-done.5), channel_id=1, source_target_pairs={{0,16},{8,24},{16,0},{24,8},{32,48},{40,56},{48,32},{56,40},{64,80... | collective-permute-start | bytes 786440 | tf_op jit(solution)/shard_map/ppermute | solution.py:296
  36.5 18.0 %collective-permute-start = (bf16[512,512]{1,0:T(8,128)(2,1)S(1)}, bf16[512,512]{1,0:T(8,128)(2,1)S(1)}, u32[]{:S(2)}, u32[]{:S(2)}) collective-permute-start(bf16[512,512]{1,0:T(8,128)(2,1)S(1)} %copy-done.6), channel_id=1, source_target_pairs={{0,8},{8,0},{16,24},{24,16},{32,40},{40,32},{48,56},{56,48},{64,72... | collective-permute-start | bytes 1572872 | tf_op jit(solution)/shard_map/ppermute | solution.py:281
  40.5 13.0 %collective-permute-start.3 = (bf16[256,1024]{1,0:T(8,128)(2,1)S(1)}, bf16[256,1024]{1,0:T(8,128)(2,1)S(1)}, u32[]{:S(2)}, u32[]{:S(2)}) collective-permute-start(bf16[256,1024]{1,0:T(8,128)(2,1)S(1)} %constant_dynamic-update-slice_fusion.near_ref), channel_id=1, source_target_pairs={{0,8},{8,0},{16,24},{24,16},{32,40},{40,32},{48,56},{56,48},{64,72... | collective-permute-start | bytes 1572872 | tf_op jit(solution)/shard_map/ppermute | solution.py:281
  50.1 5.0 %collective-permute-start.1 = (bf16[512,512]{1,0:T(8,128)(2,1)S(1)}, bf16[512,512]{1,0:T(8,128)(2,1)S(1)}, u32[]{:S(2)}, u32[]{:S(2)}) collective-permute-start(bf16[512,512]{1,0:T(8,128)(2,1)S(1)} %bitcast.10), channel_id=1, source_target_pairs={{0,8},{8,0},{16,24},{24,16},{32,40},{40,32},{48,56},{56,48},{64,72... | collective-permute-start | bytes 1572872 | tf_op jit(solution)/shard_map/ppermute | solution.py:281
  90.7 19.7 %copy-start = (bf16[3584,512]{1,0:T(8,128)(2,1)S(1)}, bf16[3584,512]{1,0:T(8,128)(2,1)}, u32[]{:S(2)}) copy-start(bf16[3584,512]{1,0:T(8,128)(2,1)} %basis_ref.3) | copy-start | bytes 11010052
  106.5 5.9 %copy-start.1 = (f32[128,512]{1,0:T(8,128)S(1)}, f32[128,512]{1,0:T(8,128)}, u32[]{:S(2)}) copy-start(f32[128,512]{1,0:T(8,128)} %first_ref.2) | copy-start | bytes 786436
  106.5 5.9 %copy-start.2 = (f32[128,512]{1,0:T(8,128)S(1)}, f32[128,512]{1,0:T(8,128)}, u32[]{:S(2)}) copy-start(f32[128,512]{1,0:T(8,128)} %second_ref.2) | copy-start | bytes 786436
  106.5 5.9 %collective-permute-start.4 = (bf16[512,512]{1,0:T(8,128)(2,1)S(1)}, bf16[512,512]{1,0:T(8,128)(2,1)S(1)}, u32[]{:S(2)}, u32[]{:S(2)}) collective-permute-start(bf16[512,512]{1,0:T(8,128)(2,1)S(1)} %bitcast.12), channel_id=1, source_target_pairs={{0,8},{8,0},{16,24},{24,16},{32,40},{40,32},{48,56},{56,48},{64,72... | collective-permute-start | bytes 1572872 | tf_op jit(solution)/shard_map/ppermute | solution.py:281

commit v5 on v4

--- a/solution.py
+++ b/solution.py
@@ -12,6 +12,7 @@
 RANK = 512
 FC = 32
 STEPS = 7
+SQUARE = 4
 
 first_keep = 0.9
 first_take = 0.1
@@ -61,7 +62,9 @@
         pltpu.make_async_copy(second_ref, second, sems.at[2 * STEPS + 1]),
         pltpu.make_async_copy(go_ref, go, sems.at[2 * STEPS + 2]),
     ]
-    for copy in [c for pair in chunks for c in pair] + extra:
+    for copy in [c for pair in chunks[:2] for c in pair] + extra:
+        copy.start()
+    for copy in [c for pair in chunks[2:] for c in pair]:
         copy.start()
     for j in range(STEPS):
         for copy in chunks[j]:
@@ -73,17 +76,18 @@
             total[...] += term
         else:
             part_ref[...] = (total[...] + term).astype(bf16)
-    for copy in extra:
-        copy.wait()
-    raw_ref[:, :RANK] = first[...].astype(bf16)
-    raw_ref[:, RANK:] = second[...].astype(bf16)
-    even = (me_ref[0] & 1) == 0
-    width = go.shape[1] // 4
-    for p in range(2):
-        low = go[:, (2 * p) * width : (2 * p + 1) * width]
-        high = go[:, (2 * p + 1) * width : (2 * p + 2) * width]
-        mine_ref[:, p * width : (p + 1) * width] = jnp.where(even, low, high)
-        other_ref[:, p * width : (p + 1) * width] = jnp.where(even, high, low)
+        if j == 2:
+            for copy in extra:
+                copy.wait()
+            raw_ref[:, :RANK] = first[...].astype(bf16)
+            raw_ref[:, RANK:] = second[...].astype(bf16)
+            even = (me_ref[0] & 1) == 0
+            width = go.shape[1] // 4
+            for p in range(2):
+                low = go[:, (2 * p) * width : (2 * p + 1) * width]
+                high = go[:, (2 * p + 1) * width : (2 * p + 2) * width]
+                mine_ref[:, p * width : (p + 1) * width] = jnp.where(even, low, high)
+                other_ref[:, p * width : (p + 1) * width] = jnp.where(even, high, low)
 
 
 def coeffs_call(me, hidden, basis, go, first, second):
@@ -93,7 +97,7 @@
     like = lambda *shape: jax.ShapeDtypeStruct(shape, bf16)
     return pl.pallas_call(
         coeffs_kernel,
-        in_specs=[SMEM] + [pl.BlockSpec(memory_space=pl.ANY)] * 5,
+        in_specs=[SMEM] + [pl.BlockSpec(memory_space=pltpu.HBM)] * 5,
         out_specs=[VMEM] * 4,
         out_shape=[
             like(tok, RANK),
@@ -117,6 +121,10 @@
 OVER_TOKENS = (((0,), (0,)), ((), ()))
 
 
+def in_square(chip):
+    return (chip & 1) + 2 * ((chip >> 2) & 1), ((chip >> 1) & 1) + 2 * (chip >> 3)
+
+
 def payload_kernel(
     dims, me_ref, owners_ref, near_ref, far_ref, mine_ref, co_ref, out_ref, proj_ref
 ):
@@ -132,28 +140,21 @@
     at = iota((chips * share, 1), 0)
     k_of, p_of, r_of = at // share, (at // piece) % pairs, at % piece
     frag = (core + 2 * p_of) * per_block + k_of // half
-    base = ((ids_row & 1) != core).astype(jnp.int32) * (2 * held) + slot_row * FC
-    base += ((ids_row >> 1) != chip).astype(jnp.int32) * held
+    base = ((ids_row & 1) != core).astype(jnp.int32) * (SQUARE * held) + slot_row * FC
+    base += (in_square(ids_row >> 1)[0] ^ in_square(chip)[0]) * held
     rows = jnp.sum(jnp.where(frag == iota((1, frags), 1), base, 0), axis=1, keepdims=True)
     rows = rows + (k_of % half) * piece + r_of
-    cols = iota((1, 2 * held), 1)
+    cols = iota((1, SQUARE * held), 1)
     hot = jnp.where(rows == cols, 1.0, 0.0).astype(bf16)
-    hot_far = jnp.where(rows == cols + 2 * held, 1.0, 0.0).astype(bf16)
-    width = RANK // 2
-    low = (chip & 1) == 0
+    hot_far = jnp.where(rows == cols + SQUARE * held, 1.0, 0.0).astype(bf16)
+    width = RANK // SQUARE
     for n in range(2):
-        near, far = (
-            jnp.where(
-                low,
-                ref[:, 2 * n * width : (2 * n + 1) * width],
-                ref[:, (2 * n + 1) * width : (2 * n + 2) * width],
-            )
-            for ref in (near_ref, far_ref)
-        )
-        old = jnp.dot(hot, near, preferred_element_type=f32)
-        old += jnp.dot(hot_far, far, preferred_element_type=f32)
-        old = old.astype(bf16).reshape(chips, share, width)
-        out_ref[:, share:, n * width : (n + 1) * width] = old
+        at_n = pl.ds(pl.multiple_of(n * RANK + in_square(chip)[0] * width, 128), width)
+        old = jnp.dot(hot, near_ref[:, at_n], preferred_element_type=f32)
+        old += jnp.dot(hot_far, far_ref[:, at_n], preferred_element_type=f32)
+        old = old.astype(bf16).reshape(chips, pairs, piece, width)
+        for p in range(pairs):
+            out_ref[:, share:, (2 * p + n) * width : (2 * p + n + 1) * width] = old[:, p]
     proj_ref[...] = lax.dot_general(
         mine_ref[...], co_ref[...], OVER_TOKENS, preferred_element_type=f32
     )
@@ -175,19 +176,31 @@
     core = me_ref[0] & 1
     chip = me_ref[0] >> 1
     ids_row = owners_ref[...]
-    at = iota((share, 1), 0)
-    frag = (core + 2 * (at // piece)) * per_block + chip // (chips // per_block)
-    sender = jnp.where(frag == iota((1, ids_row.shape[1]), 1), ids_row, 0)
-    sender = jnp.sum(sender, axis=1, keepdims=True) >> 1
-    width = RANK // 2
     grad = jnp.zeros((share, RANK), f32)
-    old = [jnp.zeros((share, 2 * width), f32) for _ in range(2)]
     for k in range(chips):
         grad += got_ref[k, :share, :].astype(f32)
-        sent = (sender >> 1) == (k >> 1)
-        old[k & 1] = jnp.where(sent, got_ref[k, share:, :].astype(f32), old[k & 1])
-    first = jnp.concatenate([old[0][:, :width], old[1][:, :width]], axis=1)
-    second = jnp.concatenate([old[0][:, width:], old[1][:, width:]], axis=1)
+    width = RANK // SQUARE
+    parts = []
+    for p in range(pairs):
+        frag = (core + 2 * p) * per_block + chip // (chips // per_block)
+        sender = jnp.where(iota(ids_row.shape, 1) == frag, ids_row, 0)
+        square = in_square(jnp.sum(sender, axis=1, keepdims=True) >> 1)[1]
+        old = [jnp.zeros((piece, 2 * width), f32) for _ in range(SQUARE)]
+        for k in range(chips):
+            place, number = in_square(k)
+            sent = got_ref[k, share:, 2 * p * width : (2 * p + 2) * width].astype(f32)
+            old[place] = jnp.where(square == number, sent, old[place])
+        parts.append(old)
+    first, second = (
+        jnp.concatenate(
+            [
+                jnp.concatenate([o[:, n * width : (n + 1) * width] for o in old], axis=1)
+                for old in parts
+            ],
+            axis=0,
+        )
+        for n in range(2)
+    )
     first = first_keep * first + first_take * grad
     second = second_keep * second + second_take * grad * grad
     factor = (first / (jnp.sqrt(second) + adam_eps)).astype(bf16)
@@ -275,7 +288,8 @@
     scale = 1.0 / math.sqrt(tok * owner_count)
     same_core = [[2 * k + c for k in range(chips)] for c in range(2)]
     swap = [(i, i ^ 1) for i in range(owner_count)]
-    next_chip = [(i, i ^ 2) for i in range(owner_count)]
+    next_x = [(i, i ^ 2) for i in range(owner_count)]
+    next_y = [(i, i ^ 8) for i in range(owner_count)]
 
     def other_core(x):
         return lax.ppermute(x, "dp", swap)
@@ -292,19 +306,24 @@
     part, go_mine, go_theirs, raw = coeffs_call(
         me, hidden, basis, grad_out, first_moment, second_moment
     )
+    part, go_theirs, raw = lax.optimization_barrier((part, go_theirs, raw))
+
+    part = over_planes(part)
+    near = jnp.concatenate([raw, lax.ppermute(raw, "dp", next_x)], axis=0)
+    near = jnp.concatenate([near, lax.ppermute(near, "dp", next_y)], axis=0)
     go_other = other_core(go_theirs)
-    near = jnp.concatenate([raw, lax.ppermute(raw, "dp", next_chip)], axis=0)
-
-    part, _ = over(over_planes, part)
+    part, near, go_other = lax.optimization_barrier((part, near, go_other))
     part = part.reshape(planes, tok // planes, RANK)
     mine = jnp.sum(part.astype(f32), axis=0).astype(bf16)
+    mine = jnp.broadcast_to(mine[None], part.shape).reshape(tok, RANK)
+    mine, near, me, owners = lax.optimization_barrier((mine, near, me, owners))
+    coeffs = over_planes(mine)
     far = other_core(near)
-    mine = jnp.broadcast_to(mine[None], part.shape).reshape(tok, RANK)
-    coeffs, (me, owners) = over(over_planes, mine, me, owners)
+    coeffs, near, far, me, owners = lax.optimization_barrier((coeffs, near, far, me, owners))
     coeffs_other = other_core(coeffs)
 
     dims = (chips, pairs, piece, per_block, slots, scale)
-    payload_shape = jax.ShapeDtypeStruct((chips, 2 * share, RANK), bf16)
+    payload_shape = jax.ShapeDtypeStruct((chips, share + piece, RANK), bf16)
     payload, proj = pl.pallas_call(
         functools.partial(payload_kernel, dims),
         in_specs=[SMEM] + [VMEM] * 5,

time: 114 us -> 115 us (level)
  blocking collectives: 75.7 us -> 69.5 us
  waiting for transfers between devices: 7.79 us -> 13.4 us
    ppermute x1 -> x2, waiting for transfers between devices: 1.25 us -> 9.37 us  [the longest x1 9.37 us: body(): near = jnp.concatenate([near, lax.ppermute(near, 'dp', next_y)], axis=0)]
    ppermute x4, starting transfers between devices: 13.7 us -> 7.2 us  [other_core(): return lax.ppermute(x, 'dp', swap)]
    all_to_all x1, starting transfers between devices: 3.49 us -> 8.19 us  [over_planes(): return lax.all_to_all(x, 'mp', 0, 0, tiled=True)]
    all_to_all x2, blocking collectives: 38.6 us -> 35.4 us  [over_chips(): lax.all_to_all(x, 'dp', 0, 0, axis_index_groups=same_core, tiled=True)]
    all_to_all x2, blocking collectives: 37.1 us -> 34.1 us  [over_planes(): return lax.all_to_all(x, 'mp', 0, 0, tiled=True)]
    all_to_all x1, waiting for transfers between devices: 5.91 us -> 3.63 us  [over_planes(): return lax.all_to_all(x, 'mp', 0, 0, tiled=True)]
    ppermute x1 -> x2, starting transfers between devices: 1.3 us -> 3.51 us  [the longest x1 2.13 us: body(): near = jnp.concatenate([raw, lax.ppermute(raw, 'dp', next_x)], axis=0)]
  transfers between devices with their start and end apart: 6 -> 7, of which waited for: 3 -> 3; matrix products, arithmetic and copies ran while one was open for 0% -> 1% of each run, Pallas kernels for 3% -> 3%
where the time goes in v5:
time: 115 us; the launch traced here: 114 us
  blocking collectives  69.5 us (60%)
  starting transfers between devices  18.9 us (16%)
  waiting for transfers between devices  13.4 us (12%)
  Pallas kernels  10.4 us (9%)
  other arithmetic  1.23 us (1%)
    all_to_all x2, blocking collectives, over_chips(): lax.all_to_all(x, 'dp', 0, 0, axis_index_groups=same_core, tiled=True)  35.4 us
    all_to_all x2, blocking collectives, over_planes(): return lax.all_to_all(x, 'mp', 0, 0, tiled=True)  34.1 us
    ppermute x1, waiting for transfers between devices, body(): near = jnp.concatenate([near, lax.ppermute(near, 'dp', next_y)], axis=0)  9.37 us
    all_to_all x1, starting transfers between devices, over_planes(): return lax.all_to_all(x, 'mp', 0, 0, tiled=True)  8.19 us
    ppermute x4, starting transfers between devices, other_core(): return lax.ppermute(x, 'dp', swap)  7.2 us
    pallas_call x1, Pallas kernels, coeffs_call(): pl.pallas_call(coeffs_kernel, in_specs=[SMEM] + [pl.BlockSpec(memory_spac...  5.12 us
    all_to_all x1, waiting for transfers between devices, over_planes(): return lax.all_to_all(x, 'mp', 0, 0, tiled=True)  3.63 us
  transfers between devices with their start and end apart: 7, of which 3 were waited for; matrix products, arithmetic and copies ran while one was open for 1% of the time, Pallas kernels for 3%

profile of v5, /device:TPU:1, one launch (start us, length us, event | category | flops | bytes accessed | tf_op | source)
XLA Modules:
  0.0 114.3 jit_solution(5830292558393495261)
XLA Ops:
  0.6 5.1 %shard_map.85 = (bf16[512,512]{1,0:T(8,128)(2,1)}, bf16[512,512]{1,0:T(8,128)(2,1)}, bf16[512,512]{1,0:T(8,128)(2,1)}, bf16[128,1024]{1,0:T(8,128)(2,1)}) custom-call(s32[1]{0:T(128)} %bitcast.me_ref, bf16[512,3584]{1,0:T(8,128)(2,1)} %hidden_ref.1, bf16[3584,512]{1,0:T(8,128)(2,1)} %basis_ref.3, bf16[512,1024]{1,0:T(8,128)(2,1)} %go_ref.1, ...), custom_call_target="tpu_custom_call" | custom-call | tf_op jit(solution)/shard_map/pallas_call | solution.py:98
  5.8 0.0 copy-start.5
  5.8 2.1 %collective-permute-start = (bf16[128,1024]{1,0:T(8,128)(2,1)}, bf16[128,1024]{1,0:T(8,128)(2,1)S(1)}, u32[]{:S(2)}, u32[]{:S(2)}) collective-permute-start(bf16[128,1024]{1,0:T(8,128)(2,1)} %get-tuple-element.50), channel_id=1, source_target_pairs={{0,16},{8,24},{16,0},{24,8},{32,48},{40,56},{48,32},{56,40},{64,80... | collective-permute-start | bytes 786440 | tf_op jit(solution)/shard_map/ppermute | solution.py:312
  7.9 8.2 %all-to-all-start = ((bf16[8,64,512]{2,1,0:T(8,128)(2,1)}), bf16[8,64,512]{2,1,0:T(8,128)(2,1)S(1)}, u32[]{:S(2)}, u32[]{:S(2)}) async-start(bf16[8,64,512]{2,1,0:T(8,128)(2,1)} %bitcast.18), calls=%async_computation | async-start | bytes 1048576 | tf_op jit(solution)/shard_map/all_to_all | solution.py:301
  16.1 0.0 collective-permute-done
  16.1 1.0 pad_maximum_fusion.2
  17.1 0.0 copy-start.4
  17.1 1.4 %collective-permute-start.1 = (bf16[256,1024]{1,0:T(8,128)(2,1)S(1)}, bf16[256,1024]{1,0:T(8,128)(2,1)S(1)}, u32[]{:S(2)}, u32[]{:S(2)}) collective-permute-start(bf16[256,1024]{1,0:T(8,128)(2,1)S(1)} %pad_maximum_fusion.2), channel_id=1, source_target_pairs={{0,64},{8,72},{16,80},{24,88},{32,96},{40,104},{48,112},{56,120},{... | collective-permute-start | bytes 1572872 | tf_op jit(solution)/shard_map/ppermute | solution.py:313
  18.5 1.5 %collective-permute-start.2 = (bf16[512,512]{1,0:T(8,128)(2,1)}, bf16[512,512]{1,0:T(8,128)(2,1)S(1)}, u32[]{:S(2)}, u32[]{:S(2)}) collective-permute-start(bf16[512,512]{1,0:T(8,128)(2,1)} %get-tuple-element.51), channel_id=1, source_target_pairs={{0,8},{8,0},{16,24},{24,16},{32,40},{40,32},{48,56},{56,48},{64,72... | collective-permute-start | bytes 1572872 | tf_op jit(solution)/shard_map/ppermute | solution.py:295
  20.0 9.4 %collective-permute-done.1 = bf16[256,1024]{1,0:T(8,128)(2,1)S(1)} collective-permute-done((bf16[256,1024]{1,0:T(8,128)(2,1)S(1)}, bf16[256,1024]{1,0:T(8,128)(2,1)S(1)}, u32[]{:S(2)}, u32[]{:S(2)}) %collective-permute-start.1) | collective-permute-done | bytes 524320 | tf_op jit(solution)/shard_map/ppermute | solution.py:313
  29.4 0.1 pad_maximum_fusion.near_ref
  29.5 0.0 collective-permute-done.2.other_ref
  29.5 3.6 %all-to-all-done = bf16[8,64,512]{2,1,0:T(8,128)(2,1)S(1)} async-done(((bf16[8,64,512]{2,1,0:T(8,128)(2,1)}), bf16[8,64,512]{2,1,0:T(8,128)(2,1)S(1)}, u32[]{:S(2)}, u32[]{:S(2)}) %all-to-all-start) | async-done | bytes 524320 | tf_op jit(solution)/shard_map/all_to_all | solution.py:301
  33.1 0.1 reduce_sum.12
  33.2 1.5 %collective-permute-start.3 = (bf16[512,1024]{1,0:T(8,128)(2,1)S(1)}, bf16[512,1024]{1,0:T(8,128)(2,1)S(1)}, u32[]{:S(2)}, u32[]{:S(2)}) collective-permute-start(bf16[512,1024]{1,0:T(8,128)(2,1)S(1)} %pad_maximum_fusion.near_ref), channel_id=1, source_target_pairs={{0,8},{8,0},{16,24},{24,16},{32,40},{40,32},{48,56},{56,48},{64,72... | collective-permute-start | bytes 3145736 | tf_op jit(solution)/shard_map/ppermute | solution.py:295
  34.7 21.5 %all_to_all.39 = bf16[8,64,512]{2,1,0:T(8,128)(2,1)S(1)} all-to-all(bf16[8,64,512]{2,1,0:T(8,128)(2,1)S(1)} %broadcast_in_dim.4), channel_id=1, replica_groups=mesh['dp'=32,'mp'=8] {'mp'}, dimensions={0} | all-to-all | bytes 1048576 | tf_op jit(solution)/shard_map/all_to_all | solution.py:301
  56.3 0.0 collective-permute-done.3.far_ref
  56.3 0.5 collective-permute-start.4
  56.8 1.2 %shard_map.86 = (bf16[16,48,512]{2,1,0:T(8,128)(2,1)S(1)}, f32[512,512]{1,0:T(8,128)S(1)}) custom-call(s32[1]{0:T(128)} %bitcast.me_ref, s32[1,32]{1,0:T(1,128)S(1)} %bitcast.14, bf16[512,1024]{1,0:T(8,128)(2,1)S(1)} %pad_maximum_fusion.near_ref, bf16[512,1024]{1,0:T(8,128)(2,1)S(1)} %collective-permute-done.3.far_ref, bf16[512,512]{1,0:T(8,128)(2,1)S(1)} %copy-done.3, ...), custom_call_target="tpu_custom_call" | custom-call | tf_op jit(solution)/shard_map/pallas_call | solution.py:327
  57.9 0.4 collective-permute-done.4.co_other_ref
  58.3 0.5 shard_map.87
  58.8 20.1 %all_to_all.40.got_ref = bf16[16,48,512]{2,1,0:T(8,128)(2,1)S(1)} all-to-all(bf16[16,48,512]{2,1,0:T(8,128)(2,1)S(1)} %shard_map.87), channel_id=1, replica_groups={{0,16,32,48,64,80,96,112,128,144,160,176,192,208,224,240},{8,24,40,56,7..., dimensions={0} | all-to-all | bytes 1572864 | tf_op jit(solution)/shard_map/all_to_all | solution.py:298
  78.8 0.2 shard_map.88
  79.0 12.6 %all_to_all.41 = bf16[8,32,512]{2,1,0:T(8,128)(2,1)S(1)} all-to-all(bf16[8,32,512]{2,1,0:T(8,128)(2,1)S(1)} %get-tuple-element.73), channel_id=1, replica_groups=mesh['dp'=32,'mp'=8] {'mp'}, dimensions={0} | all-to-all | bytes 524288 | tf_op jit(solution)/shard_map/all_to_all | solution.py:301
  91.7 0.0 copy-start
  91.7 0.1 pad_maximum_fusion.1
  91.7 15.3 %all_to_all.42.last_ref = bf16[16,48,512]{2,1,0:T(8,128)(2,1)S(1)} all-to-all(bf16[16,48,512]{2,1,0:T(8,128)(2,1)S(1)} %pad_maximum_fusion.1), channel_id=1, replica_groups={{0,16,32,48,64,80,96,112,128,144,160,176,192,208,224,240},{8,24,40,56,7..., dimensions={0} | all-to-all | bytes 1572864 | tf_op jit(solution)/shard_map/all_to_all | solution.py:298
  107.1 0.0 copy-start.1
  107.1 0.0 copy-start.2
  107.1 3.7 %collective-permute-start.5 = (bf16[512,512]{1,0:T(8,128)(2,1)S(1)}, bf16[512,512]{1,0:T(8,128)(2,1)S(1)}, u32[]{:S(2)}, u32[]{:S(2)}) collective-permute-start(bf16[512,512]{1,0:T(8,128)(2,1)S(1)} %bitcast.12), channel_id=1, source_target_pairs={{0,8},{8,0},{16,24},{24,16},{32,40},{40,32},{48,56},{56,48},{64,72... | collective-permute-start | bytes 1572872 | tf_op jit(solution)/shard_map/ppermute | solution.py:295
  110.8 2.0 %shard_map.89 = bf16[3584,256]{1,0:T(8,128)(2,1)} custom-call(bf16[3584,512]{1,0:T(8,128)(2,1)S(1)} %copy-done, bf16[16,48,512]{2,1,0:T(8,128)(2,1)S(1)} %all_to_all.42.last_ref), custom_call_target="tpu_custom_call" | custom-call | tf_op jit(solution)/shard_map/pallas_call | solution.py:230
  112.9 1.4 %shard_map.90 = (f32[128,512]{1,0:T(8,128)}, f32[128,512]{1,0:T(8,128)}) custom-call(s32[1]{0:T(128)} %bitcast.me_ref, s32[1,32]{1,0:T(1,128)S(1)} %bitcast.16, f32[128,512]{1,0:T(8,128)S(1)} %copy-done.1, f32[128,512]{1,0:T(8,128)S(1)} %copy-done.2, bf16[512,512]{1,0:T(8,128)(2,1)S(1)} %bitcast.13, bf16[512,512]{1,0:T(8,128)(2,1)S(1)} %collective-permute-done.5.sums_other_ref), custom_call_target="tpu_custom_call" | custom-call | tf_op jit(solution)/shard_map/pallas_call | solution.py:370
  (11 shorter events, 0.1 us)
Async XLA Ops:
  5.8 23.6 %copy-start.5 = (bf16[128,1024]{1,0:T(8,128)(2,1)S(1)}, bf16[128,1024]{1,0:T(8,128)(2,1)}, u32[]{:S(2)}) copy-start(bf16[128,1024]{1,0:T(8,128)(2,1)} %get-tuple-element.50) | copy-start | bytes 786436
  5.8 10.3 %collective-permute-start = (bf16[128,1024]{1,0:T(8,128)(2,1)}, bf16[128,1024]{1,0:T(8,128)(2,1)S(1)}, u32[]{:S(2)}, u32[]{:S(2)}) collective-permute-start(bf16[128,1024]{1,0:T(8,128)(2,1)} %get-tuple-element.50), channel_id=1, source_target_pairs={{0,16},{8,24},{16,0},{24,8},{32,48},{40,56},{48,32},{56,40},{64,80... | collective-permute-start | bytes 786440 | tf_op jit(solution)/shard_map/ppermute | solution.py:312
  7.9 25.2 %all-to-all-start = ((bf16[8,64,512]{2,1,0:T(8,128)(2,1)}), bf16[8,64,512]{2,1,0:T(8,128)(2,1)S(1)}, u32[]{:S(2)}, u32[]{:S(2)}) async-start(bf16[8,64,512]{2,1,0:T(8,128)(2,1)} %bitcast.18), calls=%async_computation | async-start | bytes 1048576 | tf_op jit(solution)/shard_map/all_to_all | solution.py:301
  17.1 39.6 %copy-start.3 = (bf16[512,512]{1,0:T(8,128)(2,1)S(1)}, bf16[512,512]{1,0:T(8,128)(2,1)}, u32[]{:S(2)}) copy-start(bf16[512,512]{1,0:T(8,128)(2,1)} %get-tuple-element.64.mine_ref) | copy-start | bytes 1572868
  17.1 39.6 %copy-start.4 = (s32[32,1]{0,1:T(1,128)S(1)}, s32[32,1]{0,1:T(1,128)}, u32[]{:S(2)}) copy-start(s32[32,1]{0,1:T(1,128)} %param.9) | copy-start | bytes 388
  17.1 12.3 %collective-permute-start.1 = (bf16[256,1024]{1,0:T(8,128)(2,1)S(1)}, bf16[256,1024]{1,0:T(8,128)(2,1)S(1)}, u32[]{:S(2)}, u32[]{:S(2)}) collective-permute-start(bf16[256,1024]{1,0:T(8,128)(2,1)S(1)} %pad_maximum_fusion.2), channel_id=1, source_target_pairs={{0,64},{8,72},{16,80},{24,88},{32,96},{40,104},{48,112},{56,120},{... | collective-permute-start | bytes 1572872 | tf_op jit(solution)/shard_map/ppermute | solution.py:313
  18.5 11.0 %collective-permute-start.2 = (bf16[512,512]{1,0:T(8,128)(2,1)}, bf16[512,512]{1,0:T(8,128)(2,1)S(1)}, u32[]{:S(2)}, u32[]{:S(2)}) collective-permute-start(bf16[512,512]{1,0:T(8,128)(2,1)} %get-tuple-element.51), channel_id=1, source_target_pairs={{0,8},{8,0},{16,24},{24,16},{32,40},{40,32},{48,56},{56,48},{64,72... | collective-permute-start | bytes 1572872 | tf_op jit(solution)/shard_map/ppermute | solution.py:295
  33.2 23.0 %collective-permute-start.3 = (bf16[512,1024]{1,0:T(8,128)(2,1)S(1)}, bf16[512,1024]{1,0:T(8,128)(2,1)S(1)}, u32[]{:S(2)}, u32[]{:S(2)}) collective-permute-start(bf16[512,1024]{1,0:T(8,128)(2,1)S(1)} %pad_maximum_fusion.near_ref), channel_id=1, source_target_pairs={{0,8},{8,0},{16,24},{24,16},{32,40},{40,32},{48,56},{56,48},{64,72... | collective-permute-start | bytes 3145736 | tf_op jit(solution)/shard_map/ppermute | solution.py:295
  56.3 2.0 %collective-permute-start.4 = (bf16[512,512]{1,0:T(8,128)(2,1)S(1)}, bf16[512,512]{1,0:T(8,128)(2,1)S(1)}, u32[]{:S(2)}, u32[]{:S(2)}) collective-permute-start(bf16[512,512]{1,0:T(8,128)(2,1)S(1)} %bitcast.10), channel_id=1, source_target_pairs={{0,8},{8,0},{16,24},{24,16},{32,40},{40,32},{48,56},{56,48},{64,72... | collective-permute-start | bytes 1572872 | tf_op jit(solution)/shard_map/ppermute | solution.py:295
  91.7 19.1 %copy-start = (bf16[3584,512]{1,0:T(8,128)(2,1)S(1)}, bf16[3584,512]{1,0:T(8,128)(2,1)}, u32[]{:S(2)}) copy-start(bf16[3584,512]{1,0:T(8,128)(2,1)} %basis_ref.3) | copy-start | bytes 11010052
  107.1 5.8 %copy-start.1 = (f32[128,512]{1,0:T(8,128)S(1)}, f32[128,512]{1,0:T(8,128)}, u32[]{:S(2)}) copy-start(f32[128,512]{1,0:T(8,128)} %first_ref.2) | copy-start | bytes 786436
  107.1 5.8 %copy-start.2 = (f32[128,512]{1,0:T(8,128)S(1)}, f32[128,512]{1,0:T(8,128)}, u32[]{:S(2)}) copy-start(f32[128,512]{1,0:T(8,128)} %second_ref.2) | copy-start | bytes 786436
  107.1 5.8 %collective-permute-start.5 = (bf16[512,512]{1,0:T(8,128)(2,1)S(1)}, bf16[512,512]{1,0:T(8,128)(2,1)S(1)}, u32[]{:S(2)}, u32[]{:S(2)}) collective-permute-start(bf16[512,512]{1,0:T(8,128)(2,1)S(1)} %bitcast.12), channel_id=1, source_target_pairs={{0,8},{8,0},{16,24},{24,16},{32,40},{40,32},{48,56},{56,48},{64,72... | collective-permute-start | bytes 1572872 | tf_op jit(solution)/shard_map/ppermute | solution.py:295

commit v6 on v5

--- a/solution.py
+++ b/solution.py
@@ -42,9 +42,13 @@
     return jnp.sum((same & (f0 < f1)).astype(jnp.int32), axis=0, keepdims=True)
 
 
+def in_square(chip):
+    return (chip & 1) + 2 * ((chip >> 2) & 1), ((chip >> 1) & 1) + 2 * (chip >> 3)
+
+
 def coeffs_kernel(
     me_ref, hidden_ref, basis_ref, go_ref, first_ref, second_ref,
-    part_ref, mine_ref, other_ref, raw_ref,
+    part_ref, mine_ref, other_ref, keep_ref, send_ref,
     hidden, basis, go, first, second, total, sems,
 ):
     step = hidden.shape[2]
@@ -79,8 +83,17 @@
         if j == 2:
             for copy in extra:
                 copy.wait()
-            raw_ref[:, :RANK] = first[...].astype(bf16)
-            raw_ref[:, RANK:] = second[...].astype(bf16)
+            place = in_square(me_ref[0] >> 1)[0]
+            quarter = RANK // SQUARE
+            for n, ref in enumerate((first, second)):
+                old = [ref[:, q * quarter : (q + 1) * quarter].astype(bf16) for q in range(SQUARE)]
+                for d, out in enumerate((keep_ref, send_ref)):
+                    for e in range(2):
+                        at = slice((2 * e + n) * quarter, (2 * e + n + 1) * quarter)
+                        q = place ^ (d + 2 * e)
+                        low = jnp.where((q & 1) == 0, old[0], old[1])
+                        high = jnp.where((q & 1) == 0, old[2], old[3])
+                        out[:, at] = jnp.where(q < 2, low, high)
             even = (me_ref[0] & 1) == 0
             width = go.shape[1] // 4
             for p in range(2):
@@ -98,12 +111,13 @@
     return pl.pallas_call(
         coeffs_kernel,
         in_specs=[SMEM] + [pl.BlockSpec(memory_space=pltpu.HBM)] * 5,
-        out_specs=[VMEM] * 4,
+        out_specs=[VMEM] * 5,
         out_shape=[
             like(tok, RANK),
             like(tok, go.shape[1] // 2),
             like(tok, go.shape[1] // 2),
-            like(held, 2 * RANK),
+            like(held, RANK),
+            like(held, RANK),
         ],
         scratch_shapes=[
             pltpu.VMEM((STEPS, tok, step), bf16),
@@ -119,10 +133,6 @@
 
 
 OVER_TOKENS = (((0,), (0,)), ((), ()))
-
-
-def in_square(chip):
-    return (chip & 1) + 2 * ((chip >> 2) & 1), ((chip >> 1) & 1) + 2 * (chip >> 3)
 
 
 def payload_kernel(
@@ -147,14 +157,11 @@
     cols = iota((1, SQUARE * held), 1)
     hot = jnp.where(rows == cols, 1.0, 0.0).astype(bf16)
     hot_far = jnp.where(rows == cols + SQUARE * held, 1.0, 0.0).astype(bf16)
-    width = RANK // SQUARE
-    for n in range(2):
-        at_n = pl.ds(pl.multiple_of(n * RANK + in_square(chip)[0] * width, 128), width)
-        old = jnp.dot(hot, near_ref[:, at_n], preferred_element_type=f32)
-        old += jnp.dot(hot_far, far_ref[:, at_n], preferred_element_type=f32)
-        old = old.astype(bf16).reshape(chips, pairs, piece, width)
-        for p in range(pairs):
-            out_ref[:, share:, (2 * p + n) * width : (2 * p + n + 1) * width] = old[:, p]
+    old = jnp.dot(hot, near_ref[...], preferred_element_type=f32)
+    old += jnp.dot(hot_far, far_ref[...], preferred_element_type=f32)
+    old = old.astype(bf16).reshape(chips, pairs, piece, near_ref.shape[1])
+    for p in range(pairs):
+        out_ref[:, share:, p * old.shape[3] : (p + 1) * old.shape[3]] = old[:, p]
     proj_ref[...] = lax.dot_general(
         mine_ref[...], co_ref[...], OVER_TOKENS, preferred_element_type=f32
     )
@@ -303,14 +310,15 @@
     me = lax.axis_index("dp").reshape(1)
     owners = owners.reshape(1, frags)
 
-    part, go_mine, go_theirs, raw = coeffs_call(
+    part, go_mine, go_theirs, keep, send = coeffs_call(
         me, hidden, basis, grad_out, first_moment, second_moment
     )
-    part, go_theirs, raw = lax.optimization_barrier((part, go_theirs, raw))
+    part, go_theirs, keep, send = lax.optimization_barrier((part, go_theirs, keep, send))
 
     part = over_planes(part)
-    near = jnp.concatenate([raw, lax.ppermute(raw, "dp", next_x)], axis=0)
-    near = jnp.concatenate([near, lax.ppermute(near, "dp", next_y)], axis=0)
+    near = jnp.concatenate([keep, lax.ppermute(send, "dp", next_x)], axis=0)
+    keep, send = near[:, : RANK // 2], near[:, RANK // 2 :]
+    near = jnp.concatenate([keep, lax.ppermute(send, "dp", next_y)], axis=0)
     go_other = other_core(go_theirs)
     part, near, go_other = lax.optimization_barrier((part, near, go_other))
     part = part.reshape(planes, tok // planes, RANK)

time: 115 us -> 114 us (level)
  blocking collectives: 69.5 us -> 48.2 us
  waiting for transfers between devices: 13.4 us -> 31 us
  starting transfers between devices: 18.9 us -> 21.1 us
  local copies, waits for them, and re-layouts: 0.15 us -> 1.88 us
    all_to_all x1 -> x2, waiting for transfers between devices: 3.63 us -> 25.8 us  [over_planes(): return lax.all_to_all(x, 'mp', 0, 0, tiled=True)]
    all_to_all x2 -> x1, blocking collectives: 34.1 us -> 12.6 us  [over_planes(): return lax.all_to_all(x, 'mp', 0, 0, tiled=True)]
    ppermute x2, waiting for transfers between devices: 9.37 us -> 3.46 us  [the longest x1 2.82 us: body(): near = jnp.concatenate([keep, lax.ppermute(send, 'dp', next_y)], axis=0)]
    all_to_all x1 -> x2, starting transfers between devices: 8.19 us -> 12.5 us  [over_planes(): return lax.all_to_all(x, 'mp', 0, 0, tiled=True)]
    ppermute x4, waiting for transfers between devices: 0.37 us -> 1.76 us  [other_core(): return lax.ppermute(x, 'dp', swap)]
    ppermute x4, starting transfers between devices: 7.2 us -> 6.02 us  [other_core(): return lax.ppermute(x, 'dp', swap)]
  transfers between devices with their start and end apart: 7 -> 8, of which waited for: 3 -> 6; matrix products, arithmetic and copies ran while one was open for 1% -> 1% of each run, Pallas kernels for 3% -> 3%
where the time goes in v6:
time: 114 us; the launch traced here: 113 us
  blocking collectives  48.2 us (42%)
  waiting for transfers between devices  31 us (27%)
  starting transfers between devices  21.1 us (19%)
  Pallas kernels  10.2 us (9%)
  local copies, waits for them, and re-layouts  1.88 us (2%)
    all_to_all x2, blocking collectives, over_chips(): lax.all_to_all(x, 'dp', 0, 0, axis_index_groups=same_core, tiled=True)  35.7 us
    all_to_all x2, waiting for transfers between devices, over_planes(): return lax.all_to_all(x, 'mp', 0, 0, tiled=True)  25.8 us
    all_to_all x1, blocking collectives, over_planes(): return lax.all_to_all(x, 'mp', 0, 0, tiled=True)  12.6 us
    all_to_all x2, starting transfers between devices, over_planes(): return lax.all_to_all(x, 'mp', 0, 0, tiled=True)  12.5 us
    ppermute x4, starting transfers between devices, other_core(): return lax.ppermute(x, 'dp', swap)  6.02 us
    pallas_call x1, Pallas kernels, coeffs_call(): pl.pallas_call(coeffs_kernel, in_specs=[SMEM] + [pl.BlockSpec(memory_spac...  5.18 us
    ppermute x1, waiting for transfers between devices, body(): near = jnp.concatenate([keep, lax.ppermute(send, 'dp', next_y)], axis=0)  2.82 us
  transfers between devices with their start and end apart: 8, of which 6 were waited for; matrix products, arithmetic and copies ran while one was open for 1% of the time, Pallas kernels for 3%

profile of v6, /device:TPU:1, one launch (start us, length us, event | category | flops | bytes accessed | tf_op | source)
XLA Modules:
  0.0 113.4 jit_solution(3358105930166877712)
XLA Ops:
  0.6 5.2 %shard_map.85 = (bf16[512,512]{1,0:T(8,128)(2,1)}, bf16[512,512]{1,0:T(8,128)(2,1)}, bf16[512,512]{1,0:T(8,128)(2,1)}, bf16[128,512]{1,0:T(8,128)(2,1)}, bf16[128,512]{1,0:T(8,128)(2,1)}) custom-call(s32[1]{0:T(128)} %bitcast.me_ref, bf16[512,3584]{1,0:T(8,128)(2,1)} %hidden_ref.1, bf16[3584,512]{1,0:T(8,128)(2,1)} %basis_ref.3, bf16[512,1024]{1,0:T(8,128)(2,1)} %go_ref.1, ...), custom_call_target="tpu_custom_call" | custom-call | tf_op jit(solution)/shard_map/pallas_call | solution.py:111
  5.8 9.0 %all-to-all-start = ((bf16[8,64,512]{2,1,0:T(8,128)(2,1)}), bf16[8,64,512]{2,1,0:T(8,128)(2,1)S(1)}, u32[]{:S(2)}, u32[]{:S(2)}) async-start(bf16[8,64,512]{2,1,0:T(8,128)(2,1)} %bitcast.18), calls=%async_computation | async-start | bytes 1048576 | tf_op jit(solution)/shard_map/all_to_all | solution.py:308
  14.8 1.2 %collective-permute-start = (bf16[128,512]{1,0:T(8,128)(2,1)}, bf16[128,512]{1,0:T(8,128)(2,1)S(1)}, u32[]{:S(2)}, u32[]{:S(2)}) collective-permute-start(bf16[128,512]{1,0:T(8,128)(2,1)} %get-tuple-element.54), channel_id=1, source_target_pairs={{0,16},{8,24},{16,0},{24,8},{32,48},{40,56},{48,32},{56,40},{64,80... | collective-permute-start | bytes 393224 | tf_op jit(solution)/shard_map/ppermute | solution.py:319
  16.1 1.2 %collective-permute-start.2 = (bf16[512,512]{1,0:T(8,128)(2,1)}, bf16[512,512]{1,0:T(8,128)(2,1)S(1)}, u32[]{:S(2)}, u32[]{:S(2)}) collective-permute-start(bf16[512,512]{1,0:T(8,128)(2,1)} %get-tuple-element.55), channel_id=1, source_target_pairs={{0,8},{8,0},{16,24},{24,16},{32,40},{40,32},{48,56},{56,48},{64,72... | collective-permute-start | bytes 1572872 | tf_op jit(solution)/shard_map/ppermute | solution.py:302
  17.3 0.9 constant_dynamic-update-slice_fusion.1
  18.2 0.0 copy-start.4
  18.2 0.6 collective-permute-done
  18.9 1.4 %collective-permute-start.1 = (bf16[256,256]{1,0:T(8,128)(2,1)S(1)}, bf16[256,256]{1,0:T(8,128)(2,1)S(1)}, u32[]{:S(2)}, u32[]{:S(2)}) collective-permute-start(bf16[256,256]{1,0:T(8,128)(2,1)S(1)} %get-tuple-element.94), channel_id=1, source_target_pairs={{0,64},{8,72},{16,80},{24,88},{32,96},{40,104},{48,112},{56,120},{... | collective-permute-start | bytes 393224 | tf_op jit(solution)/shard_map/ppermute | solution.py:321
  20.3 2.8 %collective-permute-done.1 = bf16[256,256]{1,0:T(8,128)(2,1)S(1)} collective-permute-done((bf16[256,256]{1,0:T(8,128)(2,1)S(1)}, bf16[256,256]{1,0:T(8,128)(2,1)S(1)}, u32[]{:S(2)}, u32[]{:S(2)}) %collective-permute-start.1) | collective-permute-done | bytes 131104 | tf_op jit(solution)/shard_map/ppermute | solution.py:321
  23.1 0.0 collective-permute-done.2.other_ref
  23.2 9.7 %all-to-all-done = bf16[8,64,512]{2,1,0:T(8,128)(2,1)S(1)} async-done(((bf16[8,64,512]{2,1,0:T(8,128)(2,1)}), bf16[8,64,512]{2,1,0:T(8,128)(2,1)S(1)}, u32[]{:S(2)}, u32[]{:S(2)}) %all-to-all-start) | async-done | bytes 524320 | tf_op jit(solution)/shard_map/all_to_all | solution.py:308
  32.8 0.1 reduce_sum.12
  32.9 0.8 broadcast_in_dim.4
  33.7 3.5 %all-to-all-start.1 = ((bf16[8,64,512]{2,1,0:T(8,128)(2,1)}), bf16[8,64,512]{2,1,0:T(8,128)(2,1)S(1)}, u32[]{:S(2)}, u32[]{:S(2)}) async-start(bf16[8,64,512]{2,1,0:T(8,128)(2,1)} %bitcast.6), calls=%async_computation.1 | async-start | bytes 1048576 | tf_op jit(solution)/shard_map/all_to_all | solution.py:308
  37.2 0.6 collective-permute-start.3
  37.8 1.2 %collective-permute-done.3.far_ref = bf16[512,256]{1,0:T(8,128)(2,1)S(1)} collective-permute-done((bf16[512,256]{1,0:T(8,128)(2,1)S(1)}, bf16[512,256]{1,0:T(8,128)(2,1)S(1)}, u32[]{:S(2)}, u32[]{:S(2)}) %collective-permute-start.3) | collective-permute-done | bytes 262176 | tf_op jit(solution)/shard_map/ppermute | solution.py:302
  39.0 16.1 %all-to-all-done.1 = bf16[8,64,512]{2,1,0:T(8,128)(2,1)S(1)} async-done(((bf16[8,64,512]{2,1,0:T(8,128)(2,1)}), bf16[8,64,512]{2,1,0:T(8,128)(2,1)S(1)}, u32[]{:S(2)}, u32[]{:S(2)}) %all-to-all-start.1) | async-done | bytes 524320 | tf_op jit(solution)/shard_map/all_to_all | solution.py:308
  55.1 0.5 collective-permute-start.4
  55.6 0.9 shard_map.86
  56.5 0.6 collective-permute-done.4.co_other_ref
  57.1 0.5 shard_map.87
  57.6 20.4 %all_to_all.39.got_ref = bf16[16,48,512]{2,1,0:T(8,128)(2,1)S(1)} all-to-all(bf16[16,48,512]{2,1,0:T(8,128)(2,1)S(1)} %shard_map.87), channel_id=1, replica_groups={{0,16,32,48,64,80,96,112,128,144,160,176,192,208,224,240},{8,24,40,56,7..., dimensions={0} | all-to-all | bytes 1572864 | tf_op jit(solution)/shard_map/all_to_all | solution.py:305
  78.0 0.2 shard_map.88
  78.1 12.6 %all_to_all.40 = bf16[8,32,512]{2,1,0:T(8,128)(2,1)S(1)} all-to-all(bf16[8,32,512]{2,1,0:T(8,128)(2,1)S(1)} %get-tuple-element.77), channel_id=1, replica_groups=mesh['dp'=32,'mp'=8] {'mp'}, dimensions={0} | all-to-all | bytes 524288 | tf_op jit(solution)/shard_map/all_to_all | solution.py:308
  90.8 0.0 copy-start
  90.8 0.1 pad_maximum_fusion
  90.9 15.3 %all_to_all.41.last_ref = bf16[16,48,512]{2,1,0:T(8,128)(2,1)S(1)} all-to-all(bf16[16,48,512]{2,1,0:T(8,128)(2,1)S(1)} %pad_maximum_fusion), channel_id=1, replica_groups={{0,16,32,48,64,80,96,112,128,144,160,176,192,208,224,240},{8,24,40,56,7..., dimensions={0} | all-to-all | bytes 1572864 | tf_op jit(solution)/shard_map/all_to_all | solution.py:305
  106.2 0.0 copy-start.1
  106.2 0.0 copy-start.2
  106.2 3.7 %collective-permute-start.5 = (bf16[512,512]{1,0:T(8,128)(2,1)S(1)}, bf16[512,512]{1,0:T(8,128)(2,1)S(1)}, u32[]{:S(2)}, u32[]{:S(2)}) collective-permute-start(bf16[512,512]{1,0:T(8,128)(2,1)S(1)} %bitcast.12), channel_id=1, source_target_pairs={{0,8},{8,0},{16,24},{24,16},{32,40},{40,32},{48,56},{56,48},{64,72... | collective-permute-start | bytes 1572872 | tf_op jit(solution)/shard_map/ppermute | solution.py:302
  109.9 2.0 %shard_map.89 = bf16[3584,256]{1,0:T(8,128)(2,1)} custom-call(bf16[3584,512]{1,0:T(8,128)(2,1)S(1)} %copy-done, bf16[16,48,512]{2,1,0:T(8,128)(2,1)S(1)} %all_to_all.41.last_ref), custom_call_target="tpu_custom_call" | custom-call | tf_op jit(solution)/shard_map/pallas_call | solution.py:237
  112.0 1.4 %shard_map.90 = (f32[128,512]{1,0:T(8,128)}, f32[128,512]{1,0:T(8,128)}) custom-call(s32[1]{0:T(128)} %bitcast.me_ref, s32[1,32]{1,0:T(1,128)S(1)} %bitcast.16, f32[128,512]{1,0:T(8,128)S(1)} %copy-done.1, f32[128,512]{1,0:T(8,128)S(1)} %copy-done.2, bf16[512,512]{1,0:T(8,128)(2,1)S(1)} %bitcast.13, bf16[512,512]{1,0:T(8,128)(2,1)S(1)} %collective-permute-done.5.sums_other_ref), custom_call_target="tpu_custom_call" | custom-call | tf_op jit(solution)/shard_map/pallas_call | solution.py:378
  (12 shorter events, 0.1 us)
Async XLA Ops:
  5.8 27.0 %all-to-all-start = ((bf16[8,64,512]{2,1,0:T(8,128)(2,1)}), bf16[8,64,512]{2,1,0:T(8,128)(2,1)S(1)}, u32[]{:S(2)}, u32[]{:S(2)}) async-start(bf16[8,64,512]{2,1,0:T(8,128)(2,1)} %bitcast.18), calls=%async_computation | async-start | bytes 1048576 | tf_op jit(solution)/shard_map/all_to_all | solution.py:308
  14.8 4.0 %collective-permute-start = (bf16[128,512]{1,0:T(8,128)(2,1)}, bf16[128,512]{1,0:T(8,128)(2,1)S(1)}, u32[]{:S(2)}, u32[]{:S(2)}) collective-permute-start(bf16[128,512]{1,0:T(8,128)(2,1)} %get-tuple-element.54), channel_id=1, source_target_pairs={{0,16},{8,24},{16,0},{24,8},{32,48},{40,56},{48,32},{56,40},{64,80... | collective-permute-start | bytes 393224 | tf_op jit(solution)/shard_map/ppermute | solution.py:319
  16.1 7.1 %collective-permute-start.2 = (bf16[512,512]{1,0:T(8,128)(2,1)}, bf16[512,512]{1,0:T(8,128)(2,1)S(1)}, u32[]{:S(2)}, u32[]{:S(2)}) collective-permute-start(bf16[512,512]{1,0:T(8,128)(2,1)} %get-tuple-element.55), channel_id=1, source_target_pairs={{0,8},{8,0},{16,24},{24,16},{32,40},{40,32},{48,56},{56,48},{64,72... | collective-permute-start | bytes 1572872 | tf_op jit(solution)/shard_map/ppermute | solution.py:302
  18.2 37.4 %copy-start.3 = (bf16[512,512]{1,0:T(8,128)(2,1)S(1)}, bf16[512,512]{1,0:T(8,128)(2,1)}, u32[]{:S(2)}) copy-start(bf16[512,512]{1,0:T(8,128)(2,1)} %get-tuple-element.68.mine_ref) | copy-start | bytes 1572868
  18.2 37.4 %copy-start.4 = (s32[32,1]{0,1:T(1,128)S(1)}, s32[32,1]{0,1:T(1,128)}, u32[]{:S(2)}) copy-start(s32[32,1]{0,1:T(1,128)} %param.9) | copy-start | bytes 388
  18.9 4.2 %collective-permute-start.1 = (bf16[256,256]{1,0:T(8,128)(2,1)S(1)}, bf16[256,256]{1,0:T(8,128)(2,1)S(1)}, u32[]{:S(2)}, u32[]{:S(2)}) collective-permute-start(bf16[256,256]{1,0:T(8,128)(2,1)S(1)} %get-tuple-element.94), channel_id=1, source_target_pairs={{0,64},{8,72},{16,80},{24,88},{32,96},{40,104},{48,112},{56,120},{... | collective-permute-start | bytes 393224 | tf_op jit(solution)/shard_map/ppermute | solution.py:321
  33.7 21.4 %all-to-all-start.1 = ((bf16[8,64,512]{2,1,0:T(8,128)(2,1)}), bf16[8,64,512]{2,1,0:T(8,128)(2,1)S(1)}, u32[]{:S(2)}, u32[]{:S(2)}) async-start(bf16[8,64,512]{2,1,0:T(8,128)(2,1)} %bitcast.6), calls=%async_computation.1 | async-start | bytes 1048576 | tf_op jit(solution)/shard_map/all_to_all | solution.py:308
  37.2 1.7 %collective-permute-start.3 = (bf16[512,256]{1,0:T(8,128)(2,1)S(1)}, bf16[512,256]{1,0:T(8,128)(2,1)S(1)}, u32[]{:S(2)}, u32[]{:S(2)}) collective-permute-start(bf16[512,256]{1,0:T(8,128)(2,1)S(1)} %pad_maximum_fusion.1.near_ref), channel_id=1, source_target_pairs={{0,8},{8,0},{16,24},{24,16},{32,40},{40,32},{48,56},{56,48},{64,72... | collective-permute-start | bytes 786440 | tf_op jit(solution)/shard_map/ppermute | solution.py:302
  55.1 2.0 %collective-permute-start.4 = (bf16[512,512]{1,0:T(8,128)(2,1)S(1)}, bf16[512,512]{1,0:T(8,128)(2,1)S(1)}, u32[]{:S(2)}, u32[]{:S(2)}) collective-permute-start(bf16[512,512]{1,0:T(8,128)(2,1)S(1)} %bitcast.10), channel_id=1, source_target_pairs={{0,8},{8,0},{16,24},{24,16},{32,40},{40,32},{48,56},{56,48},{64,72... | collective-permute-start | bytes 1572872 | tf_op jit(solution)/shard_map/ppermute | solution.py:302
  90.8 19.2 %copy-start = (bf16[3584,512]{1,0:T(8,128)(2,1)S(1)}, bf16[3584,512]{1,0:T(8,128)(2,1)}, u32[]{:S(2)}) copy-start(bf16[3584,512]{1,0:T(8,128)(2,1)} %basis_ref.3) | copy-start | bytes 11010052
  106.2 5.8 %copy-start.1 = (f32[128,512]{1,0:T(8,128)S(1)}, f32[128,512]{1,0:T(8,128)}, u32[]{:S(2)}) copy-start(f32[128,512]{1,0:T(8,128)} %first_ref.2) | copy-start | bytes 786436
  106.2 5.8 %copy-start.2 = (f32[128,512]{1,0:T(8,128)S(1)}, f32[128,512]{1,0:T(8,128)}, u32[]{:S(2)}) copy-start(f32[128,512]{1,0:T(8,128)} %second_ref.2) | copy-start | bytes 786436
  106.2 5.7 %collective-permute-start.5 = (bf16[512,512]{1,0:T(8,128)(2,1)S(1)}, bf16[512,512]{1,0:T(8,128)(2,1)S(1)}, u32[]{:S(2)}, u32[]{:S(2)}) collective-permute-start(bf16[512,512]{1,0:T(8,128)(2,1)S(1)} %bitcast.12), channel_id=1, source_target_pairs={{0,8},{8,0},{16,24},{24,16},{32,40},{40,32},{48,56},{56,48},{64,72... | collective-permute-start | bytes 1572872 | tf_op jit(solution)/shard_map/ppermute | solution.py:302

commit v7 on v6

--- a/solution.py
+++ b/solution.py
@@ -46,11 +46,7 @@
     return (chip & 1) + 2 * ((chip >> 2) & 1), ((chip >> 1) & 1) + 2 * (chip >> 3)
 
 
-def coeffs_kernel(
-    me_ref, hidden_ref, basis_ref, go_ref, first_ref, second_ref,
-    part_ref, mine_ref, other_ref, keep_ref, send_ref,
-    hidden, basis, go, first, second, total, sems,
-):
+def coeffs_kernel(hidden_ref, basis_ref, part_ref, hidden, basis, total, sems):
     step = hidden.shape[2]
 
     def chunk(j):
@@ -61,15 +57,9 @@
         )
 
     chunks = [chunk(j) for j in range(STEPS)]
-    extra = [
-        pltpu.make_async_copy(first_ref, first, sems.at[2 * STEPS]),
-        pltpu.make_async_copy(second_ref, second, sems.at[2 * STEPS + 1]),
-        pltpu.make_async_copy(go_ref, go, sems.at[2 * STEPS + 2]),
-    ]
-    for copy in [c for pair in chunks[:2] for c in pair] + extra:
-        copy.start()
-    for copy in [c for pair in chunks[2:] for c in pair]:
-        copy.start()
+    for pair in chunks:
+        for copy in pair:
+            copy.start()
     for j in range(STEPS):
         for copy in chunks[j]:
             copy.wait()
@@ -80,56 +70,63 @@
             total[...] += term
         else:
             part_ref[...] = (total[...] + term).astype(bf16)
-        if j == 2:
-            for copy in extra:
-                copy.wait()
-            place = in_square(me_ref[0] >> 1)[0]
-            quarter = RANK // SQUARE
-            for n, ref in enumerate((first, second)):
-                old = [ref[:, q * quarter : (q + 1) * quarter].astype(bf16) for q in range(SQUARE)]
-                for d, out in enumerate((keep_ref, send_ref)):
-                    for e in range(2):
-                        at = slice((2 * e + n) * quarter, (2 * e + n + 1) * quarter)
-                        q = place ^ (d + 2 * e)
-                        low = jnp.where((q & 1) == 0, old[0], old[1])
-                        high = jnp.where((q & 1) == 0, old[2], old[3])
-                        out[:, at] = jnp.where(q < 2, low, high)
-            even = (me_ref[0] & 1) == 0
-            width = go.shape[1] // 4
-            for p in range(2):
-                low = go[:, (2 * p) * width : (2 * p + 1) * width]
-                high = go[:, (2 * p + 1) * width : (2 * p + 2) * width]
-                mine_ref[:, p * width : (p + 1) * width] = jnp.where(even, low, high)
-                other_ref[:, p * width : (p + 1) * width] = jnp.where(even, high, low)
-
-
-def coeffs_call(me, hidden, basis, go, first, second):
+
+
+def coeffs_call(hidden, basis):
     tok, ff = hidden.shape
     step = ff // STEPS
-    held = first.shape[0]
-    like = lambda *shape: jax.ShapeDtypeStruct(shape, bf16)
     return pl.pallas_call(
         coeffs_kernel,
-        in_specs=[SMEM] + [pl.BlockSpec(memory_space=pltpu.HBM)] * 5,
-        out_specs=[VMEM] * 5,
-        out_shape=[
-            like(tok, RANK),
-            like(tok, go.shape[1] // 2),
-            like(tok, go.shape[1] // 2),
-            like(held, RANK),
-            like(held, RANK),
-        ],
+        in_specs=[pl.BlockSpec(memory_space=pl.ANY)] * 2,
+        out_specs=VMEM,
+        out_shape=jax.ShapeDtypeStruct((tok, RANK), bf16),
         scratch_shapes=[
             pltpu.VMEM((STEPS, tok, step), bf16),
             pltpu.VMEM((STEPS, step, RANK), bf16),
-            pltpu.VMEM(go.shape, bf16),
-            pltpu.VMEM(first.shape, f32),
-            pltpu.VMEM(second.shape, f32),
             pltpu.VMEM((tok, RANK), f32),
-            pltpu.SemaphoreType.DMA((2 * STEPS + 3,)),
+            pltpu.SemaphoreType.DMA((2 * STEPS,)),
         ],
         compiler_params=kernel_params(56),
-    )(me, hidden, basis, go, first, second)
+    )(hidden, basis)
+
+
+def sort_kernel(me_ref, go_ref, first_ref, second_ref, mine_ref, other_ref, keep_ref, send_ref):
+    even = (me_ref[0] & 1) == 0
+    width = go_ref.shape[1] // 4
+    for p in range(2):
+        low = go_ref[:, (2 * p) * width : (2 * p + 1) * width]
+        high = go_ref[:, (2 * p + 1) * width : (2 * p + 2) * width]
+        mine_ref[:, p * width : (p + 1) * width] = jnp.where(even, low, high)
+        other_ref[:, p * width : (p + 1) * width] = jnp.where(even, high, low)
+    place = in_square(me_ref[0] >> 1)[0]
+    width = RANK // SQUARE
+    for n, ref in enumerate((first_ref, second_ref)):
+        old = [ref[:, q * width : (q + 1) * width].astype(bf16) for q in range(SQUARE)]
+        for d, out in enumerate((keep_ref, send_ref)):
+            for e in range(2):
+                at = slice((2 * e + n) * width, (2 * e + n + 1) * width)
+                q = place ^ (d + 2 * e)
+                low = jnp.where((q & 1) == 0, old[0], old[1])
+                high = jnp.where((q & 1) == 0, old[2], old[3])
+                out[:, at] = jnp.where(q < 2, low, high)
+
+
+def sort_call(me, go, first, second):
+    tok, col = go.shape
+    like = lambda *shape: jax.ShapeDtypeStruct(shape, bf16)
+    return pl.pallas_call(
+        sort_kernel,
+        in_specs=[SMEM] + [VMEM] * 3,
+        out_specs=[VMEM] * 4,
+        out_shape=[
+            like(tok, col // 2),
+            like(tok, col // 2),
+            like(first.shape[0], RANK),
+            like(first.shape[0], RANK),
+        ],
+        compiler_params=kernel_params(),
+        cost_estimate=pl.CostEstimate(flops=2**28, bytes_accessed=2**24, transcendentals=0),
+    )(me, go, first, second)
 
 
 OVER_TOKENS = (((0,), (0,)), ((), ()))
@@ -310,24 +307,26 @@
     me = lax.axis_index("dp").reshape(1)
     owners = owners.reshape(1, frags)
 
-    part, go_mine, go_theirs, keep, send = coeffs_call(
-        me, hidden, basis, grad_out, first_moment, second_moment
-    )
-    part, go_theirs, keep, send = lax.optimization_barrier((part, go_theirs, keep, send))
-
+    part = coeffs_call(hidden, basis)
+    part, grad_out, first, second = lax.optimization_barrier(
+        (part, grad_out, first_moment, second_moment)
+    )
     part = over_planes(part)
+    go_mine, go_theirs, keep, send = sort_call(me, grad_out, first, second)
+    go_other = other_core(go_theirs)
     near = jnp.concatenate([keep, lax.ppermute(send, "dp", next_x)], axis=0)
     keep, send = near[:, : RANK // 2], near[:, RANK // 2 :]
     near = jnp.concatenate([keep, lax.ppermute(send, "dp", next_y)], axis=0)
-    go_other = other_core(go_theirs)
-    part, near, go_other = lax.optimization_barrier((part, near, go_other))
+    far = other_core(near)
+    part, near, far, go_mine, go_other = lax.optimization_barrier(
+        (part, near, far, go_mine, go_other)
+    )
     part = part.reshape(planes, tok // planes, RANK)
     mine = jnp.sum(part.astype(f32), axis=0).astype(bf16)
     mine = jnp.broadcast_to(mine[None], part.shape).reshape(tok, RANK)
-    mine, near, me, owners = lax.optimization_barrier((mine, near, me, owners))
-    coeffs = over_planes(mine)
-    far = other_core(near)
-    coeffs, near, far, me, owners = lax.optimization_barrier((coeffs, near, far, me, owners))
+    coeffs, (near, far, go_mine, go_other, me, owners) = over(
+        over_planes, mine, near, far, go_mine, go_other, me, owners
+    )
     coeffs_other = other_core(coeffs)
 
     dims = (chips, pairs, piece, per_block, slots, scale)

time: 114 us -> 114 us (level)
  blocking collectives: 48.2 us -> 68.2 us
  waiting for transfers between devices: 31 us -> 16 us
  starting transfers between devices: 21.1 us -> 18.1 us
  local copies, waits for them, and re-layouts: 1.88 us -> 0.18 us
    all_to_all x1 -> x2, blocking collectives: 12.6 us -> 32.9 us  [over_planes(): return lax.all_to_all(x, 'mp', 0, 0, tiled=True)]
    all_to_all x2 -> x1, waiting for transfers between devices: 25.8 us -> 10.7 us  [over_planes(): return lax.all_to_all(x, 'mp', 0, 0, tiled=True)]
    all_to_all x2 -> x1, starting transfers between devices: 12.5 us -> 7.84 us  [over_planes(): return lax.all_to_all(x, 'mp', 0, 0, tiled=True)]
    pallas_call x1 -> x2, Pallas kernels: 5.18 us -> 4.76 us  [the longest x1 4.61 us: coeffs_call(): pl.pallas_call(coeffs_kernel, in_specs=[pl.BlockSpec(memory_space=pl.ANY)...]
  transfers between devices with their start and end apart: 8 -> 7, of which waited for: 6 -> 4; matrix products, arithmetic and copies ran while one was open for 1% -> 0% of each run, Pallas kernels for 3% -> 3%
where the time goes in v7:
time: 114 us; the launch traced here: 113 us
  blocking collectives  68.2 us (60%)
  starting transfers between devices  18.1 us (16%)
  waiting for transfers between devices  16 us (14%)
  Pallas kernels  9.77 us (9%)
    all_to_all x2, blocking collectives, over_chips(): lax.all_to_all(x, 'dp', 0, 0, axis_index_groups=same_core, tiled=True)  35.4 us
    all_to_all x2, blocking collectives, over_planes(): return lax.all_to_all(x, 'mp', 0, 0, tiled=True)  32.9 us
    all_to_all x1, waiting for transfers between devices, over_planes(): return lax.all_to_all(x, 'mp', 0, 0, tiled=True)  10.7 us
    all_to_all x1, starting transfers between devices, over_planes(): return lax.all_to_all(x, 'mp', 0, 0, tiled=True)  7.84 us
    ppermute x4, starting transfers between devices, other_core(): return lax.ppermute(x, 'dp', swap)  6.78 us
    pallas_call x1, Pallas kernels, coeffs_call(): pl.pallas_call(coeffs_kernel, in_specs=[pl.BlockSpec(memory_space=pl.ANY)...  4.61 us
    ppermute x1, waiting for transfers between devices, body(): near = jnp.concatenate([keep, lax.ppermute(send, 'dp', next_y)], axis=0)  3.51 us
  transfers between devices with their start and end apart: 7, of which 4 were waited for; matrix products, arithmetic and copies ran while one was open for 0% of the time, Pallas kernels for 3%

profile of v7, /device:TPU:1, one launch (start us, length us, event | category | flops | bytes accessed | tf_op | source)
XLA Modules:
  0.0 113.2 jit_solution(625200400071924597)
XLA Ops:
  0.6 0.0 copy-start.1
  0.6 0.0 copy-start.2
  0.7 0.0 copy-start.3
  0.7 4.6 %shard_map.85 = bf16[512,512]{1,0:T(8,128)(2,1)} custom-call(bf16[512,3584]{1,0:T(8,128)(2,1)} %hidden_ref.1, bf16[3584,512]{1,0:T(8,128)(2,1)} %basis_ref.3), custom_call_target="tpu_custom_call" | custom-call | tf_op jit(solution)/shard_map/pallas_call | solution.py:78
  5.3 0.1 shard_map.86
  5.5 2.1 %collective-permute-start = (bf16[128,512]{1,0:T(8,128)(2,1)S(1)}, bf16[128,512]{1,0:T(8,128)(2,1)S(1)}, u32[]{:S(2)}, u32[]{:S(2)}) collective-permute-start(bf16[128,512]{1,0:T(8,128)(2,1)S(1)} %get-tuple-element.59), channel_id=1, source_target_pairs={{0,16},{8,24},{16,0},{24,8},{32,48},{40,56},{48,32},{56,40},{64,80... | collective-permute-start | bytes 393224 | tf_op jit(solution)/shard_map/ppermute | solution.py:317
  7.6 1.3 %collective-permute-start.3 = (bf16[512,512]{1,0:T(8,128)(2,1)S(1)}, bf16[512,512]{1,0:T(8,128)(2,1)S(1)}, u32[]{:S(2)}, u32[]{:S(2)}) collective-permute-start(bf16[512,512]{1,0:T(8,128)(2,1)S(1)} %get-tuple-element.61), channel_id=1, source_target_pairs={{0,8},{8,0},{16,24},{24,16},{32,40},{40,32},{48,56},{56,48},{64,72... | collective-permute-start | bytes 1572872 | tf_op jit(solution)/shard_map/ppermute | solution.py:299
  8.9 7.8 %all-to-all-start = ((bf16[8,64,512]{2,1,0:T(8,128)(2,1)}), bf16[8,64,512]{2,1,0:T(8,128)(2,1)S(1)}, u32[]{:S(2)}, u32[]{:S(2)}) async-start(bf16[8,64,512]{2,1,0:T(8,128)(2,1)} %bitcast.17), calls=%async_computation | async-start | bytes 1048576 | tf_op jit(solution)/shard_map/all_to_all | solution.py:305
  16.8 0.0 copy-start.4
  16.8 0.0 collective-permute-done
  16.8 1.4 %collective-permute-start.1 = (bf16[256,256]{1,0:T(8,128)(2,1)S(1)}, bf16[256,256]{1,0:T(8,128)(2,1)S(1)}, u32[]{:S(2)}, u32[]{:S(2)}) collective-permute-start(bf16[256,256]{1,0:T(8,128)(2,1)S(1)} %get-tuple-element.106), channel_id=1, source_target_pairs={{0,64},{8,72},{16,80},{24,88},{32,96},{40,104},{48,112},{56,120},{... | collective-permute-start | bytes 393224 | tf_op jit(solution)/shard_map/ppermute | solution.py:319
  18.2 3.5 %collective-permute-done.1 = bf16[256,256]{1,0:T(8,128)(2,1)S(1)} collective-permute-done((bf16[256,256]{1,0:T(8,128)(2,1)S(1)}, bf16[256,256]{1,0:T(8,128)(2,1)S(1)}, u32[]{:S(2)}, u32[]{:S(2)}) %collective-permute-start.1) | collective-permute-done | bytes 131104 | tf_op jit(solution)/shard_map/ppermute | solution.py:319
  21.7 1.2 %collective-permute-start.2 = (bf16[512,256]{1,0:T(8,128)(2,1)S(1)}, bf16[512,256]{1,0:T(8,128)(2,1)S(1)}, u32[]{:S(2)}, u32[]{:S(2)}) collective-permute-start(bf16[512,256]{1,0:T(8,128)(2,1)S(1)} %pad_maximum_fusion.1.near_ref), channel_id=1, source_target_pairs={{0,8},{8,0},{16,24},{24,16},{32,40},{40,32},{48,56},{56,48},{64,72... | collective-permute-start | bytes 786440 | tf_op jit(solution)/shard_map/ppermute | solution.py:299
  22.9 1.2 %collective-permute-done.2.far_ref = bf16[512,256]{1,0:T(8,128)(2,1)S(1)} collective-permute-done((bf16[512,256]{1,0:T(8,128)(2,1)S(1)}, bf16[512,256]{1,0:T(8,128)(2,1)S(1)}, u32[]{:S(2)}, u32[]{:S(2)}) %collective-permute-start.2) | collective-permute-done | bytes 262176 | tf_op jit(solution)/shard_map/ppermute | solution.py:299
  24.1 0.0 collective-permute-done.3.other_ref
  24.1 10.7 %all-to-all-done = bf16[8,64,512]{2,1,0:T(8,128)(2,1)S(1)} async-done(((bf16[8,64,512]{2,1,0:T(8,128)(2,1)}), bf16[8,64,512]{2,1,0:T(8,128)(2,1)S(1)}, u32[]{:S(2)}, u32[]{:S(2)}) %all-to-all-start) | async-done | bytes 524320 | tf_op jit(solution)/shard_map/all_to_all | solution.py:305
  34.8 0.1 reduce_sum.12
  34.9 20.3 %all_to_all.39 = bf16[8,64,512]{2,1,0:T(8,128)(2,1)S(1)} all-to-all(bf16[8,64,512]{2,1,0:T(8,128)(2,1)S(1)} %broadcast_in_dim.4), channel_id=1, replica_groups=mesh['dp'=32,'mp'=8] {'mp'}, dimensions={0} | all-to-all | bytes 1048576 | tf_op jit(solution)/shard_map/all_to_all | solution.py:305
  55.2 0.6 collective-permute-start.4
  55.8 0.9 shard_map.87
  56.7 0.6 collective-permute-done.4.co_other_ref
  57.3 0.5 shard_map.88
  57.8 20.1 %all_to_all.40.got_ref = bf16[16,48,512]{2,1,0:T(8,128)(2,1)S(1)} all-to-all(bf16[16,48,512]{2,1,0:T(8,128)(2,1)S(1)} %shard_map.88), channel_id=1, replica_groups={{0,16,32,48,64,80,96,112,128,144,160,176,192,208,224,240},{8,24,40,56,7..., dimensions={0} | all-to-all | bytes 1572864 | tf_op jit(solution)/shard_map/all_to_all | solution.py:302
  77.8 0.2 shard_map.89
  78.0 12.6 %all_to_all.41 = bf16[8,32,512]{2,1,0:T(8,128)(2,1)S(1)} all-to-all(bf16[8,32,512]{2,1,0:T(8,128)(2,1)S(1)} %get-tuple-element.89), channel_id=1, replica_groups=mesh['dp'=32,'mp'=8] {'mp'}, dimensions={0} | all-to-all | bytes 524288 | tf_op jit(solution)/shard_map/all_to_all | solution.py:305
  90.7 0.0 copy-start
  90.7 0.1 pad_maximum_fusion
  90.7 15.3 %all_to_all.42.last_ref = bf16[16,48,512]{2,1,0:T(8,128)(2,1)S(1)} all-to-all(bf16[16,48,512]{2,1,0:T(8,128)(2,1)S(1)} %pad_maximum_fusion), channel_id=1, replica_groups={{0,16,32,48,64,80,96,112,128,144,160,176,192,208,224,240},{8,24,40,56,7..., dimensions={0} | all-to-all | bytes 1572864 | tf_op jit(solution)/shard_map/all_to_all | solution.py:302
  106.1 3.7 %collective-permute-start.5 = (bf16[512,512]{1,0:T(8,128)(2,1)S(1)}, bf16[512,512]{1,0:T(8,128)(2,1)S(1)}, u32[]{:S(2)}, u32[]{:S(2)}) collective-permute-start(bf16[512,512]{1,0:T(8,128)(2,1)S(1)} %bitcast.10), channel_id=1, source_target_pairs={{0,8},{8,0},{16,24},{24,16},{32,40},{40,32},{48,56},{56,48},{64,72... | collective-permute-start | bytes 1572872 | tf_op jit(solution)/shard_map/ppermute | solution.py:299
  109.8 2.0 %shard_map.90 = bf16[3584,256]{1,0:T(8,128)(2,1)} custom-call(bf16[3584,512]{1,0:T(8,128)(2,1)S(1)} %copy-done, bf16[16,48,512]{2,1,0:T(8,128)(2,1)S(1)} %all_to_all.42.last_ref), custom_call_target="tpu_custom_call" | custom-call | tf_op jit(solution)/shard_map/pallas_call | solution.py:234
  111.8 0.0 collective-permute-done.5.sums_other_ref
  111.8 1.4 %shard_map.91 = (f32[128,512]{1,0:T(8,128)}, f32[128,512]{1,0:T(8,128)}) custom-call(s32[1]{0:T(128)} %bitcast.2.me_ref, s32[1,32]{1,0:T(1,128)S(1)} %bitcast.16, f32[128,512]{1,0:T(8,128)S(1)} %copy-done.2, f32[128,512]{1,0:T(8,128)S(1)} %copy-done.3, bf16[512,512]{1,0:T(8,128)(2,1)S(1)} %bitcast.11, bf16[512,512]{1,0:T(8,128)(2,1)S(1)} %collective-permute-done.5.sums_other_ref), custom_call_target="tpu_custom_call" | custom-call | tf_op jit(solution)/shard_map/pallas_call | solution.py:377
  (12 shorter events, 0.2 us)
Async XLA Ops:
  0.6 4.7 %copy-start.1 = (bf16[512,1024]{1,0:T(8,128)(2,1)S(1)}, bf16[512,1024]{1,0:T(8,128)(2,1)}, u32[]{:S(2)}) copy-start(bf16[512,1024]{1,0:T(8,128)(2,1)} %go_ref) | copy-start | bytes 3145732
  0.6 4.7 %copy-start.2 = (f32[128,512]{1,0:T(8,128)S(1)}, f32[128,512]{1,0:T(8,128)}, u32[]{:S(2)}) copy-start(f32[128,512]{1,0:T(8,128)} %first_ref.1) | copy-start | bytes 786436
  0.7 4.7 %copy-start.3 = (f32[128,512]{1,0:T(8,128)S(1)}, f32[128,512]{1,0:T(8,128)}, u32[]{:S(2)}) copy-start(f32[128,512]{1,0:T(8,128)} %second_ref.1) | copy-start | bytes 786436
  5.5 11.3 %collective-permute-start = (bf16[128,512]{1,0:T(8,128)(2,1)S(1)}, bf16[128,512]{1,0:T(8,128)(2,1)S(1)}, u32[]{:S(2)}, u32[]{:S(2)}) collective-permute-start(bf16[128,512]{1,0:T(8,128)(2,1)S(1)} %get-tuple-element.59), channel_id=1, source_target_pairs={{0,16},{8,24},{16,0},{24,8},{32,48},{40,56},{48,32},{56,40},{64,80... | collective-permute-start | bytes 393224 | tf_op jit(solution)/shard_map/ppermute | solution.py:317
  7.6 16.5 %collective-permute-start.3 = (bf16[512,512]{1,0:T(8,128)(2,1)S(1)}, bf16[512,512]{1,0:T(8,128)(2,1)S(1)}, u32[]{:S(2)}, u32[]{:S(2)}) collective-permute-start(bf16[512,512]{1,0:T(8,128)(2,1)S(1)} %get-tuple-element.61), channel_id=1, source_target_pairs={{0,8},{8,0},{16,24},{24,16},{32,40},{40,32},{48,56},{56,48},{64,72... | collective-permute-start | bytes 1572872 | tf_op jit(solution)/shard_map/ppermute | solution.py:299
  8.9 25.9 %all-to-all-start = ((bf16[8,64,512]{2,1,0:T(8,128)(2,1)}), bf16[8,64,512]{2,1,0:T(8,128)(2,1)S(1)}, u32[]{:S(2)}, u32[]{:S(2)}) async-start(bf16[8,64,512]{2,1,0:T(8,128)(2,1)} %bitcast.17), calls=%async_computation | async-start | bytes 1048576 | tf_op jit(solution)/shard_map/all_to_all | solution.py:305
  16.8 39.0 %copy-start.4 = (s32[32,1]{0,1:T(1,128)S(1)}, s32[32,1]{0,1:T(1,128)}, u32[]{:S(2)}) copy-start(s32[32,1]{0,1:T(1,128)} %param.9) | copy-start | bytes 388
  16.8 4.9 %collective-permute-start.1 = (bf16[256,256]{1,0:T(8,128)(2,1)S(1)}, bf16[256,256]{1,0:T(8,128)(2,1)S(1)}, u32[]{:S(2)}, u32[]{:S(2)}) collective-permute-start(bf16[256,256]{1,0:T(8,128)(2,1)S(1)} %get-tuple-element.106), channel_id=1, source_target_pairs={{0,64},{8,72},{16,80},{24,88},{32,96},{40,104},{48,112},{56,120},{... | collective-permute-start | bytes 393224 | tf_op jit(solution)/shard_map/ppermute | solution.py:319
  21.7 2.4 %collective-permute-start.2 = (bf16[512,256]{1,0:T(8,128)(2,1)S(1)}, bf16[512,256]{1,0:T(8,128)(2,1)S(1)}, u32[]{:S(2)}, u32[]{:S(2)}) collective-permute-start(bf16[512,256]{1,0:T(8,128)(2,1)S(1)} %pad_maximum_fusion.1.near_ref), channel_id=1, source_target_pairs={{0,8},{8,0},{16,24},{24,16},{32,40},{40,32},{48,56},{56,48},{64,72... | collective-permute-start | bytes 786440 | tf_op jit(solution)/shard_map/ppermute | solution.py:299
  55.2 2.1 %collective-permute-start.4 = (bf16[512,512]{1,0:T(8,128)(2,1)S(1)}, bf16[512,512]{1,0:T(8,128)(2,1)S(1)}, u32[]{:S(2)}, u32[]{:S(2)}) collective-permute-start(bf16[512,512]{1,0:T(8,128)(2,1)S(1)} %bitcast.12), channel_id=1, source_target_pairs={{0,8},{8,0},{16,24},{24,16},{32,40},{40,32},{48,56},{56,48},{64,72... | collective-permute-start | bytes 1572872 | tf_op jit(solution)/shard_map/ppermute | solution.py:299
  90.7 19.1 %copy-start = (bf16[3584,512]{1,0:T(8,128)(2,1)S(1)}, bf16[3584,512]{1,0:T(8,128)(2,1)}, u32[]{:S(2)}) copy-start(bf16[3584,512]{1,0:T(8,128)(2,1)} %basis_ref.3) | copy-start | bytes 11010052
  106.1 5.7 %collective-permute-start.5 = (bf16[512,512]{1,0:T(8,128)(2,1)S(1)}, bf16[512,512]{1,0:T(8,128)(2,1)S(1)}, u32[]{:S(2)}, u32[]{:S(2)}) collective-permute-start(bf16[512,512]{1,0:T(8,128)(2,1)S(1)} %bitcast.10), channel_id=1, source_target_pairs={{0,8},{8,0},{16,24},{24,16},{32,40},{40,32},{48,56},{56,48},{64,72... | collective-permute-start | bytes 1572872 | tf_op jit(solution)/shard_map/ppermute | solution.py:299

commit v8 on v7

--- a/solution.py
+++ b/solution.py
@@ -308,24 +308,21 @@
     owners = owners.reshape(1, frags)
 
     part = coeffs_call(hidden, basis)
-    part, grad_out, first, second = lax.optimization_barrier(
-        (part, grad_out, first_moment, second_moment)
-    )
-    part = over_planes(part)
+    part, (me, owners, grad_out, first, second) = over(
+        over_planes, part, me, owners, grad_out, first_moment, second_moment
+    )
+    part = part.reshape(planes, tok // planes, RANK)
+    mine = jnp.sum(part.astype(f32), axis=0).astype(bf16)
+    mine = jnp.broadcast_to(mine[None], part.shape).reshape(tok, RANK)
+    coeffs = over_planes(mine)
     go_mine, go_theirs, keep, send = sort_call(me, grad_out, first, second)
-    go_other = other_core(go_theirs)
     near = jnp.concatenate([keep, lax.ppermute(send, "dp", next_x)], axis=0)
     keep, send = near[:, : RANK // 2], near[:, RANK // 2 :]
     near = jnp.concatenate([keep, lax.ppermute(send, "dp", next_y)], axis=0)
     far = other_core(near)
-    part, near, far, go_mine, go_other = lax.optimization_barrier(
-        (part, near, far, go_mine, go_other)
-    )
-    part = part.reshape(planes, tok // planes, RANK)
-    mine = jnp.sum(part.astype(f32), axis=0).astype(bf16)
-    mine = jnp.broadcast_to(mine[None], part.shape).reshape(tok, RANK)
-    coeffs, (near, far, go_mine, go_other, me, owners) = over(
-        over_planes, mine, near, far, go_mine, go_other, me, owners
+    go_other = other_core(go_theirs)
+    coeffs, near, far, go_mine, go_other, me, owners = lax.optimization_barrier(
+        (coeffs, near, far, go_mine, go_other, me, owners)
     )
     coeffs_other = other_core(coeffs)
 

time: 114 us -> 112 us (0.982)
  waiting for transfers between devices: 16 us -> 10 us
  blocking collectives: 68.2 us -> 73 us
    all_to_all x1, waiting for transfers between devices: 10.7 us -> 4.42 us  [over_planes(): return lax.all_to_all(x, 'mp', 0, 0, tiled=True)]
    all_to_all x2, blocking collectives: 32.9 us -> 37.6 us  [over_planes(): return lax.all_to_all(x, 'mp', 0, 0, tiled=True)]
    ppermute x4, starting transfers between devices: 6.78 us -> 11.2 us  [other_core(): return lax.ppermute(x, 'dp', swap)]
    all_to_all x1, starting transfers between devices: 7.84 us -> 3.49 us  [over_planes(): return lax.all_to_all(x, 'mp', 0, 0, tiled=True)]
  transfers between devices with their start and end apart: 7 -> 7, of which waited for: 4 -> 4; matrix products, arithmetic and copies ran while one was open for 0% -> 1% of each run, Pallas kernels for 3% -> 3%
where the time goes in v8:
time: 112 us
  blocking collectives  73 us (65%)
  starting transfers between devices  17.4 us (16%)
  waiting for transfers between devices  10 us (9%)
  Pallas kernels  9.77 us (9%)
    all_to_all x2, blocking collectives, over_planes(): return lax.all_to_all(x, 'mp', 0, 0, tiled=True)  37.6 us
    all_to_all x2, blocking collectives, over_chips(): lax.all_to_all(x, 'dp', 0, 0, axis_index_groups=same_core, tiled=True)  35.4 us
    ppermute x4, starting transfers between devices, other_core(): return lax.ppermute(x, 'dp', swap)  11.2 us
    pallas_call x1, Pallas kernels, coeffs_call(): pl.pallas_call(coeffs_kernel, in_specs=[pl.BlockSpec(memory_space=pl.ANY)...  4.61 us
    all_to_all x1, waiting for transfers between devices, over_planes(): return lax.all_to_all(x, 'mp', 0, 0, tiled=True)  4.42 us
    ppermute x1, waiting for transfers between devices, body(): near = jnp.concatenate([keep, lax.ppermute(send, 'dp', next_y)], axis=0)  3.81 us
    all_to_all x1, starting transfers between devices, over_planes(): return lax.all_to_all(x, 'mp', 0, 0, tiled=True)  3.49 us
  transfers between devices with their start and end apart: 7, of which 4 were waited for; matrix products, arithmetic and copies ran while one was open for 1% of the time, Pallas kernels for 3%

profile of v8, /device:TPU:1, one launch (start us, length us, event | category | flops | bytes accessed | tf_op | source)
XLA Modules:
  0.0 112.0 jit_solution(4477804046203740238)
XLA Ops:
  0.6 0.0 copy-start.1
  0.7 4.6 %shard_map.85 = bf16[512,512]{1,0:T(8,128)(2,1)} custom-call(bf16[512,3584]{1,0:T(8,128)(2,1)} %hidden_ref.1, bf16[3584,512]{1,0:T(8,128)(2,1)} %basis_ref.3), custom_call_target="tpu_custom_call" | custom-call | tf_op jit(solution)/shard_map/pallas_call | solution.py:78
  5.3 25.0 %all_to_all.36 = bf16[8,64,512]{2,1,0:T(8,128)(2,1)S(1)} all-to-all(bf16[8,64,512]{2,1,0:T(8,128)(2,1)} %bitcast.15), channel_id=1, replica_groups=mesh['dp'=32,'mp'=8] {'mp'}, dimensions={0} | all-to-all | bytes 1048576 | tf_op jit(solution)/shard_map/all_to_all | solution.py:305
  30.3 0.0 copy-done.2
  30.3 0.1 shard_map.86
  30.4 1.3 %collective-permute-start = (bf16[128,512]{1,0:T(8,128)(2,1)S(1)}, bf16[128,512]{1,0:T(8,128)(2,1)S(1)}, u32[]{:S(2)}, u32[]{:S(2)}) collective-permute-start(bf16[128,512]{1,0:T(8,128)(2,1)S(1)} %get-tuple-element.62), channel_id=1, source_target_pairs={{0,16},{8,24},{16,0},{24,8},{32,48},{40,56},{48,32},{56,40},{64,80... | collective-permute-start | bytes 393224 | tf_op jit(solution)/shard_map/ppermute | solution.py:319
  31.8 0.1 reduce_sum.12
  31.8 0.8 broadcast_in_dim.4
  32.7 3.5 %all-to-all-start.1 = ((bf16[8,64,512]{2,1,0:T(8,128)(2,1)}), bf16[8,64,512]{2,1,0:T(8,128)(2,1)S(1)}, u32[]{:S(2)}, u32[]{:S(2)}) async-start(bf16[8,64,512]{2,1,0:T(8,128)(2,1)} %broadcast_in_dim.4), calls=%async_computation.1 | async-start | bytes 1048576 | tf_op jit(solution)/shard_map/all_to_all | solution.py:305
  36.2 2.8 %collective-permute-start.3 = (bf16[512,512]{1,0:T(8,128)(2,1)S(1)}, bf16[512,512]{1,0:T(8,128)(2,1)S(1)}, u32[]{:S(2)}, u32[]{:S(2)}) collective-permute-start(bf16[512,512]{1,0:T(8,128)(2,1)S(1)} %get-tuple-element.64), channel_id=1, source_target_pairs={{0,8},{8,0},{16,24},{24,16},{32,40},{40,32},{48,56},{56,48},{64,72... | collective-permute-start | bytes 1572872 | tf_op jit(solution)/shard_map/ppermute | solution.py:299
  39.0 0.0 collective-permute-done
  39.1 1.4 %collective-permute-start.1 = (bf16[256,256]{1,0:T(8,128)(2,1)S(1)}, bf16[256,256]{1,0:T(8,128)(2,1)S(1)}, u32[]{:S(2)}, u32[]{:S(2)}) collective-permute-start(bf16[256,256]{1,0:T(8,128)(2,1)S(1)} %get-tuple-element.98), channel_id=1, source_target_pairs={{0,64},{8,72},{16,80},{24,88},{32,96},{40,104},{48,112},{56,120},{... | collective-permute-start | bytes 393224 | tf_op jit(solution)/shard_map/ppermute | solution.py:321
  40.4 3.8 %collective-permute-done.1 = bf16[256,256]{1,0:T(8,128)(2,1)S(1)} collective-permute-done((bf16[256,256]{1,0:T(8,128)(2,1)S(1)}, bf16[256,256]{1,0:T(8,128)(2,1)S(1)}, u32[]{:S(2)}, u32[]{:S(2)}) %collective-permute-start.1) | collective-permute-done | bytes 131104 | tf_op jit(solution)/shard_map/ppermute | solution.py:321
  44.3 0.9 collective-permute-start.2
  45.2 1.2 %collective-permute-done.2.far_ref = bf16[512,256]{1,0:T(8,128)(2,1)S(1)} collective-permute-done((bf16[512,256]{1,0:T(8,128)(2,1)S(1)}, bf16[512,256]{1,0:T(8,128)(2,1)S(1)}, u32[]{:S(2)}, u32[]{:S(2)}) %collective-permute-start.2) | collective-permute-done | bytes 262176 | tf_op jit(solution)/shard_map/ppermute | solution.py:299
  46.3 0.0 collective-permute-done.3.other_ref
  46.3 4.4 %all-to-all-done.1 = bf16[8,64,512]{2,1,0:T(8,128)(2,1)S(1)} async-done(((bf16[8,64,512]{2,1,0:T(8,128)(2,1)}), bf16[8,64,512]{2,1,0:T(8,128)(2,1)S(1)}, u32[]{:S(2)}, u32[]{:S(2)}) %all-to-all-start.1) | async-done | bytes 524320 | tf_op jit(solution)/shard_map/all_to_all | solution.py:305
  50.8 3.8 %collective-permute-start.4 = (bf16[512,512]{1,0:T(8,128)(2,1)S(1)}, bf16[512,512]{1,0:T(8,128)(2,1)S(1)}, u32[]{:S(2)}, u32[]{:S(2)}) collective-permute-start(bf16[512,512]{1,0:T(8,128)(2,1)S(1)} %bitcast.8), channel_id=1, source_target_pairs={{0,8},{8,0},{16,24},{24,16},{32,40},{40,32},{48,56},{56,48},{64,72... | collective-permute-start | bytes 1572872 | tf_op jit(solution)/shard_map/ppermute | solution.py:299
  54.5 0.9 shard_map.87
  55.5 0.6 collective-permute-done.4.co_other_ref
  56.1 0.5 shard_map.88
  56.5 20.1 %all_to_all.37.got_ref = bf16[16,48,512]{2,1,0:T(8,128)(2,1)S(1)} all-to-all(bf16[16,48,512]{2,1,0:T(8,128)(2,1)S(1)} %shard_map.88), channel_id=1, replica_groups={{0,16,32,48,64,80,96,112,128,144,160,176,192,208,224,240},{8,24,40,56,7..., dimensions={0} | all-to-all | bytes 1572864 | tf_op jit(solution)/shard_map/all_to_all | solution.py:302
  76.6 0.2 shard_map.89
  76.8 12.6 %all_to_all.38 = bf16[8,32,512]{2,1,0:T(8,128)(2,1)S(1)} all-to-all(bf16[8,32,512]{2,1,0:T(8,128)(2,1)S(1)} %get-tuple-element.81), channel_id=1, replica_groups=mesh['dp'=32,'mp'=8] {'mp'}, dimensions={0} | all-to-all | bytes 524288 | tf_op jit(solution)/shard_map/all_to_all | solution.py:305
  89.4 0.0 copy-start
  89.5 0.1 pad_maximum_fusion
  89.5 15.3 %all_to_all.39.last_ref = bf16[16,48,512]{2,1,0:T(8,128)(2,1)S(1)} all-to-all(bf16[16,48,512]{2,1,0:T(8,128)(2,1)S(1)} %pad_maximum_fusion), channel_id=1, replica_groups={{0,16,32,48,64,80,96,112,128,144,160,176,192,208,224,240},{8,24,40,56,7..., dimensions={0} | all-to-all | bytes 1572864 | tf_op jit(solution)/shard_map/all_to_all | solution.py:302
  104.9 3.7 %collective-permute-start.5 = (bf16[512,512]{1,0:T(8,128)(2,1)S(1)}, bf16[512,512]{1,0:T(8,128)(2,1)S(1)}, u32[]{:S(2)}, u32[]{:S(2)}) collective-permute-start(bf16[512,512]{1,0:T(8,128)(2,1)S(1)} %bitcast.10), channel_id=1, source_target_pairs={{0,8},{8,0},{16,24},{24,16},{32,40},{40,32},{48,56},{56,48},{64,72... | collective-permute-start | bytes 1572872 | tf_op jit(solution)/shard_map/ppermute | solution.py:299
  108.6 0.0 copy-done
  108.6 2.0 %shard_map.90 = bf16[3584,256]{1,0:T(8,128)(2,1)} custom-call(bf16[3584,512]{1,0:T(8,128)(2,1)S(1)} %copy-done, bf16[16,48,512]{2,1,0:T(8,128)(2,1)S(1)} %all_to_all.39.last_ref), custom_call_target="tpu_custom_call" | custom-call | tf_op jit(solution)/shard_map/pallas_call | solution.py:234
  110.6 0.0 collective-permute-done.5.sums_other_ref
  110.6 1.4 %shard_map.91 = (f32[128,512]{1,0:T(8,128)}, f32[128,512]{1,0:T(8,128)}) custom-call(s32[1]{0:T(128)} %bitcast.me_ref, s32[1,32]{1,0:T(1,128)S(1)} %bitcast.14, f32[128,512]{1,0:T(8,128)S(1)} %copy-done.2, f32[128,512]{1,0:T(8,128)S(1)} %copy-done.3, bf16[512,512]{1,0:T(8,128)(2,1)S(1)} %bitcast.11, bf16[512,512]{1,0:T(8,128)(2,1)S(1)} %collective-permute-done.5.sums_other_ref), custom_call_target="tpu_custom_call" | custom-call | tf_op jit(solution)/shard_map/pallas_call | solution.py:374
  (12 shorter events, 0.1 us)
Async XLA Ops:
  0.6 29.7 %copy-start.1 = (bf16[512,1024]{1,0:T(8,128)(2,1)S(1)}, bf16[512,1024]{1,0:T(8,128)(2,1)}, u32[]{:S(2)}) copy-start(bf16[512,1024]{1,0:T(8,128)(2,1)} %go_ref) | copy-start | bytes 3145732
  0.6 29.7 %copy-start.2 = (f32[128,512]{1,0:T(8,128)S(1)}, f32[128,512]{1,0:T(8,128)}, u32[]{:S(2)}) copy-start(f32[128,512]{1,0:T(8,128)} %first_ref.1) | copy-start | bytes 786436
  0.7 29.6 %copy-start.3 = (f32[128,512]{1,0:T(8,128)S(1)}, f32[128,512]{1,0:T(8,128)}, u32[]{:S(2)}) copy-start(f32[128,512]{1,0:T(8,128)} %second_ref.1) | copy-start | bytes 786436
  30.4 8.6 %collective-permute-start = (bf16[128,512]{1,0:T(8,128)(2,1)S(1)}, bf16[128,512]{1,0:T(8,128)(2,1)S(1)}, u32[]{:S(2)}, u32[]{:S(2)}) collective-permute-start(bf16[128,512]{1,0:T(8,128)(2,1)S(1)} %get-tuple-element.62), channel_id=1, source_target_pairs={{0,16},{8,24},{16,0},{24,8},{32,48},{40,56},{48,32},{56,40},{64,80... | collective-permute-start | bytes 393224 | tf_op jit(solution)/shard_map/ppermute | solution.py:319
  31.8 22.8 %copy-start.4 = (s32[32,1]{0,1:T(1,128)S(1)}, s32[32,1]{0,1:T(1,128)}, u32[]{:S(2)}) copy-start(s32[32,1]{0,1:T(1,128)} %param.9) | copy-start | bytes 388
  32.7 18.1 %all-to-all-start.1 = ((bf16[8,64,512]{2,1,0:T(8,128)(2,1)}), bf16[8,64,512]{2,1,0:T(8,128)(2,1)S(1)}, u32[]{:S(2)}, u32[]{:S(2)}) async-start(bf16[8,64,512]{2,1,0:T(8,128)(2,1)} %broadcast_in_dim.4), calls=%async_computation.1 | async-start | bytes 1048576 | tf_op jit(solution)/shard_map/all_to_all | solution.py:305
  36.2 10.1 %collective-permute-start.3 = (bf16[512,512]{1,0:T(8,128)(2,1)S(1)}, bf16[512,512]{1,0:T(8,128)(2,1)S(1)}, u32[]{:S(2)}, u32[]{:S(2)}) collective-permute-start(bf16[512,512]{1,0:T(8,128)(2,1)S(1)} %get-tuple-element.64), channel_id=1, source_target_pairs={{0,8},{8,0},{16,24},{24,16},{32,40},{40,32},{48,56},{56,48},{64,72... | collective-permute-start | bytes 1572872 | tf_op jit(solution)/shard_map/ppermute | solution.py:299
  39.1 5.2 %collective-permute-start.1 = (bf16[256,256]{1,0:T(8,128)(2,1)S(1)}, bf16[256,256]{1,0:T(8,128)(2,1)S(1)}, u32[]{:S(2)}, u32[]{:S(2)}) collective-permute-start(bf16[256,256]{1,0:T(8,128)(2,1)S(1)} %get-tuple-element.98), channel_id=1, source_target_pairs={{0,64},{8,72},{16,80},{24,88},{32,96},{40,104},{48,112},{56,120},{... | collective-permute-start | bytes 393224 | tf_op jit(solution)/shard_map/ppermute | solution.py:321
  44.3 2.1 %collective-permute-start.2 = (bf16[512,256]{1,0:T(8,128)(2,1)S(1)}, bf16[512,256]{1,0:T(8,128)(2,1)S(1)}, u32[]{:S(2)}, u32[]{:S(2)}) collective-permute-start(bf16[512,256]{1,0:T(8,128)(2,1)S(1)} %pad_maximum_fusion.1.near_ref), channel_id=1, source_target_pairs={{0,8},{8,0},{16,24},{24,16},{32,40},{40,32},{48,56},{56,48},{64,72... | collective-permute-start | bytes 786440 | tf_op jit(solution)/shard_map/ppermute | solution.py:299
  50.8 5.3 %collective-permute-start.4 = (bf16[512,512]{1,0:T(8,128)(2,1)S(1)}, bf16[512,512]{1,0:T(8,128)(2,1)S(1)}, u32[]{:S(2)}, u32[]{:S(2)}) collective-permute-start(bf16[512,512]{1,0:T(8,128)(2,1)S(1)} %bitcast.8), channel_id=1, source_target_pairs={{0,8},{8,0},{16,24},{24,16},{32,40},{40,32},{48,56},{56,48},{64,72... | collective-permute-start | bytes 1572872 | tf_op jit(solution)/shard_map/ppermute | solution.py:299
  89.4 19.1 %copy-start = (bf16[3584,512]{1,0:T(8,128)(2,1)S(1)}, bf16[3584,512]{1,0:T(8,128)(2,1)}, u32[]{:S(2)}) copy-start(bf16[3584,512]{1,0:T(8,128)(2,1)} %basis_ref.3) | copy-start | bytes 11010052
  104.9 5.7 %collective-permute-start.5 = (bf16[512,512]{1,0:T(8,128)(2,1)S(1)}, bf16[512,512]{1,0:T(8,128)(2,1)S(1)}, u32[]{:S(2)}, u32[]{:S(2)}) collective-permute-start(bf16[512,512]{1,0:T(8,128)(2,1)S(1)} %bitcast.10), channel_id=1, source_target_pairs={{0,8},{8,0},{16,24},{24,16},{32,40},{40,32},{48,56},{56,48},{64,72... | collective-permute-start | bytes 1572872 | tf_op jit(solution)/shard_map/ppermute | solution.py:299

commit v9 on v8

--- a/solution.py
+++ b/solution.py
@@ -308,15 +308,20 @@
     owners = owners.reshape(1, frags)
 
     part = coeffs_call(hidden, basis)
-    part, (me, owners, grad_out, first, second) = over(
-        over_planes, part, me, owners, grad_out, first_moment, second_moment
+    part, me, grad_out, first, second = lax.optimization_barrier(
+        (part, me, grad_out, first_moment, second_moment)
+    )
+    go_mine, go_theirs, keep, send = sort_call(me, grad_out, first, second)
+    got_x = lax.ppermute(send, "dp", next_x[0::2])
+    part, (me, owners, go_mine, go_theirs, keep, send, got_x) = over(
+        over_planes, part, me, owners, go_mine, go_theirs, keep, send, got_x
     )
     part = part.reshape(planes, tok // planes, RANK)
     mine = jnp.sum(part.astype(f32), axis=0).astype(bf16)
     mine = jnp.broadcast_to(mine[None], part.shape).reshape(tok, RANK)
     coeffs = over_planes(mine)
-    go_mine, go_theirs, keep, send = sort_call(me, grad_out, first, second)
-    near = jnp.concatenate([keep, lax.ppermute(send, "dp", next_x)], axis=0)
+    got_x = got_x + lax.ppermute(send, "dp", next_x[1::2])
+    near = jnp.concatenate([keep, got_x], axis=0)
     keep, send = near[:, : RANK // 2], near[:, RANK // 2 :]
     near = jnp.concatenate([keep, lax.ppermute(send, "dp", next_y)], axis=0)
     far = other_core(near)

time: 112 us -> 111 us (level)
  starting transfers between devices: 17.4 us -> 24.1 us
  waiting for transfers between devices: 10 us -> 5.58 us
  blocking collectives: 73 us -> 69.2 us
    all_to_all x1, waiting for transfers between devices: 4.42 us -> 0.01 us  [over_planes(): return lax.all_to_all(x, 'mp', 0, 0, tiled=True)]
    ppermute x4, starting transfers between devices: 11.2 us -> 15.4 us  [other_core(): return lax.ppermute(x, 'dp', swap)]
    all_to_all x2, blocking collectives: 37.6 us -> 33.5 us  [over_planes(): return lax.all_to_all(x, 'mp', 0, 0, tiled=True)]
    ppermute x1 -> x2, starting transfers between devices: 1.31 us -> 3.79 us  [the longest x1 3.12 us: body(): got_x = got_x + lax.ppermute(send, 'dp', next_x[1::2])]
  transfers between devices with their start and end apart: 7 -> 8, of which waited for: 4 -> 3; matrix products, arithmetic and copies ran while one was open for 1% -> 0% of each run, Pallas kernels for 3% -> 3%
where the time goes in v9:
time: 111 us
  blocking collectives  69.2 us (62%)
  starting transfers between devices  24.1 us (22%)
  Pallas kernels  9.75 us (9%)
  waiting for transfers between devices  5.58 us (5%)
  local copies, waits for them, and re-layouts  1.11 us (1%)
    all_to_all x2, blocking collectives, over_chips(): lax.all_to_all(x, 'dp', 0, 0, axis_index_groups=same_core, tiled=True)  35.6 us
    all_to_all x2, blocking collectives, over_planes(): return lax.all_to_all(x, 'mp', 0, 0, tiled=True)  33.5 us
    ppermute x4, starting transfers between devices, other_core(): return lax.ppermute(x, 'dp', swap)  15.4 us
    pallas_call x1, Pallas kernels, coeffs_call(): pl.pallas_call(coeffs_kernel, in_specs=[pl.BlockSpec(memory_space=pl.ANY)...  4.61 us
    ppermute x1, waiting for transfers between devices, body(): near = jnp.concatenate([keep, lax.ppermute(send, 'dp', next_y)], axis=0)  3.81 us
    all_to_all x1, starting transfers between devices, over_planes(): return lax.all_to_all(x, 'mp', 0, 0, tiled=True)  3.49 us
    ppermute x1, starting transfers between devices, body(): got_x = got_x + lax.ppermute(send, 'dp', next_x[1::2])  3.12 us
  transfers between devices with their start and end apart: 8, of which 3 were waited for; matrix products, arithmetic and copies ran while one was open for 0% of the time, Pallas kernels for 3%

profile of v9, /device:TPU:1, one launch (start us, length us, event | category | flops | bytes accessed | tf_op | source)
XLA Modules:
  0.0 110.8 jit_solution(12835170485302975294)
XLA Ops:
  0.7 4.6 %shard_map.85 = bf16[512,512]{1,0:T(8,128)(2,1)} custom-call(bf16[512,3584]{1,0:T(8,128)(2,1)} %hidden_ref.1, bf16[3584,512]{1,0:T(8,128)(2,1)} %basis_ref.3), custom_call_target="tpu_custom_call" | custom-call | tf_op jit(solution)/shard_map/pallas_call | solution.py:78
  5.3 0.0 copy-start.5
  5.3 0.1 shard_map.86
  5.5 0.7 collective-permute-start
  6.2 0.0 collective-permute-done
  6.2 0.2 copy-done.5
  6.3 20.9 %all_to_all.36 = bf16[8,64,512]{2,1,0:T(8,128)(2,1)S(1)} all-to-all(bf16[8,64,512]{2,1,0:T(8,128)(2,1)S(1)} %bitcast.15), channel_id=1, replica_groups=mesh['dp'=32,'mp'=8] {'mp'}, dimensions={0} | all-to-all | bytes 1048576 | tf_op jit(solution)/shard_map/all_to_all | solution.py:305
  27.3 0.1 reduce_sum.12
  27.4 0.8 broadcast_in_dim.4
  28.2 3.5 %all-to-all-start.1 = ((bf16[8,64,512]{2,1,0:T(8,128)(2,1)}), bf16[8,64,512]{2,1,0:T(8,128)(2,1)S(1)}, u32[]{:S(2)}, u32[]{:S(2)}) async-start(bf16[8,64,512]{2,1,0:T(8,128)(2,1)} %broadcast_in_dim.4), calls=%async_computation.1 | async-start | bytes 1048576 | tf_op jit(solution)/shard_map/all_to_all | solution.py:305
  31.7 3.1 %collective-permute-start.1 = (bf16[128,512]{1,0:T(8,128)(2,1)S(1)}, bf16[128,512]{1,0:T(8,128)(2,1)S(1)}, u32[]{:S(2)}, u32[]{:S(2)}) collective-permute-start(bf16[128,512]{1,0:T(8,128)(2,1)S(1)} %get-tuple-element.79), channel_id=1, source_target_pairs={{8,24},{24,8},{40,56},{56,40},{72,88},{88,72},{104,120},{120,104},... | collective-permute-start | bytes 393224 | tf_op jit(solution)/shard_map/ppermute | solution.py:323
  34.8 5.7 %collective-permute-start.4 = (bf16[512,512]{1,0:T(8,128)(2,1)S(1)}, bf16[512,512]{1,0:T(8,128)(2,1)S(1)}, u32[]{:S(2)}, u32[]{:S(2)}) collective-permute-start(bf16[512,512]{1,0:T(8,128)(2,1)S(1)} %get-tuple-element.81), channel_id=1, source_target_pairs={{0,8},{8,0},{16,24},{24,16},{32,40},{40,32},{48,56},{56,48},{64,72... | collective-permute-start | bytes 1572872 | tf_op jit(solution)/shard_map/ppermute | solution.py:299
  40.6 1.4 %collective-permute-start.2 = (bf16[256,256]{1,0:T(8,128)(2,1)S(1)}, bf16[256,256]{1,0:T(8,128)(2,1)S(1)}, u32[]{:S(2)}, u32[]{:S(2)}) collective-permute-start(bf16[256,256]{1,0:T(8,128)(2,1)S(1)} %get-tuple-element.116), channel_id=1, source_target_pairs={{0,64},{8,72},{16,80},{24,88},{32,96},{40,104},{48,112},{56,120},{... | collective-permute-start | bytes 393224 | tf_op jit(solution)/shard_map/ppermute | solution.py:326
  42.0 3.8 %collective-permute-done.2 = bf16[256,256]{1,0:T(8,128)(2,1)S(1)} collective-permute-done((bf16[256,256]{1,0:T(8,128)(2,1)S(1)}, bf16[256,256]{1,0:T(8,128)(2,1)S(1)}, u32[]{:S(2)}, u32[]{:S(2)}) %collective-permute-start.2) | collective-permute-done | bytes 131104 | tf_op jit(solution)/shard_map/ppermute | solution.py:326
  45.9 0.9 collective-permute-start.3
  46.7 1.2 %collective-permute-done.3.far_ref = bf16[512,256]{1,0:T(8,128)(2,1)S(1)} collective-permute-done((bf16[512,256]{1,0:T(8,128)(2,1)S(1)}, bf16[512,256]{1,0:T(8,128)(2,1)S(1)}, u32[]{:S(2)}, u32[]{:S(2)}) %collective-permute-start.3) | collective-permute-done | bytes 262176 | tf_op jit(solution)/shard_map/ppermute | solution.py:299
  47.9 0.0 collective-permute-done.4.other_ref
  47.9 0.0 all-to-all-done.1
  47.9 5.1 %collective-permute-start.5 = (bf16[512,512]{1,0:T(8,128)(2,1)S(1)}, bf16[512,512]{1,0:T(8,128)(2,1)S(1)}, u32[]{:S(2)}, u32[]{:S(2)}) collective-permute-start(bf16[512,512]{1,0:T(8,128)(2,1)S(1)} %bitcast.8), channel_id=1, source_target_pairs={{0,8},{8,0},{16,24},{24,16},{32,40},{40,32},{48,56},{56,48},{64,72... | collective-permute-start | bytes 1572872 | tf_op jit(solution)/shard_map/ppermute | solution.py:299
  53.0 0.9 shard_map.87
  53.9 0.6 collective-permute-done.5.co_other_ref
  54.5 0.5 shard_map.88
  55.0 20.4 %all_to_all.37.got_ref = bf16[16,48,512]{2,1,0:T(8,128)(2,1)S(1)} all-to-all(bf16[16,48,512]{2,1,0:T(8,128)(2,1)S(1)} %shard_map.88), channel_id=1, replica_groups={{0,16,32,48,64,80,96,112,128,144,160,176,192,208,224,240},{8,24,40,56,7..., dimensions={0} | all-to-all | bytes 1572864 | tf_op jit(solution)/shard_map/all_to_all | solution.py:302
  75.4 0.2 shard_map.89
  75.6 12.6 %all_to_all.38 = bf16[8,32,512]{2,1,0:T(8,128)(2,1)S(1)} all-to-all(bf16[8,32,512]{2,1,0:T(8,128)(2,1)S(1)} %get-tuple-element.99), channel_id=1, replica_groups=mesh['dp'=32,'mp'=8] {'mp'}, dimensions={0} | all-to-all | bytes 524288 | tf_op jit(solution)/shard_map/all_to_all | solution.py:305
  88.2 0.0 copy-start
  88.2 0.1 pad_maximum_fusion
  88.3 15.3 %all_to_all.39.last_ref = bf16[16,48,512]{2,1,0:T(8,128)(2,1)S(1)} all-to-all(bf16[16,48,512]{2,1,0:T(8,128)(2,1)S(1)} %pad_maximum_fusion), channel_id=1, replica_groups={{0,16,32,48,64,80,96,112,128,144,160,176,192,208,224,240},{8,24,40,56,7..., dimensions={0} | all-to-all | bytes 1572864 | tf_op jit(solution)/shard_map/all_to_all | solution.py:302
  103.6 3.7 %collective-permute-start.6 = (bf16[512,512]{1,0:T(8,128)(2,1)S(1)}, bf16[512,512]{1,0:T(8,128)(2,1)S(1)}, u32[]{:S(2)}, u32[]{:S(2)}) collective-permute-start(bf16[512,512]{1,0:T(8,128)(2,1)S(1)} %bitcast.10), channel_id=1, source_target_pairs={{0,8},{8,0},{16,24},{24,16},{32,40},{40,32},{48,56},{56,48},{64,72... | collective-permute-start | bytes 1572872 | tf_op jit(solution)/shard_map/ppermute | solution.py:299
  107.3 2.0 %shard_map.90 = bf16[3584,256]{1,0:T(8,128)(2,1)} custom-call(bf16[3584,512]{1,0:T(8,128)(2,1)S(1)} %copy-done, bf16[16,48,512]{2,1,0:T(8,128)(2,1)S(1)} %all_to_all.39.last_ref), custom_call_target="tpu_custom_call" | custom-call | tf_op jit(solution)/shard_map/pallas_call | solution.py:234
  109.3 0.0 collective-permute-done.6.sums_other_ref
  109.4 1.4 %shard_map.91 = (f32[128,512]{1,0:T(8,128)}, f32[128,512]{1,0:T(8,128)}) custom-call(s32[1]{0:T(128)} %bitcast.me_ref, s32[1,32]{1,0:T(1,128)S(1)} %bitcast.14, f32[128,512]{1,0:T(8,128)S(1)} %copy-done.2, f32[128,512]{1,0:T(8,128)S(1)} %copy-done.3, bf16[512,512]{1,0:T(8,128)(2,1)S(1)} %bitcast.11, bf16[512,512]{1,0:T(8,128)(2,1)S(1)} %collective-permute-done.6.sums_other_ref), custom_call_target="tpu_custom_call" | custom-call | tf_op jit(solution)/shard_map/pallas_call | solution.py:379
  (15 shorter events, 0.2 us)
Async XLA Ops:
  0.6 4.7 %copy-start.1 = (bf16[512,1024]{1,0:T(8,128)(2,1)S(1)}, bf16[512,1024]{1,0:T(8,128)(2,1)}, u32[]{:S(2)}) copy-start(bf16[512,1024]{1,0:T(8,128)(2,1)} %go_ref) | copy-start | bytes 3145732
  0.6 4.7 %copy-start.2 = (f32[128,512]{1,0:T(8,128)S(1)}, f32[128,512]{1,0:T(8,128)}, u32[]{:S(2)}) copy-start(f32[128,512]{1,0:T(8,128)} %first_ref.1) | copy-start | bytes 786436
  0.7 4.7 %copy-start.3 = (f32[128,512]{1,0:T(8,128)S(1)}, f32[128,512]{1,0:T(8,128)}, u32[]{:S(2)}) copy-start(f32[128,512]{1,0:T(8,128)} %second_ref.1) | copy-start | bytes 786436
  5.3 1.0 copy-start.5
  5.5 0.7 collective-permute-start
  27.3 25.7 %copy-start.4 = (s32[32,1]{0,1:T(1,128)S(1)}, s32[32,1]{0,1:T(1,128)}, u32[]{:S(2)}) copy-start(s32[32,1]{0,1:T(1,128)} %param.9) | copy-start | bytes 388
  28.2 19.7 %all-to-all-start.1 = ((bf16[8,64,512]{2,1,0:T(8,128)(2,1)}), bf16[8,64,512]{2,1,0:T(8,128)(2,1)S(1)}, u32[]{:S(2)}, u32[]{:S(2)}) async-start(bf16[8,64,512]{2,1,0:T(8,128)(2,1)} %broadcast_in_dim.4), calls=%async_computation.1 | async-start | bytes 1048576 | tf_op jit(solution)/shard_map/all_to_all | solution.py:305
  31.7 8.9 %collective-permute-start.1 = (bf16[128,512]{1,0:T(8,128)(2,1)S(1)}, bf16[128,512]{1,0:T(8,128)(2,1)S(1)}, u32[]{:S(2)}, u32[]{:S(2)}) collective-permute-start(bf16[128,512]{1,0:T(8,128)(2,1)S(1)} %get-tuple-element.79), channel_id=1, source_target_pairs={{8,24},{24,8},{40,56},{56,40},{72,88},{88,72},{104,120},{120,104},... | collective-permute-start | bytes 393224 | tf_op jit(solution)/shard_map/ppermute | solution.py:323
  34.8 13.1 %collective-permute-start.4 = (bf16[512,512]{1,0:T(8,128)(2,1)S(1)}, bf16[512,512]{1,0:T(8,128)(2,1)S(1)}, u32[]{:S(2)}, u32[]{:S(2)}) collective-permute-start(bf16[512,512]{1,0:T(8,128)(2,1)S(1)} %get-tuple-element.81), channel_id=1, source_target_pairs={{0,8},{8,0},{16,24},{24,16},{32,40},{40,32},{48,56},{56,48},{64,72... | collective-permute-start | bytes 1572872 | tf_op jit(solution)/shard_map/ppermute | solution.py:299
  40.6 5.2 %collective-permute-start.2 = (bf16[256,256]{1,0:T(8,128)(2,1)S(1)}, bf16[256,256]{1,0:T(8,128)(2,1)S(1)}, u32[]{:S(2)}, u32[]{:S(2)}) collective-permute-start(bf16[256,256]{1,0:T(8,128)(2,1)S(1)} %get-tuple-element.116), channel_id=1, source_target_pairs={{0,64},{8,72},{16,80},{24,88},{32,96},{40,104},{48,112},{56,120},{... | collective-permute-start | bytes 393224 | tf_op jit(solution)/shard_map/ppermute | solution.py:326
  45.9 2.1 %collective-permute-start.3 = (bf16[512,256]{1,0:T(8,128)(2,1)S(1)}, bf16[512,256]{1,0:T(8,128)(2,1)S(1)}, u32[]{:S(2)}, u32[]{:S(2)}) collective-permute-start(bf16[512,256]{1,0:T(8,128)(2,1)S(1)} %pad_maximum_fusion.1.near_ref), channel_id=1, source_target_pairs={{0,8},{8,0},{16,24},{24,16},{32,40},{40,32},{48,56},{56,48},{64,72... | collective-permute-start | bytes 786440 | tf_op jit(solution)/shard_map/ppermute | solution.py:299
  47.9 6.6 %collective-permute-start.5 = (bf16[512,512]{1,0:T(8,128)(2,1)S(1)}, bf16[512,512]{1,0:T(8,128)(2,1)S(1)}, u32[]{:S(2)}, u32[]{:S(2)}) collective-permute-start(bf16[512,512]{1,0:T(8,128)(2,1)S(1)} %bitcast.8), channel_id=1, source_target_pairs={{0,8},{8,0},{16,24},{24,16},{32,40},{40,32},{48,56},{56,48},{64,72... | collective-permute-start | bytes 1572872 | tf_op jit(solution)/shard_map/ppermute | solution.py:299
  88.2 19.1 %copy-start = (bf16[3584,512]{1,0:T(8,128)(2,1)S(1)}, bf16[3584,512]{1,0:T(8,128)(2,1)}, u32[]{:S(2)}) copy-start(bf16[3584,512]{1,0:T(8,128)(2,1)} %basis_ref.3) | copy-start | bytes 11010052
  103.6 5.7 %collective-permute-start.6 = (bf16[512,512]{1,0:T(8,128)(2,1)S(1)}, bf16[512,512]{1,0:T(8,128)(2,1)S(1)}, u32[]{:S(2)}, u32[]{:S(2)}) collective-permute-start(bf16[512,512]{1,0:T(8,128)(2,1)S(1)} %bitcast.10), channel_id=1, source_target_pairs={{0,8},{8,0},{16,24},{24,16},{32,40},{40,32},{48,56},{56,48},{64,72... | collective-permute-start | bytes 1572872 | tf_op jit(solution)/shard_map/ppermute | solution.py:299

commit v10 on v9

--- a/solution.py
+++ b/solution.py
@@ -312,7 +312,8 @@
         (part, me, grad_out, first_moment, second_moment)
     )
     go_mine, go_theirs, keep, send = sort_call(me, grad_out, first, second)
-    got_x = lax.ppermute(send, "dp", next_x[0::2])
+    early = RANK // SQUARE
+    got_x = lax.ppermute(send[:, :early], "dp", next_x[0::2])
     part, (me, owners, go_mine, go_theirs, keep, send, got_x) = over(
         over_planes, part, me, owners, go_mine, go_theirs, keep, send, got_x
     )
@@ -320,7 +321,8 @@
     mine = jnp.sum(part.astype(f32), axis=0).astype(bf16)
     mine = jnp.broadcast_to(mine[None], part.shape).reshape(tok, RANK)
     coeffs = over_planes(mine)
-    got_x = got_x + lax.ppermute(send, "dp", next_x[1::2])
+    got_x = got_x + lax.ppermute(send[:, :early], "dp", next_x[1::2])
+    got_x = jnp.concatenate([got_x, lax.ppermute(send[:, early:], "dp", next_x)], axis=1)
     near = jnp.concatenate([keep, got_x], axis=0)
     keep, send = near[:, : RANK // 2], near[:, RANK // 2 :]
     near = jnp.concatenate([keep, lax.ppermute(send, "dp", next_y)], axis=0)

time: 111 us -> 111 us (level)
    ppermute x2 -> x3, starting transfers between devices: 3.79 us -> 4.12 us  [the longest x1 2.16 us: body(): got_x = got_x + lax.ppermute(send[:, :early], 'dp', next_x[1::2])]
  transfers between devices with their start and end apart: 8 -> 9, of which waited for: 3 -> 3; matrix products, arithmetic and copies ran while one was open for 0% -> 1% of each run, Pallas kernels for 3% -> 3%
where the time goes in v10:
time: 111 us
  blocking collectives  69 us (62%)
  starting transfers between devices  24.5 us (22%)
  Pallas kernels  9.76 us (9%)
  waiting for transfers between devices  5.58 us (5%)
  local copies, waits for them, and re-layouts  1.15 us (1%)
    all_to_all x2, blocking collectives, over_chips(): lax.all_to_all(x, 'dp', 0, 0, axis_index_groups=same_core, tiled=True)  35.4 us
    all_to_all x2, blocking collectives, over_planes(): return lax.all_to_all(x, 'mp', 0, 0, tiled=True)  33.6 us
    ppermute x4, starting transfers between devices, other_core(): return lax.ppermute(x, 'dp', swap)  15.5 us
    pallas_call x1, Pallas kernels, coeffs_call(): pl.pallas_call(coeffs_kernel, in_specs=[pl.BlockSpec(memory_space=pl.ANY)...  4.61 us
    ppermute x1, waiting for transfers between devices, body(): near = jnp.concatenate([keep, lax.ppermute(send, 'dp', next_y)], axis=0)  3.81 us
    all_to_all x1, starting transfers between devices, over_planes(): return lax.all_to_all(x, 'mp', 0, 0, tiled=True)  3.49 us
  transfers between devices with their start and end apart: 9, of which 3 were waited for; matrix products, arithmetic and copies ran while one was open for 1% of the time, Pallas kernels for 3%

profile of v10, /device:TPU:1, one launch (start us, length us, event | category | flops | bytes accessed | tf_op | source)
XLA Modules:
  0.0 111.1 jit_solution(16205602119564012511)
XLA Ops:
  0.7 4.6 %shard_map.85 = bf16[512,512]{1,0:T(8,128)(2,1)} custom-call(bf16[512,3584]{1,0:T(8,128)(2,1)} %hidden_ref.1, bf16[3584,512]{1,0:T(8,128)(2,1)} %basis_ref.3), custom_call_target="tpu_custom_call" | custom-call | tf_op jit(solution)/shard_map/pallas_call | solution.py:78
  5.3 0.0 copy-start.5
  5.3 0.1 shard_map.86
  5.5 0.7 collective-permute-start
  6.2 0.2 copy-done.5
  6.3 21.1 %all_to_all.36 = bf16[8,64,512]{2,1,0:T(8,128)(2,1)S(1)} all-to-all(bf16[8,64,512]{2,1,0:T(8,128)(2,1)S(1)} %bitcast.15), channel_id=1, replica_groups=mesh['dp'=32,'mp'=8] {'mp'}, dimensions={0} | all-to-all | bytes 1048576 | tf_op jit(solution)/shard_map/all_to_all | solution.py:305
  27.4 1.3 %collective-permute-start.2 = (bf16[128,384]{1,0:T(8,128)(2,1)S(1)}, bf16[128,384]{1,0:T(8,128)(2,1)S(1)}, u32[]{:S(2)}, u32[]{:S(2)}) collective-permute-start(bf16[128,384]{1,0:T(8,128)(2,1)S(1)} %slice.20), channel_id=1, source_target_pairs={{0,16},{8,24},{16,0},{24,8},{32,48},{40,56},{48,32},{56,40},{64,80... | collective-permute-start | bytes 294920 | tf_op jit(solution)/shard_map/ppermute | solution.py:325
  28.7 0.1 reduce_sum.12
  28.8 0.0 copy-start.4
  28.8 0.8 broadcast_in_dim.4
  29.6 3.5 %all-to-all-start.1 = ((bf16[8,64,512]{2,1,0:T(8,128)(2,1)}), bf16[8,64,512]{2,1,0:T(8,128)(2,1)S(1)}, u32[]{:S(2)}, u32[]{:S(2)}) async-start(bf16[8,64,512]{2,1,0:T(8,128)(2,1)} %broadcast_in_dim.4), calls=%async_computation.1 | async-start | bytes 1048576 | tf_op jit(solution)/shard_map/all_to_all | solution.py:305
  33.1 2.2 %collective-permute-start.1 = (bf16[128,128]{1,0:T(8,128)(2,1)S(1)}, bf16[128,128]{1,0:T(8,128)(2,1)S(1)}, u32[]{:S(2)}, u32[]{:S(2)}) collective-permute-start(bf16[128,128]{1,0:T(8,128)(2,1)S(1)} %slice.19), channel_id=1, source_target_pairs={{8,24},{24,8},{40,56},{56,40},{72,88},{88,72},{104,120},{120,104},... | collective-permute-start | bytes 98312 | tf_op jit(solution)/shard_map/ppermute | solution.py:324
  35.3 5.8 %collective-permute-start.5 = (bf16[512,512]{1,0:T(8,128)(2,1)S(1)}, bf16[512,512]{1,0:T(8,128)(2,1)S(1)}, u32[]{:S(2)}, u32[]{:S(2)}) collective-permute-start(bf16[512,512]{1,0:T(8,128)(2,1)S(1)} %get-tuple-element.81), channel_id=1, source_target_pairs={{0,8},{8,0},{16,24},{24,16},{32,40},{40,32},{48,56},{56,48},{64,72... | collective-permute-start | bytes 1572872 | tf_op jit(solution)/shard_map/ppermute | solution.py:299
  41.1 0.0 collective-permute-done.1
  41.2 0.0 collective-permute-done.2
  41.2 1.4 %collective-permute-start.3 = (bf16[256,256]{1,0:T(8,128)(2,1)S(1)}, bf16[256,256]{1,0:T(8,128)(2,1)S(1)}, u32[]{:S(2)}, u32[]{:S(2)}) collective-permute-start(bf16[256,256]{1,0:T(8,128)(2,1)S(1)} %get-tuple-element.116), channel_id=1, source_target_pairs={{0,64},{8,72},{16,80},{24,88},{32,96},{40,104},{48,112},{56,120},{... | collective-permute-start | bytes 393224 | tf_op jit(solution)/shard_map/ppermute | solution.py:328
  42.6 3.8 %collective-permute-done.3 = bf16[256,256]{1,0:T(8,128)(2,1)S(1)} collective-permute-done((bf16[256,256]{1,0:T(8,128)(2,1)S(1)}, bf16[256,256]{1,0:T(8,128)(2,1)S(1)}, u32[]{:S(2)}, u32[]{:S(2)}) %collective-permute-start.3) | collective-permute-done | bytes 131104 | tf_op jit(solution)/shard_map/ppermute | solution.py:328
  46.4 0.9 collective-permute-start.4
  47.3 1.2 %collective-permute-done.4.far_ref = bf16[512,256]{1,0:T(8,128)(2,1)S(1)} collective-permute-done((bf16[512,256]{1,0:T(8,128)(2,1)S(1)}, bf16[512,256]{1,0:T(8,128)(2,1)S(1)}, u32[]{:S(2)}, u32[]{:S(2)}) %collective-permute-start.4) | collective-permute-done | bytes 262176 | tf_op jit(solution)/shard_map/ppermute | solution.py:299
  48.5 5.1 %collective-permute-start.6 = (bf16[512,512]{1,0:T(8,128)(2,1)S(1)}, bf16[512,512]{1,0:T(8,128)(2,1)S(1)}, u32[]{:S(2)}, u32[]{:S(2)}) collective-permute-start(bf16[512,512]{1,0:T(8,128)(2,1)S(1)} %bitcast.8), channel_id=1, source_target_pairs={{0,8},{8,0},{16,24},{24,16},{32,40},{40,32},{48,56},{56,48},{64,72... | collective-permute-start | bytes 1572872 | tf_op jit(solution)/shard_map/ppermute | solution.py:299
  53.6 0.9 shard_map.87
  54.5 0.6 collective-permute-done.6.co_other_ref
  55.1 0.5 shard_map.88
  55.6 20.1 %all_to_all.37.got_ref = bf16[16,48,512]{2,1,0:T(8,128)(2,1)S(1)} all-to-all(bf16[16,48,512]{2,1,0:T(8,128)(2,1)S(1)} %shard_map.88), channel_id=1, replica_groups={{0,16,32,48,64,80,96,112,128,144,160,176,192,208,224,240},{8,24,40,56,7..., dimensions={0} | all-to-all | bytes 1572864 | tf_op jit(solution)/shard_map/all_to_all | solution.py:302
  75.7 0.2 shard_map.89
  75.8 12.6 %all_to_all.38 = bf16[8,32,512]{2,1,0:T(8,128)(2,1)S(1)} all-to-all(bf16[8,32,512]{2,1,0:T(8,128)(2,1)S(1)} %get-tuple-element.99), channel_id=1, replica_groups=mesh['dp'=32,'mp'=8] {'mp'}, dimensions={0} | all-to-all | bytes 524288 | tf_op jit(solution)/shard_map/all_to_all | solution.py:305
  88.5 0.0 copy-start
  88.5 0.1 pad_maximum_fusion
  88.6 15.3 %all_to_all.39.last_ref = bf16[16,48,512]{2,1,0:T(8,128)(2,1)S(1)} all-to-all(bf16[16,48,512]{2,1,0:T(8,128)(2,1)S(1)} %pad_maximum_fusion), channel_id=1, replica_groups={{0,16,32,48,64,80,96,112,128,144,160,176,192,208,224,240},{8,24,40,56,7..., dimensions={0} | all-to-all | bytes 1572864 | tf_op jit(solution)/shard_map/all_to_all | solution.py:302
  103.9 3.7 %collective-permute-start.7 = (bf16[512,512]{1,0:T(8,128)(2,1)S(1)}, bf16[512,512]{1,0:T(8,128)(2,1)S(1)}, u32[]{:S(2)}, u32[]{:S(2)}) collective-permute-start(bf16[512,512]{1,0:T(8,128)(2,1)S(1)} %bitcast.10), channel_id=1, source_target_pairs={{0,8},{8,0},{16,24},{24,16},{32,40},{40,32},{48,56},{56,48},{64,72... | collective-permute-start | bytes 1572872 | tf_op jit(solution)/shard_map/ppermute | solution.py:299
  107.6 2.0 %shard_map.90 = bf16[3584,256]{1,0:T(8,128)(2,1)} custom-call(bf16[3584,512]{1,0:T(8,128)(2,1)S(1)} %copy-done, bf16[16,48,512]{2,1,0:T(8,128)(2,1)S(1)} %all_to_all.39.last_ref), custom_call_target="tpu_custom_call" | custom-call | tf_op jit(solution)/shard_map/pallas_call | solution.py:234
  109.6 1.4 %shard_map.91 = (f32[128,512]{1,0:T(8,128)}, f32[128,512]{1,0:T(8,128)}) custom-call(s32[1]{0:T(128)} %bitcast.me_ref, s32[1,32]{1,0:T(1,128)S(1)} %bitcast.14, f32[128,512]{1,0:T(8,128)S(1)} %copy-done.2, f32[128,512]{1,0:T(8,128)S(1)} %copy-done.3, bf16[512,512]{1,0:T(8,128)(2,1)S(1)} %bitcast.11, bf16[512,512]{1,0:T(8,128)(2,1)S(1)} %collective-permute-done.7.sums_other_ref), custom_call_target="tpu_custom_call" | custom-call | tf_op jit(solution)/shard_map/pallas_call | solution.py:381
  (21 shorter events, 0.2 us)
Async XLA Ops:
  0.6 4.7 %copy-start.1 = (bf16[512,1024]{1,0:T(8,128)(2,1)S(1)}, bf16[512,1024]{1,0:T(8,128)(2,1)}, u32[]{:S(2)}) copy-start(bf16[512,1024]{1,0:T(8,128)(2,1)} %go_ref) | copy-start | bytes 3145732
  0.6 4.7 %copy-start.2 = (f32[128,512]{1,0:T(8,128)S(1)}, f32[128,512]{1,0:T(8,128)}, u32[]{:S(2)}) copy-start(f32[128,512]{1,0:T(8,128)} %first_ref.1) | copy-start | bytes 786436
  0.7 4.7 %copy-start.3 = (f32[128,512]{1,0:T(8,128)S(1)}, f32[128,512]{1,0:T(8,128)}, u32[]{:S(2)}) copy-start(f32[128,512]{1,0:T(8,128)} %second_ref.1) | copy-start | bytes 786436
  5.3 1.0 copy-start.5
  5.5 0.7 collective-permute-start
  27.4 13.8 %collective-permute-start.2 = (bf16[128,384]{1,0:T(8,128)(2,1)S(1)}, bf16[128,384]{1,0:T(8,128)(2,1)S(1)}, u32[]{:S(2)}, u32[]{:S(2)}) collective-permute-start(bf16[128,384]{1,0:T(8,128)(2,1)S(1)} %slice.20), channel_id=1, source_target_pairs={{0,16},{8,24},{16,0},{24,8},{32,48},{40,56},{48,32},{56,40},{64,80... | collective-permute-start | bytes 294920 | tf_op jit(solution)/shard_map/ppermute | solution.py:325
  28.8 24.8 %copy-start.4 = (s32[32,1]{0,1:T(1,128)S(1)}, s32[32,1]{0,1:T(1,128)}, u32[]{:S(2)}) copy-start(s32[32,1]{0,1:T(1,128)} %param.9) | copy-start | bytes 388
  29.6 18.9 %all-to-all-start.1 = ((bf16[8,64,512]{2,1,0:T(8,128)(2,1)}), bf16[8,64,512]{2,1,0:T(8,128)(2,1)S(1)}, u32[]{:S(2)}, u32[]{:S(2)}) async-start(bf16[8,64,512]{2,1,0:T(8,128)(2,1)} %broadcast_in_dim.4), calls=%async_computation.1 | async-start | bytes 1048576 | tf_op jit(solution)/shard_map/all_to_all | solution.py:305
  33.1 8.0 %collective-permute-start.1 = (bf16[128,128]{1,0:T(8,128)(2,1)S(1)}, bf16[128,128]{1,0:T(8,128)(2,1)S(1)}, u32[]{:S(2)}, u32[]{:S(2)}) collective-permute-start(bf16[128,128]{1,0:T(8,128)(2,1)S(1)} %slice.19), channel_id=1, source_target_pairs={{8,24},{24,8},{40,56},{56,40},{72,88},{88,72},{104,120},{120,104},... | collective-permute-start | bytes 98312 | tf_op jit(solution)/shard_map/ppermute | solution.py:324
  35.3 13.2 %collective-permute-start.5 = (bf16[512,512]{1,0:T(8,128)(2,1)S(1)}, bf16[512,512]{1,0:T(8,128)(2,1)S(1)}, u32[]{:S(2)}, u32[]{:S(2)}) collective-permute-start(bf16[512,512]{1,0:T(8,128)(2,1)S(1)} %get-tuple-element.81), channel_id=1, source_target_pairs={{0,8},{8,0},{16,24},{24,16},{32,40},{40,32},{48,56},{56,48},{64,72... | collective-permute-start | bytes 1572872 | tf_op jit(solution)/shard_map/ppermute | solution.py:299
  41.2 5.2 %collective-permute-start.3 = (bf16[256,256]{1,0:T(8,128)(2,1)S(1)}, bf16[256,256]{1,0:T(8,128)(2,1)S(1)}, u32[]{:S(2)}, u32[]{:S(2)}) collective-permute-start(bf16[256,256]{1,0:T(8,128)(2,1)S(1)} %get-tuple-element.116), channel_id=1, source_target_pairs={{0,64},{8,72},{16,80},{24,88},{32,96},{40,104},{48,112},{56,120},{... | collective-permute-start | bytes 393224 | tf_op jit(solution)/shard_map/ppermute | solution.py:328
  46.4 2.1 %collective-permute-start.4 = (bf16[512,256]{1,0:T(8,128)(2,1)S(1)}, bf16[512,256]{1,0:T(8,128)(2,1)S(1)}, u32[]{:S(2)}, u32[]{:S(2)}) collective-permute-start(bf16[512,256]{1,0:T(8,128)(2,1)S(1)} %pad_maximum_fusion.1.near_ref), channel_id=1, source_target_pairs={{0,8},{8,0},{16,24},{24,16},{32,40},{40,32},{48,56},{56,48},{64,72... | collective-permute-start | bytes 786440 | tf_op jit(solution)/shard_map/ppermute | solution.py:299
  48.5 6.6 %collective-permute-start.6 = (bf16[512,512]{1,0:T(8,128)(2,1)S(1)}, bf16[512,512]{1,0:T(8,128)(2,1)S(1)}, u32[]{:S(2)}, u32[]{:S(2)}) collective-permute-start(bf16[512,512]{1,0:T(8,128)(2,1)S(1)} %bitcast.8), channel_id=1, source_target_pairs={{0,8},{8,0},{16,24},{24,16},{32,40},{40,32},{48,56},{56,48},{64,72... | collective-permute-start | bytes 1572872 | tf_op jit(solution)/shard_map/ppermute | solution.py:299
  88.5 19.1 %copy-start = (bf16[3584,512]{1,0:T(8,128)(2,1)S(1)}, bf16[3584,512]{1,0:T(8,128)(2,1)}, u32[]{:S(2)}) copy-start(bf16[3584,512]{1,0:T(8,128)(2,1)} %basis_ref.3) | copy-start | bytes 11010052
  103.9 5.7 %collective-permute-start.7 = (bf16[512,512]{1,0:T(8,128)(2,1)S(1)}, bf16[512,512]{1,0:T(8,128)(2,1)S(1)}, u32[]{:S(2)}, u32[]{:S(2)}) collective-permute-start(bf16[512,512]{1,0:T(8,128)(2,1)S(1)} %bitcast.10), channel_id=1, source_target_pairs={{0,8},{8,0},{16,24},{24,16},{32,40},{40,32},{48,56},{56,48},{64,72... | collective-permute-start | bytes 1572872 | tf_op jit(solution)/shard_map/ppermute | solution.py:299

commit v11 on v7

--- a/solution.py
+++ b/solution.py
@@ -308,18 +308,22 @@
     owners = owners.reshape(1, frags)
 
     part = coeffs_call(hidden, basis)
-    part, grad_out, first, second = lax.optimization_barrier(
-        (part, grad_out, first_moment, second_moment)
-    )
+    part, me, grad_out, first, second = lax.optimization_barrier(
+        (part, me, grad_out, first_moment, second_moment)
+    )
+    go_mine, go_theirs, keep, send = sort_call(me, grad_out, first, second)
+    got_x = lax.ppermute(send, "dp", next_x[0::2])
+    part, keep, send, got_x, go_theirs = lax.optimization_barrier((part, keep, send, got_x, go_theirs))
     part = over_planes(part)
-    go_mine, go_theirs, keep, send = sort_call(me, grad_out, first, second)
-    go_other = other_core(go_theirs)
-    near = jnp.concatenate([keep, lax.ppermute(send, "dp", next_x)], axis=0)
+    got_x = got_x + lax.ppermute(send, "dp", next_x[1::2])
+    near = jnp.concatenate([keep, got_x], axis=0)
     keep, send = near[:, : RANK // 2], near[:, RANK // 2 :]
     near = jnp.concatenate([keep, lax.ppermute(send, "dp", next_y)], axis=0)
+    near, go_theirs = lax.optimization_barrier((near, go_theirs))
     far = other_core(near)
-    part, near, far, go_mine, go_other = lax.optimization_barrier(
-        (part, near, far, go_mine, go_other)
+    go_other = other_core(go_theirs)
+    part, near, far, go_mine, go_other, me, owners = lax.optimization_barrier(
+        (part, near, far, go_mine, go_other, me, owners)
     )
     part = part.reshape(planes, tok // planes, RANK)
     mine = jnp.sum(part.astype(f32), axis=0).astype(bf16)

time: 114 us -> 115 us (level)
  waiting for transfers between devices: 16 us -> 4.94 us
  starting transfers between devices: 18.1 us -> 28.6 us
  blocking collectives: 68.2 us -> 69.7 us
    all_to_all x1, waiting for transfers between devices: 10.7 us -> 0.01 us  [over_planes(): return lax.all_to_all(x, 'mp', 0, 0, tiled=True)]
    ppermute x4, starting transfers between devices: 6.78 us -> 14.4 us  [other_core(): return lax.ppermute(x, 'dp', swap)]
    ppermute x1 -> x2, starting transfers between devices: 2.13 us -> 4.62 us  [the longest x1 3.95 us: body(): got_x = got_x + lax.ppermute(send, 'dp', next_x[1::2])]
    all_to_all x2, blocking collectives: 32.9 us -> 34.1 us  [over_planes(): return lax.all_to_all(x, 'mp', 0, 0, tiled=True)]
  transfers between devices with their start and end apart: 7 -> 8, of which waited for: 4 -> 3; matrix products, arithmetic and copies ran while one was open for 0% -> 0% of each run, Pallas kernels for 3% -> 3%
where the time goes in v11:
time: 115 us; the launch traced here: 114 us
  blocking collectives  69.7 us (61%)
  starting transfers between devices  28.6 us (25%)
  Pallas kernels  9.78 us (9%)
  waiting for transfers between devices  4.94 us (4%)
    all_to_all x2, blocking collectives, over_chips(): lax.all_to_all(x, 'dp', 0, 0, axis_index_groups=same_core, tiled=True)  35.7 us
    all_to_all x2, blocking collectives, over_planes(): return lax.all_to_all(x, 'mp', 0, 0, tiled=True)  34.1 us
    ppermute x4, starting transfers between devices, other_core(): return lax.ppermute(x, 'dp', swap)  14.4 us
    all_to_all x1, starting transfers between devices, over_planes(): return lax.all_to_all(x, 'mp', 0, 0, tiled=True)  8.2 us
    pallas_call x1, Pallas kernels, coeffs_call(): pl.pallas_call(coeffs_kernel, in_specs=[pl.BlockSpec(memory_space=pl.ANY)...  4.61 us
    ppermute x1, starting transfers between devices, body(): got_x = got_x + lax.ppermute(send, 'dp', next_x[1::2])  3.95 us
    ppermute x1, waiting for transfers between devices, body(): near = jnp.concatenate([keep, lax.ppermute(send, 'dp', next_y)], axis=0)  2.52 us
    ppermute x4, waiting for transfers between devices, other_core(): return lax.ppermute(x, 'dp', swap)  2.41 us
  transfers between devices with their start and end apart: 8, of which 3 were waited for; matrix products, arithmetic and copies ran while one was open for 0% of the time, Pallas kernels for 3%

profile of v11, /device:TPU:1, one launch (start us, length us, event | category | flops | bytes accessed | tf_op | source)
XLA Modules:
  0.0 114.2 jit_solution(2443715113253072812)
XLA Ops:
  0.6 0.0 copy-start.1
  0.7 4.6 %shard_map.85 = bf16[512,512]{1,0:T(8,128)(2,1)} custom-call(bf16[512,3584]{1,0:T(8,128)(2,1)} %hidden_ref.1, bf16[3584,512]{1,0:T(8,128)(2,1)} %basis_ref.3), custom_call_target="tpu_custom_call" | custom-call | tf_op jit(solution)/shard_map/pallas_call | solution.py:78
  5.3 0.1 shard_map.86
  5.5 0.7 collective-permute-start
  6.2 0.0 collective-permute-done
  6.2 3.9 %collective-permute-start.1 = (bf16[128,512]{1,0:T(8,128)(2,1)S(1)}, bf16[128,512]{1,0:T(8,128)(2,1)S(1)}, u32[]{:S(2)}, u32[]{:S(2)}) collective-permute-start(bf16[128,512]{1,0:T(8,128)(2,1)S(1)} %get-tuple-element.75), channel_id=1, source_target_pairs={{8,24},{24,8},{40,56},{56,40},{72,88},{88,72},{104,120},{120,104},... | collective-permute-start | bytes 393224 | tf_op jit(solution)/shard_map/ppermute | solution.py:318
  10.1 8.2 %all-to-all-start = ((bf16[8,64,512]{2,1,0:T(8,128)(2,1)}), bf16[8,64,512]{2,1,0:T(8,128)(2,1)S(1)}, u32[]{:S(2)}, u32[]{:S(2)}) async-start(bf16[8,64,512]{2,1,0:T(8,128)(2,1)} %bitcast.17), calls=%async_computation | async-start | bytes 1048576 | tf_op jit(solution)/shard_map/all_to_all | solution.py:305
  18.3 0.0 collective-permute-done.1
  18.4 1.4 %collective-permute-start.2 = (bf16[256,256]{1,0:T(8,128)(2,1)S(1)}, bf16[256,256]{1,0:T(8,128)(2,1)S(1)}, u32[]{:S(2)}, u32[]{:S(2)}) collective-permute-start(bf16[256,256]{1,0:T(8,128)(2,1)S(1)} %get-tuple-element.126), channel_id=1, source_target_pairs={{0,64},{8,72},{16,80},{24,88},{32,96},{40,104},{48,112},{56,120},{... | collective-permute-start | bytes 393224 | tf_op jit(solution)/shard_map/ppermute | solution.py:321
  19.8 2.5 %collective-permute-done.2 = bf16[256,256]{1,0:T(8,128)(2,1)S(1)} collective-permute-done((bf16[256,256]{1,0:T(8,128)(2,1)S(1)}, bf16[256,256]{1,0:T(8,128)(2,1)S(1)}, u32[]{:S(2)}, u32[]{:S(2)}) %collective-permute-start.2) | collective-permute-done | bytes 131104 | tf_op jit(solution)/shard_map/ppermute | solution.py:321
  22.3 6.9 %collective-permute-start.4 = (bf16[512,512]{1,0:T(8,128)(2,1)S(1)}, bf16[512,512]{1,0:T(8,128)(2,1)S(1)}, u32[]{:S(2)}, u32[]{:S(2)}) collective-permute-start(bf16[512,512]{1,0:T(8,128)(2,1)S(1)} %get-tuple-element.79), channel_id=1, source_target_pairs={{0,8},{8,0},{16,24},{24,16},{32,40},{40,32},{48,56},{56,48},{64,72... | collective-permute-start | bytes 1572872 | tf_op jit(solution)/shard_map/ppermute | solution.py:299
  29.2 0.1 collective-permute-start.3
  29.3 1.8 %collective-permute-done.3.far_ref = bf16[512,256]{1,0:T(8,128)(2,1)S(1)} collective-permute-done((bf16[512,256]{1,0:T(8,128)(2,1)S(1)}, bf16[512,256]{1,0:T(8,128)(2,1)S(1)}, u32[]{:S(2)}, u32[]{:S(2)}) %collective-permute-start.3) | collective-permute-done | bytes 262176 | tf_op jit(solution)/shard_map/ppermute | solution.py:299
  31.1 0.0 collective-permute-done.4.other_ref
  31.1 0.0 all-to-all-done
  31.1 0.1 reduce_sum.12
  31.2 21.5 %all_to_all.39 = bf16[8,64,512]{2,1,0:T(8,128)(2,1)S(1)} all-to-all(bf16[8,64,512]{2,1,0:T(8,128)(2,1)S(1)} %broadcast_in_dim.4), channel_id=1, replica_groups=mesh['dp'=32,'mp'=8] {'mp'}, dimensions={0} | all-to-all | bytes 1048576 | tf_op jit(solution)/shard_map/all_to_all | solution.py:305
  52.7 3.7 %collective-permute-start.5 = (bf16[512,512]{1,0:T(8,128)(2,1)S(1)}, bf16[512,512]{1,0:T(8,128)(2,1)S(1)}, u32[]{:S(2)}, u32[]{:S(2)}) collective-permute-start(bf16[512,512]{1,0:T(8,128)(2,1)S(1)} %bitcast.12), channel_id=1, source_target_pairs={{0,8},{8,0},{16,24},{24,16},{32,40},{40,32},{48,56},{56,48},{64,72... | collective-permute-start | bytes 1572872 | tf_op jit(solution)/shard_map/ppermute | solution.py:299
  56.4 0.9 shard_map.87
  57.3 0.6 collective-permute-done.5.co_other_ref
  57.9 0.5 shard_map.88
  58.4 20.4 %all_to_all.40.got_ref = bf16[16,48,512]{2,1,0:T(8,128)(2,1)S(1)} all-to-all(bf16[16,48,512]{2,1,0:T(8,128)(2,1)S(1)} %shard_map.88), channel_id=1, replica_groups={{0,16,32,48,64,80,96,112,128,144,160,176,192,208,224,240},{8,24,40,56,7..., dimensions={0} | all-to-all | bytes 1572864 | tf_op jit(solution)/shard_map/all_to_all | solution.py:302
  78.8 0.2 shard_map.89
  79.0 12.6 %all_to_all.41 = bf16[8,32,512]{2,1,0:T(8,128)(2,1)S(1)} all-to-all(bf16[8,32,512]{2,1,0:T(8,128)(2,1)S(1)} %get-tuple-element.109), channel_id=1, replica_groups=mesh['dp'=32,'mp'=8] {'mp'}, dimensions={0} | all-to-all | bytes 524288 | tf_op jit(solution)/shard_map/all_to_all | solution.py:305
  91.6 0.0 copy-start
  91.6 0.1 pad_maximum_fusion
  91.7 15.3 %all_to_all.42.last_ref = bf16[16,48,512]{2,1,0:T(8,128)(2,1)S(1)} all-to-all(bf16[16,48,512]{2,1,0:T(8,128)(2,1)S(1)} %pad_maximum_fusion), channel_id=1, replica_groups={{0,16,32,48,64,80,96,112,128,144,160,176,192,208,224,240},{8,24,40,56,7..., dimensions={0} | all-to-all | bytes 1572864 | tf_op jit(solution)/shard_map/all_to_all | solution.py:302
  107.0 3.7 %collective-permute-start.6 = (bf16[512,512]{1,0:T(8,128)(2,1)S(1)}, bf16[512,512]{1,0:T(8,128)(2,1)S(1)}, u32[]{:S(2)}, u32[]{:S(2)}) collective-permute-start(bf16[512,512]{1,0:T(8,128)(2,1)S(1)} %bitcast.10), channel_id=1, source_target_pairs={{0,8},{8,0},{16,24},{24,16},{32,40},{40,32},{48,56},{56,48},{64,72... | collective-permute-start | bytes 1572872 | tf_op jit(solution)/shard_map/ppermute | solution.py:299
  110.7 0.0 copy-done
  110.7 2.0 %shard_map.90 = bf16[3584,256]{1,0:T(8,128)(2,1)} custom-call(bf16[3584,512]{1,0:T(8,128)(2,1)S(1)} %copy-done, bf16[16,48,512]{2,1,0:T(8,128)(2,1)S(1)} %all_to_all.42.last_ref), custom_call_target="tpu_custom_call" | custom-call | tf_op jit(solution)/shard_map/pallas_call | solution.py:234
  112.8 0.0 collective-permute-done.6.sums_other_ref
  112.8 1.4 %shard_map.91 = (f32[128,512]{1,0:T(8,128)}, f32[128,512]{1,0:T(8,128)}) custom-call(s32[1]{0:T(128)} %bitcast.me_ref, s32[1,32]{1,0:T(1,128)S(1)} %bitcast.16, f32[128,512]{1,0:T(8,128)S(1)} %copy-done.2, f32[128,512]{1,0:T(8,128)S(1)} %copy-done.3, bf16[512,512]{1,0:T(8,128)(2,1)S(1)} %bitcast.11, bf16[512,512]{1,0:T(8,128)(2,1)S(1)} %collective-permute-done.6.sums_other_ref), custom_call_target="tpu_custom_call" | custom-call | tf_op jit(solution)/shard_map/pallas_call | solution.py:381
  (13 shorter events, 0.2 us)
Async XLA Ops:
  0.6 4.7 %copy-start.1 = (bf16[512,1024]{1,0:T(8,128)(2,1)S(1)}, bf16[512,1024]{1,0:T(8,128)(2,1)}, u32[]{:S(2)}) copy-start(bf16[512,1024]{1,0:T(8,128)(2,1)} %go_ref) | copy-start | bytes 3145732
  0.6 4.7 %copy-start.2 = (f32[128,512]{1,0:T(8,128)S(1)}, f32[128,512]{1,0:T(8,128)}, u32[]{:S(2)}) copy-start(f32[128,512]{1,0:T(8,128)} %first_ref.1) | copy-start | bytes 786436
  0.7 4.7 %copy-start.3 = (f32[128,512]{1,0:T(8,128)S(1)}, f32[128,512]{1,0:T(8,128)}, u32[]{:S(2)}) copy-start(f32[128,512]{1,0:T(8,128)} %second_ref.1) | copy-start | bytes 786436
  5.5 0.7 collective-permute-start
  6.2 12.2 %collective-permute-start.1 = (bf16[128,512]{1,0:T(8,128)(2,1)S(1)}, bf16[128,512]{1,0:T(8,128)(2,1)S(1)}, u32[]{:S(2)}, u32[]{:S(2)}) collective-permute-start(bf16[128,512]{1,0:T(8,128)(2,1)S(1)} %get-tuple-element.75), channel_id=1, source_target_pairs={{8,24},{24,8},{40,56},{56,40},{72,88},{88,72},{104,120},{120,104},... | collective-permute-start | bytes 393224 | tf_op jit(solution)/shard_map/ppermute | solution.py:318
  10.1 21.0 %all-to-all-start = ((bf16[8,64,512]{2,1,0:T(8,128)(2,1)}), bf16[8,64,512]{2,1,0:T(8,128)(2,1)S(1)}, u32[]{:S(2)}, u32[]{:S(2)}) async-start(bf16[8,64,512]{2,1,0:T(8,128)(2,1)} %bitcast.17), calls=%async_computation | async-start | bytes 1048576 | tf_op jit(solution)/shard_map/all_to_all | solution.py:305
  18.3 38.1 %copy-start.4 = (s32[32,1]{0,1:T(1,128)S(1)}, s32[32,1]{0,1:T(1,128)}, u32[]{:S(2)}) copy-start(s32[32,1]{0,1:T(1,128)} %param.9) | copy-start | bytes 388
  18.4 3.9 %collective-permute-start.2 = (bf16[256,256]{1,0:T(8,128)(2,1)S(1)}, bf16[256,256]{1,0:T(8,128)(2,1)S(1)}, u32[]{:S(2)}, u32[]{:S(2)}) collective-permute-start(bf16[256,256]{1,0:T(8,128)(2,1)S(1)} %get-tuple-element.126), channel_id=1, source_target_pairs={{0,64},{8,72},{16,80},{24,88},{32,96},{40,104},{48,112},{56,120},{... | collective-permute-start | bytes 393224 | tf_op jit(solution)/shard_map/ppermute | solution.py:321
  22.3 8.8 %collective-permute-start.4 = (bf16[512,512]{1,0:T(8,128)(2,1)S(1)}, bf16[512,512]{1,0:T(8,128)(2,1)S(1)}, u32[]{:S(2)}, u32[]{:S(2)}) collective-permute-start(bf16[512,512]{1,0:T(8,128)(2,1)S(1)} %get-tuple-element.79), channel_id=1, source_target_pairs={{0,8},{8,0},{16,24},{24,16},{32,40},{40,32},{48,56},{56,48},{64,72... | collective-permute-start | bytes 1572872 | tf_op jit(solution)/shard_map/ppermute | solution.py:299
  29.2 1.9 %collective-permute-start.3 = (bf16[512,256]{1,0:T(8,128)(2,1)S(1)}, bf16[512,256]{1,0:T(8,128)(2,1)S(1)}, u32[]{:S(2)}, u32[]{:S(2)}) collective-permute-start(bf16[512,256]{1,0:T(8,128)(2,1)S(1)} %pad_maximum_fusion.1.near_ref), channel_id=1, source_target_pairs={{0,8},{8,0},{16,24},{24,16},{32,40},{40,32},{48,56},{56,48},{64,72... | collective-permute-start | bytes 786440 | tf_op jit(solution)/shard_map/ppermute | solution.py:299
  52.7 5.2 %collective-permute-start.5 = (bf16[512,512]{1,0:T(8,128)(2,1)S(1)}, bf16[512,512]{1,0:T(8,128)(2,1)S(1)}, u32[]{:S(2)}, u32[]{:S(2)}) collective-permute-start(bf16[512,512]{1,0:T(8,128)(2,1)S(1)} %bitcast.12), channel_id=1, source_target_pairs={{0,8},{8,0},{16,24},{24,16},{32,40},{40,32},{48,56},{56,48},{64,72... | collective-permute-start | bytes 1572872 | tf_op jit(solution)/shard_map/ppermute | solution.py:299
  91.6 19.1 %copy-start = (bf16[3584,512]{1,0:T(8,128)(2,1)S(1)}, bf16[3584,512]{1,0:T(8,128)(2,1)}, u32[]{:S(2)}) copy-start(bf16[3584,512]{1,0:T(8,128)(2,1)} %basis_ref.3) | copy-start | bytes 11010052
  107.0 5.7 %collective-permute-start.6 = (bf16[512,512]{1,0:T(8,128)(2,1)S(1)}, bf16[512,512]{1,0:T(8,128)(2,1)S(1)}, u32[]{:S(2)}, u32[]{:S(2)}) collective-permute-start(bf16[512,512]{1,0:T(8,128)(2,1)S(1)} %bitcast.10), channel_id=1, source_target_pairs={{0,8},{8,0},{16,24},{24,16},{32,40},{40,32},{48,56},{56,48},{64,72... | collective-permute-start | bytes 1572872 | tf_op jit(solution)/shard_map/ppermute | solution.py:299

commit v12 on v9

--- a/solution.py
+++ b/solution.py
@@ -307,23 +307,31 @@
     me = lax.axis_index("dp").reshape(1)
     owners = owners.reshape(1, frags)
 
+    even, odd = slice(0, None, 2), slice(1, None, 2)
+    early, half = RANK // SQUARE, RANK // 2
     part = coeffs_call(hidden, basis)
     part, me, grad_out, first, second = lax.optimization_barrier(
         (part, me, grad_out, first_moment, second_moment)
     )
     go_mine, go_theirs, keep, send = sort_call(me, grad_out, first, second)
-    got_x = lax.ppermute(send, "dp", next_x[0::2])
-    part, (me, owners, go_mine, go_theirs, keep, send, got_x) = over(
-        over_planes, part, me, owners, go_mine, go_theirs, keep, send, got_x
+    got_x = lax.ppermute(send[:, :early], "dp", next_x[even])
+    part, keep, send, got_x = lax.optimization_barrier((part, keep, send, got_x))
+    part = over_planes(part)
+    got_x = jnp.concatenate([got_x, lax.ppermute(send[:, early:], "dp", next_x[even])], axis=1)
+    near = jnp.concatenate([keep, got_x], axis=0)
+    got_y = lax.ppermute(near[:, half:], "dp", next_y[even])
+    part, keep, send, got_x, got_y, go_mine, go_theirs, me, owners = lax.optimization_barrier(
+        (part, keep, send, got_x, got_y, go_mine, go_theirs, me, owners)
     )
     part = part.reshape(planes, tok // planes, RANK)
     mine = jnp.sum(part.astype(f32), axis=0).astype(bf16)
     mine = jnp.broadcast_to(mine[None], part.shape).reshape(tok, RANK)
     coeffs = over_planes(mine)
-    got_x = got_x + lax.ppermute(send, "dp", next_x[1::2])
+    got_x = got_x + lax.ppermute(send, "dp", next_x[odd])
     near = jnp.concatenate([keep, got_x], axis=0)
-    keep, send = near[:, : RANK // 2], near[:, RANK // 2 :]
-    near = jnp.concatenate([keep, lax.ppermute(send, "dp", next_y)], axis=0)
+    got_y = got_y + lax.ppermute(near[:, half:], "dp", next_y[odd])
+    near = jnp.concatenate([near[:, :half], got_y], axis=0)
+    near, go_theirs = lax.optimization_barrier((near, go_theirs))
     far = other_core(near)
     go_other = other_core(go_theirs)
     coeffs, near, far, go_mine, go_other, me, owners = lax.optimization_barrier(

time: 111 us -> 116 us (1.045)
  blocking collectives: 69.2 us -> 48.2 us
  starting transfers between devices: 24.1 us -> 39.5 us
  waiting for transfers between devices: 5.58 us -> 15.8 us
    all_to_all x2 -> x1, blocking collectives: 33.5 us -> 12.6 us  [over_planes(): return lax.all_to_all(x, 'mp', 0, 0, tiled=True)]
    all_to_all x1 -> x2, waiting for transfers between devices: 0.01 us -> 10.9 us  [over_planes(): return lax.all_to_all(x, 'mp', 0, 0, tiled=True)]
    all_to_all x1 -> x2, starting transfers between devices: 3.49 us -> 12.5 us  [over_planes(): return lax.all_to_all(x, 'mp', 0, 0, tiled=True)]
    ppermute x4, starting transfers between devices: 15.4 us -> 18.6 us  [other_core(): return lax.ppermute(x, 'dp', swap)]
    ppermute x3 -> x5, starting transfers between devices: 5.17 us -> 8.31 us  [the longest x1 3.2 us: body(): got_y = got_y + lax.ppermute(near[:, half:], 'dp', next_y[odd])]
    ppermute x3 -> x5, waiting for transfers between devices: 3.81 us -> 2.51 us  [the longest x1 2.5 us: body(): got_y = got_y + lax.ppermute(near[:, half:], 'dp', next_y[odd])]
  transfers between devices with their start and end apart: 8 -> 11, of which waited for: 3 -> 4; matrix products, arithmetic and copies ran while one was open for 0% -> 1% of each run, Pallas kernels for 3% -> 3%
where the time goes in v12:
time: 116 us; the launch traced here: 115 us
  blocking collectives  48.2 us (42%)
  starting transfers between devices  39.5 us (34%)
  waiting for transfers between devices  15.8 us (14%)
  Pallas kernels  9.79 us (8%)
    all_to_all x2, blocking collectives, over_chips(): lax.all_to_all(x, 'dp', 0, 0, axis_index_groups=same_core, tiled=True)  35.7 us
    ppermute x4, starting transfers between devices, other_core(): return lax.ppermute(x, 'dp', swap)  18.6 us
    all_to_all x1, blocking collectives, over_planes(): return lax.all_to_all(x, 'mp', 0, 0, tiled=True)  12.6 us
    all_to_all x2, starting transfers between devices, over_planes(): return lax.all_to_all(x, 'mp', 0, 0, tiled=True)  12.5 us
    all_to_all x2, waiting for transfers between devices, over_planes(): return lax.all_to_all(x, 'mp', 0, 0, tiled=True)  10.9 us
    pallas_call x1, Pallas kernels, coeffs_call(): pl.pallas_call(coeffs_kernel, in_specs=[pl.BlockSpec(memory_space=pl.ANY)...  4.61 us
    ppermute x1, starting transfers between devices, body(): got_y = got_y + lax.ppermute(near[:, half:], 'dp', next_y[odd])  3.2 us
    ppermute x1, starting transfers between devices, body(): got_x = got_x + lax.ppermute(send, 'dp', next_x[odd])  3.11 us
  transfers between devices with their start and end apart: 11, of which 4 were waited for; matrix products, arithmetic and copies ran while one was open for 1% of the time, Pallas kernels for 3%

profile of v12, /device:TPU:1, one launch (start us, length us, event | category | flops | bytes accessed | tf_op | source)
XLA Modules:
  0.0 115.4 jit_solution(4060838140503939737)
XLA Ops:
  0.7 4.6 %shard_map.85 = bf16[512,512]{1,0:T(8,128)(2,1)} custom-call(bf16[512,3584]{1,0:T(8,128)(2,1)} %hidden_ref.1, bf16[3584,512]{1,0:T(8,128)(2,1)} %basis_ref.3), custom_call_target="tpu_custom_call" | custom-call | tf_op jit(solution)/shard_map/pallas_call | solution.py:78
  5.3 0.1 shard_map.86
  5.5 0.7 collective-permute-start
  6.2 0.0 collective-permute-done
  6.2 9.0 %all-to-all-start = ((bf16[8,64,512]{2,1,0:T(8,128)(2,1)}), bf16[8,64,512]{2,1,0:T(8,128)(2,1)S(1)}, u32[]{:S(2)}, u32[]{:S(2)}) async-start(bf16[8,64,512]{2,1,0:T(8,128)(2,1)} %bitcast.15), calls=%async_computation | async-start | bytes 1048576 | tf_op jit(solution)/shard_map/all_to_all | solution.py:305
  15.2 0.7 collective-permute-start.1
  15.9 0.0 collective-permute-done.1
  16.0 0.7 collective-permute-start.2
  16.6 10.9 %all-to-all-done = bf16[8,64,512]{2,1,0:T(8,128)(2,1)S(1)} async-done(((bf16[8,64,512]{2,1,0:T(8,128)(2,1)}), bf16[8,64,512]{2,1,0:T(8,128)(2,1)S(1)}, u32[]{:S(2)}, u32[]{:S(2)}) %all-to-all-start) | async-done | bytes 524320 | tf_op jit(solution)/shard_map/all_to_all | solution.py:305
  27.5 3.1 %collective-permute-start.3 = (bf16[128,512]{1,0:T(8,128)(2,1)S(1)}, bf16[128,512]{1,0:T(8,128)(2,1)S(1)}, u32[]{:S(2)}, u32[]{:S(2)}) collective-permute-start(bf16[128,512]{1,0:T(8,128)(2,1)S(1)} %get-tuple-element.74), channel_id=1, source_target_pairs={{8,24},{24,8},{40,56},{56,40},{72,88},{88,72},{104,120},{120,104},... | collective-permute-start | bytes 393224 | tf_op jit(solution)/shard_map/ppermute | solution.py:330
  30.6 0.1 reduce_sum.12
  30.7 0.0 copy-start.4
  30.7 0.8 broadcast_in_dim.4
  31.5 3.5 %all-to-all-start.1 = ((bf16[8,64,512]{2,1,0:T(8,128)(2,1)}), bf16[8,64,512]{2,1,0:T(8,128)(2,1)S(1)}, u32[]{:S(2)}, u32[]{:S(2)}) async-start(bf16[8,64,512]{2,1,0:T(8,128)(2,1)} %broadcast_in_dim.4), calls=%async_computation.1 | async-start | bytes 1048576 | tf_op jit(solution)/shard_map/all_to_all | solution.py:305
  35.1 3.2 %collective-permute-start.4 = (bf16[256,256]{1,0:T(8,128)(2,1)S(1)}, bf16[256,256]{1,0:T(8,128)(2,1)S(1)}, u32[]{:S(2)}, u32[]{:S(2)}) collective-permute-start(bf16[256,256]{1,0:T(8,128)(2,1)S(1)} %get-tuple-element.114), channel_id=1, source_target_pairs={{8,72},{24,88},{40,104},{56,120},{72,8},{88,24},{104,40},{120,56},... | collective-permute-start | bytes 393224 | tf_op jit(solution)/shard_map/ppermute | solution.py:332
  38.3 2.5 %collective-permute-done.4 = bf16[256,256]{1,0:T(8,128)(2,1)S(1)} collective-permute-done((bf16[256,256]{1,0:T(8,128)(2,1)S(1)}, bf16[256,256]{1,0:T(8,128)(2,1)S(1)}, u32[]{:S(2)}, u32[]{:S(2)}) %collective-permute-start.4) | collective-permute-done | bytes 131104 | tf_op jit(solution)/shard_map/ppermute | solution.py:332
  40.9 4.3 %collective-permute-start.6 = (bf16[512,512]{1,0:T(8,128)(2,1)S(1)}, bf16[512,512]{1,0:T(8,128)(2,1)S(1)}, u32[]{:S(2)}, u32[]{:S(2)}) collective-permute-start(bf16[512,512]{1,0:T(8,128)(2,1)S(1)} %get-tuple-element.79), channel_id=1, source_target_pairs={{0,8},{8,0},{16,24},{24,16},{32,40},{40,32},{48,56},{56,48},{64,72... | collective-permute-start | bytes 1572872 | tf_op jit(solution)/shard_map/ppermute | solution.py:299
  45.3 0.1 collective-permute-start.5
  45.4 1.8 %collective-permute-done.5.far_ref = bf16[512,256]{1,0:T(8,128)(2,1)S(1)} collective-permute-done((bf16[512,256]{1,0:T(8,128)(2,1)S(1)}, bf16[512,256]{1,0:T(8,128)(2,1)S(1)}, u32[]{:S(2)}, u32[]{:S(2)}) %collective-permute-start.5) | collective-permute-done | bytes 262176 | tf_op jit(solution)/shard_map/ppermute | solution.py:299
  47.2 10.5 %collective-permute-start.7 = (bf16[512,512]{1,0:T(8,128)(2,1)S(1)}, bf16[512,512]{1,0:T(8,128)(2,1)S(1)}, u32[]{:S(2)}, u32[]{:S(2)}) collective-permute-start(bf16[512,512]{1,0:T(8,128)(2,1)S(1)} %bitcast.8), channel_id=1, source_target_pairs={{0,8},{8,0},{16,24},{24,16},{32,40},{40,32},{48,56},{56,48},{64,72... | collective-permute-start | bytes 1572872 | tf_op jit(solution)/shard_map/ppermute | solution.py:299
  57.6 0.9 shard_map.87
  58.6 0.6 collective-permute-done.7.co_other_ref
  59.2 0.5 shard_map.88
  59.6 20.4 %all_to_all.36.got_ref = bf16[16,48,512]{2,1,0:T(8,128)(2,1)S(1)} all-to-all(bf16[16,48,512]{2,1,0:T(8,128)(2,1)S(1)} %shard_map.88), channel_id=1, replica_groups={{0,16,32,48,64,80,96,112,128,144,160,176,192,208,224,240},{8,24,40,56,7..., dimensions={0} | all-to-all | bytes 1572864 | tf_op jit(solution)/shard_map/all_to_all | solution.py:302
  80.0 0.2 shard_map.89
  80.2 12.6 %all_to_all.37 = bf16[8,32,512]{2,1,0:T(8,128)(2,1)S(1)} all-to-all(bf16[8,32,512]{2,1,0:T(8,128)(2,1)S(1)} %get-tuple-element.97), channel_id=1, replica_groups=mesh['dp'=32,'mp'=8] {'mp'}, dimensions={0} | all-to-all | bytes 524288 | tf_op jit(solution)/shard_map/all_to_all | solution.py:305
  92.8 0.0 copy-start
  92.8 0.1 pad_maximum_fusion
  92.9 15.3 %all_to_all.38.last_ref = bf16[16,48,512]{2,1,0:T(8,128)(2,1)S(1)} all-to-all(bf16[16,48,512]{2,1,0:T(8,128)(2,1)S(1)} %pad_maximum_fusion), channel_id=1, replica_groups={{0,16,32,48,64,80,96,112,128,144,160,176,192,208,224,240},{8,24,40,56,7..., dimensions={0} | all-to-all | bytes 1572864 | tf_op jit(solution)/shard_map/all_to_all | solution.py:302
  108.2 3.7 %collective-permute-start.8 = (bf16[512,512]{1,0:T(8,128)(2,1)S(1)}, bf16[512,512]{1,0:T(8,128)(2,1)S(1)}, u32[]{:S(2)}, u32[]{:S(2)}) collective-permute-start(bf16[512,512]{1,0:T(8,128)(2,1)S(1)} %bitcast.10), channel_id=1, source_target_pairs={{0,8},{8,0},{16,24},{24,16},{32,40},{40,32},{48,56},{56,48},{64,72... | collective-permute-start | bytes 1572872 | tf_op jit(solution)/shard_map/ppermute | solution.py:299
  112.0 2.0 %shard_map.90 = bf16[3584,256]{1,0:T(8,128)(2,1)} custom-call(bf16[3584,512]{1,0:T(8,128)(2,1)S(1)} %copy-done, bf16[16,48,512]{2,1,0:T(8,128)(2,1)S(1)} %all_to_all.38.last_ref), custom_call_target="tpu_custom_call" | custom-call | tf_op jit(solution)/shard_map/pallas_call | solution.py:234
  114.0 1.4 %shard_map.91 = (f32[128,512]{1,0:T(8,128)}, f32[128,512]{1,0:T(8,128)}) custom-call(s32[1]{0:T(128)} %bitcast.me_ref, s32[1,32]{1,0:T(1,128)S(1)} %bitcast.14, f32[128,512]{1,0:T(8,128)S(1)} %copy-done.2, f32[128,512]{1,0:T(8,128)S(1)} %copy-done.3, bf16[512,512]{1,0:T(8,128)(2,1)S(1)} %bitcast.11, bf16[512,512]{1,0:T(8,128)(2,1)S(1)} %collective-permute-done.8.sums_other_ref), custom_call_target="tpu_custom_call" | custom-call | tf_op jit(solution)/shard_map/pallas_call | solution.py:387
  (24 shorter events, 0.3 us)
Async XLA Ops:
  0.6 4.7 %copy-start.1 = (bf16[512,1024]{1,0:T(8,128)(2,1)S(1)}, bf16[512,1024]{1,0:T(8,128)(2,1)}, u32[]{:S(2)}) copy-start(bf16[512,1024]{1,0:T(8,128)(2,1)} %go_ref) | copy-start | bytes 3145732
  0.6 4.7 %copy-start.2 = (f32[128,512]{1,0:T(8,128)S(1)}, f32[128,512]{1,0:T(8,128)}, u32[]{:S(2)}) copy-start(f32[128,512]{1,0:T(8,128)} %first_ref.1) | copy-start | bytes 786436
  0.7 4.7 %copy-start.3 = (f32[128,512]{1,0:T(8,128)S(1)}, f32[128,512]{1,0:T(8,128)}, u32[]{:S(2)}) copy-start(f32[128,512]{1,0:T(8,128)} %second_ref.1) | copy-start | bytes 786436
  5.5 0.7 collective-permute-start
  6.2 21.3 %all-to-all-start = ((bf16[8,64,512]{2,1,0:T(8,128)(2,1)}), bf16[8,64,512]{2,1,0:T(8,128)(2,1)S(1)}, u32[]{:S(2)}, u32[]{:S(2)}) async-start(bf16[8,64,512]{2,1,0:T(8,128)(2,1)} %bitcast.15), calls=%async_computation | async-start | bytes 1048576 | tf_op jit(solution)/shard_map/all_to_all | solution.py:305
  15.2 0.7 collective-permute-start.1
  16.0 0.7 collective-permute-start.2
  27.5 7.6 %collective-permute-start.3 = (bf16[128,512]{1,0:T(8,128)(2,1)S(1)}, bf16[128,512]{1,0:T(8,128)(2,1)S(1)}, u32[]{:S(2)}, u32[]{:S(2)}) collective-permute-start(bf16[128,512]{1,0:T(8,128)(2,1)S(1)} %get-tuple-element.74), channel_id=1, source_target_pairs={{8,24},{24,8},{40,56},{56,40},{72,88},{88,72},{104,120},{120,104},... | collective-permute-start | bytes 393224 | tf_op jit(solution)/shard_map/ppermute | solution.py:330
  30.7 26.9 %copy-start.4 = (s32[32,1]{0,1:T(1,128)S(1)}, s32[32,1]{0,1:T(1,128)}, u32[]{:S(2)}) copy-start(s32[32,1]{0,1:T(1,128)} %param.9) | copy-start | bytes 388
  31.5 15.6 %all-to-all-start.1 = ((bf16[8,64,512]{2,1,0:T(8,128)(2,1)}), bf16[8,64,512]{2,1,0:T(8,128)(2,1)S(1)}, u32[]{:S(2)}, u32[]{:S(2)}) async-start(bf16[8,64,512]{2,1,0:T(8,128)(2,1)} %broadcast_in_dim.4), calls=%async_computation.1 | async-start | bytes 1048576 | tf_op jit(solution)/shard_map/all_to_all | solution.py:305
  35.1 5.7 %collective-permute-start.4 = (bf16[256,256]{1,0:T(8,128)(2,1)S(1)}, bf16[256,256]{1,0:T(8,128)(2,1)S(1)}, u32[]{:S(2)}, u32[]{:S(2)}) collective-permute-start(bf16[256,256]{1,0:T(8,128)(2,1)S(1)} %get-tuple-element.114), channel_id=1, source_target_pairs={{8,72},{24,88},{40,104},{56,120},{72,8},{88,24},{104,40},{120,56},... | collective-permute-start | bytes 393224 | tf_op jit(solution)/shard_map/ppermute | solution.py:332
  40.9 6.3 %collective-permute-start.6 = (bf16[512,512]{1,0:T(8,128)(2,1)S(1)}, bf16[512,512]{1,0:T(8,128)(2,1)S(1)}, u32[]{:S(2)}, u32[]{:S(2)}) collective-permute-start(bf16[512,512]{1,0:T(8,128)(2,1)S(1)} %get-tuple-element.79), channel_id=1, source_target_pairs={{0,8},{8,0},{16,24},{24,16},{32,40},{40,32},{48,56},{56,48},{64,72... | collective-permute-start | bytes 1572872 | tf_op jit(solution)/shard_map/ppermute | solution.py:299
  45.3 1.9 %collective-permute-start.5 = (bf16[512,256]{1,0:T(8,128)(2,1)S(1)}, bf16[512,256]{1,0:T(8,128)(2,1)S(1)}, u32[]{:S(2)}, u32[]{:S(2)}) collective-permute-start(bf16[512,256]{1,0:T(8,128)(2,1)S(1)} %pad_maximum_fusion.1.near_ref), channel_id=1, source_target_pairs={{0,8},{8,0},{16,24},{24,16},{32,40},{40,32},{48,56},{56,48},{64,72... | collective-permute-start | bytes 786440 | tf_op jit(solution)/shard_map/ppermute | solution.py:299
  47.2 12.0 %collective-permute-start.7 = (bf16[512,512]{1,0:T(8,128)(2,1)S(1)}, bf16[512,512]{1,0:T(8,128)(2,1)S(1)}, u32[]{:S(2)}, u32[]{:S(2)}) collective-permute-start(bf16[512,512]{1,0:T(8,128)(2,1)S(1)} %bitcast.8), channel_id=1, source_target_pairs={{0,8},{8,0},{16,24},{24,16},{32,40},{40,32},{48,56},{56,48},{64,72... | collective-permute-start | bytes 1572872 | tf_op jit(solution)/shard_map/ppermute | solution.py:299
  92.8 19.1 %copy-start = (bf16[3584,512]{1,0:T(8,128)(2,1)S(1)}, bf16[3584,512]{1,0:T(8,128)(2,1)}, u32[]{:S(2)}) copy-start(bf16[3584,512]{1,0:T(8,128)(2,1)} %basis_ref.3) | copy-start | bytes 11010052
  108.2 5.7 %collective-permute-start.8 = (bf16[512,512]{1,0:T(8,128)(2,1)S(1)}, bf16[512,512]{1,0:T(8,128)(2,1)S(1)}, u32[]{:S(2)}, u32[]{:S(2)}) collective-permute-start(bf16[512,512]{1,0:T(8,128)(2,1)S(1)} %bitcast.10), channel_id=1, source_target_pairs={{0,8},{8,0},{16,24},{24,16},{32,40},{40,32},{48,56},{56,48},{64,72... | collective-permute-start | bytes 1572872 | tf_op jit(solution)/shard_map/ppermute | solution.py:299

commit v13 on v12

--- a/solution.py
+++ b/solution.py
@@ -318,18 +318,17 @@
     part, keep, send, got_x = lax.optimization_barrier((part, keep, send, got_x))
     part = over_planes(part)
     got_x = jnp.concatenate([got_x, lax.ppermute(send[:, early:], "dp", next_x[even])], axis=1)
-    near = jnp.concatenate([keep, got_x], axis=0)
-    got_y = lax.ppermute(near[:, half:], "dp", next_y[even])
-    part, keep, send, got_x, got_y, go_mine, go_theirs, me, owners = lax.optimization_barrier(
-        (part, keep, send, got_x, got_y, go_mine, go_theirs, me, owners)
+    part, keep, send, got_x, go_mine, go_theirs, me, owners = lax.optimization_barrier(
+        (part, keep, send, got_x, go_mine, go_theirs, me, owners)
     )
     part = part.reshape(planes, tok // planes, RANK)
     mine = jnp.sum(part.astype(f32), axis=0).astype(bf16)
     mine = jnp.broadcast_to(mine[None], part.shape).reshape(tok, RANK)
+    mine, send = lax.optimization_barrier((mine, send))
     coeffs = over_planes(mine)
     got_x = got_x + lax.ppermute(send, "dp", next_x[odd])
     near = jnp.concatenate([keep, got_x], axis=0)
-    got_y = got_y + lax.ppermute(near[:, half:], "dp", next_y[odd])
+    got_y = lax.ppermute(near[:, half:], "dp", next_y)
     near = jnp.concatenate([near[:, :half], got_y], axis=0)
     near, go_theirs = lax.optimization_barrier((near, go_theirs))
     far = other_core(near)

time: 116 us -> 111 us (0.957)
  starting transfers between devices: 39.5 us -> 34.8 us
    ppermute x2 -> x1, starting transfers between devices: 3.87 us -> 1.38 us  [body(): got_y = lax.ppermute(near[:, half:], 'dp', next_y)]
    ppermute x4, starting transfers between devices: 18.6 us -> 16.4 us  [other_core(): return lax.ppermute(x, 'dp', swap)]
    ppermute x2 -> x1, waiting for transfers between devices: 2.5 us -> 2.52 us  [body(): got_y = lax.ppermute(near[:, half:], 'dp', next_y)]
  transfers between devices with their start and end apart: 11 -> 10, of which waited for: 4 -> 4; matrix products, arithmetic and copies ran while one was open for 1% -> 0% of each run, Pallas kernels for 3% -> 3%
where the time goes in v13:
time: 111 us
  blocking collectives  47.8 us (43%)
  starting transfers between devices  34.8 us (31%)
  waiting for transfers between devices  16.5 us (15%)
  Pallas kernels  9.77 us (9%)
    all_to_all x2, blocking collectives, over_chips(): lax.all_to_all(x, 'dp', 0, 0, axis_index_groups=same_core, tiled=True)  35.2 us
    ppermute x4, starting transfers between devices, other_core(): return lax.ppermute(x, 'dp', swap)  16.4 us
    all_to_all x1, blocking collectives, over_planes(): return lax.all_to_all(x, 'mp', 0, 0, tiled=True)  12.6 us
    all_to_all x2, starting transfers between devices, over_planes(): return lax.all_to_all(x, 'mp', 0, 0, tiled=True)  12.5 us
    all_to_all x2, waiting for transfers between devices, over_planes(): return lax.all_to_all(x, 'mp', 0, 0, tiled=True)  11.6 us
    pallas_call x1, Pallas kernels, coeffs_call(): pl.pallas_call(coeffs_kernel, in_specs=[pl.BlockSpec(memory_space=pl.ANY)...  4.61 us
    ppermute x1, starting transfers between devices, body(): got_x = got_x + lax.ppermute(send, 'dp', next_x[odd])  3.11 us
    ppermute x1, waiting for transfers between devices, body(): got_y = lax.ppermute(near[:, half:], 'dp', next_y)  2.52 us
  transfers between devices with their start and end apart: 10, of which 4 were waited for; matrix products, arithmetic and copies ran while one was open for 0% of the time, Pallas kernels for 3%

profile of v13, /device:TPU:1, one launch (start us, length us, event | category | flops | bytes accessed | tf_op | source)
XLA Modules:
  0.0 110.9 jit_solution(3039727022541483842)
XLA Ops:
  0.7 4.6 %shard_map.85 = bf16[512,512]{1,0:T(8,128)(2,1)} custom-call(bf16[512,3584]{1,0:T(8,128)(2,1)} %hidden_ref.1, bf16[3584,512]{1,0:T(8,128)(2,1)} %basis_ref.3), custom_call_target="tpu_custom_call" | custom-call | tf_op jit(solution)/shard_map/pallas_call | solution.py:78
  5.3 0.1 shard_map.86
  5.5 0.7 collective-permute-start
  6.1 0.0 collective-permute-done
  6.2 9.0 %all-to-all-start = ((bf16[8,64,512]{2,1,0:T(8,128)(2,1)}), bf16[8,64,512]{2,1,0:T(8,128)(2,1)S(1)}, u32[]{:S(2)}, u32[]{:S(2)}) async-start(bf16[8,64,512]{2,1,0:T(8,128)(2,1)} %bitcast.17), calls=%async_computation | async-start | bytes 1048576 | tf_op jit(solution)/shard_map/all_to_all | solution.py:305
  15.2 0.7 collective-permute-start.1
  15.9 0.0 collective-permute-done.1
  15.9 11.6 %all-to-all-done = bf16[8,64,512]{2,1,0:T(8,128)(2,1)S(1)} async-done(((bf16[8,64,512]{2,1,0:T(8,128)(2,1)}), bf16[8,64,512]{2,1,0:T(8,128)(2,1)S(1)}, u32[]{:S(2)}, u32[]{:S(2)}) %all-to-all-start) | async-done | bytes 524320 | tf_op jit(solution)/shard_map/all_to_all | solution.py:305
  27.5 0.1 reduce_sum.12
  27.6 0.8 broadcast_in_dim.4
  28.4 3.1 %collective-permute-start.2 = (bf16[128,512]{1,0:T(8,128)(2,1)S(1)}, bf16[128,512]{1,0:T(8,128)(2,1)S(1)}, u32[]{:S(2)}, u32[]{:S(2)}) collective-permute-start(bf16[128,512]{1,0:T(8,128)(2,1)S(1)} %get-tuple-element.77), channel_id=1, source_target_pairs={{8,24},{24,8},{40,56},{56,40},{72,88},{88,72},{104,120},{120,104},... | collective-permute-start | bytes 393224 | tf_op jit(solution)/shard_map/ppermute | solution.py:329
  31.5 3.5 %all-to-all-start.1 = ((bf16[8,64,512]{2,1,0:T(8,128)(2,1)}), bf16[8,64,512]{2,1,0:T(8,128)(2,1)S(1)}, u32[]{:S(2)}, u32[]{:S(2)}) async-start(bf16[8,64,512]{2,1,0:T(8,128)(2,1)} %bitcast.6), calls=%async_computation.1 | async-start | bytes 1048576 | tf_op jit(solution)/shard_map/all_to_all | solution.py:305
  35.0 0.0 collective-permute-done.2
  35.1 1.4 %collective-permute-start.3 = (bf16[256,256]{1,0:T(8,128)(2,1)S(1)}, bf16[256,256]{1,0:T(8,128)(2,1)S(1)}, u32[]{:S(2)}, u32[]{:S(2)}) collective-permute-start(bf16[256,256]{1,0:T(8,128)(2,1)S(1)} %get-tuple-element.116), channel_id=1, source_target_pairs={{0,64},{8,72},{16,80},{24,88},{32,96},{40,104},{48,112},{56,120},{... | collective-permute-start | bytes 393224 | tf_op jit(solution)/shard_map/ppermute | solution.py:331
  36.5 2.5 %collective-permute-done.3 = bf16[256,256]{1,0:T(8,128)(2,1)S(1)} collective-permute-done((bf16[256,256]{1,0:T(8,128)(2,1)S(1)}, bf16[256,256]{1,0:T(8,128)(2,1)S(1)}, u32[]{:S(2)}, u32[]{:S(2)}) %collective-permute-start.3) | collective-permute-done | bytes 131104 | tf_op jit(solution)/shard_map/ppermute | solution.py:331
  39.0 5.9 %collective-permute-start.5 = (bf16[512,512]{1,0:T(8,128)(2,1)S(1)}, bf16[512,512]{1,0:T(8,128)(2,1)S(1)}, u32[]{:S(2)}, u32[]{:S(2)}) collective-permute-start(bf16[512,512]{1,0:T(8,128)(2,1)S(1)} %get-tuple-element.81), channel_id=1, source_target_pairs={{0,8},{8,0},{16,24},{24,16},{32,40},{40,32},{48,56},{56,48},{64,72... | collective-permute-start | bytes 1572872 | tf_op jit(solution)/shard_map/ppermute | solution.py:299
  44.9 0.1 collective-permute-start.4
  45.0 1.8 %collective-permute-done.4.far_ref = bf16[512,256]{1,0:T(8,128)(2,1)S(1)} collective-permute-done((bf16[512,256]{1,0:T(8,128)(2,1)S(1)}, bf16[512,256]{1,0:T(8,128)(2,1)S(1)}, u32[]{:S(2)}, u32[]{:S(2)}) %collective-permute-start.4) | collective-permute-done | bytes 262176 | tf_op jit(solution)/shard_map/ppermute | solution.py:299
  46.8 0.0 collective-permute-done.5.other_ref
  46.8 6.7 %collective-permute-start.6 = (bf16[512,512]{1,0:T(8,128)(2,1)S(1)}, bf16[512,512]{1,0:T(8,128)(2,1)S(1)}, u32[]{:S(2)}, u32[]{:S(2)}) collective-permute-start(bf16[512,512]{1,0:T(8,128)(2,1)S(1)} %bitcast.10), channel_id=1, source_target_pairs={{0,8},{8,0},{16,24},{24,16},{32,40},{40,32},{48,56},{56,48},{64,72... | collective-permute-start | bytes 1572872 | tf_op jit(solution)/shard_map/ppermute | solution.py:299
  53.5 0.9 shard_map.87
  54.5 0.6 collective-permute-done.6.co_other_ref
  55.1 0.5 shard_map.88
  55.5 19.9 %all_to_all.39.got_ref = bf16[16,48,512]{2,1,0:T(8,128)(2,1)S(1)} all-to-all(bf16[16,48,512]{2,1,0:T(8,128)(2,1)S(1)} %shard_map.88), channel_id=1, replica_groups={{0,16,32,48,64,80,96,112,128,144,160,176,192,208,224,240},{8,24,40,56,7..., dimensions={0} | all-to-all | bytes 1572864 | tf_op jit(solution)/shard_map/all_to_all | solution.py:302
  75.5 0.2 shard_map.89
  75.7 12.6 %all_to_all.40 = bf16[8,32,512]{2,1,0:T(8,128)(2,1)S(1)} all-to-all(bf16[8,32,512]{2,1,0:T(8,128)(2,1)S(1)} %get-tuple-element.99), channel_id=1, replica_groups=mesh['dp'=32,'mp'=8] {'mp'}, dimensions={0} | all-to-all | bytes 524288 | tf_op jit(solution)/shard_map/all_to_all | solution.py:305
  88.3 0.0 copy-start
  88.3 0.1 pad_maximum_fusion
  88.4 15.3 %all_to_all.41.last_ref = bf16[16,48,512]{2,1,0:T(8,128)(2,1)S(1)} all-to-all(bf16[16,48,512]{2,1,0:T(8,128)(2,1)S(1)} %pad_maximum_fusion), channel_id=1, replica_groups={{0,16,32,48,64,80,96,112,128,144,160,176,192,208,224,240},{8,24,40,56,7..., dimensions={0} | all-to-all | bytes 1572864 | tf_op jit(solution)/shard_map/all_to_all | solution.py:302
  103.7 3.7 %collective-permute-start.7 = (bf16[512,512]{1,0:T(8,128)(2,1)S(1)}, bf16[512,512]{1,0:T(8,128)(2,1)S(1)}, u32[]{:S(2)}, u32[]{:S(2)}) collective-permute-start(bf16[512,512]{1,0:T(8,128)(2,1)S(1)} %bitcast.12), channel_id=1, source_target_pairs={{0,8},{8,0},{16,24},{24,16},{32,40},{40,32},{48,56},{56,48},{64,72... | collective-permute-start | bytes 1572872 | tf_op jit(solution)/shard_map/ppermute | solution.py:299
  107.4 2.0 %shard_map.90 = bf16[3584,256]{1,0:T(8,128)(2,1)} custom-call(bf16[3584,512]{1,0:T(8,128)(2,1)S(1)} %copy-done, bf16[16,48,512]{2,1,0:T(8,128)(2,1)S(1)} %all_to_all.41.last_ref), custom_call_target="tpu_custom_call" | custom-call | tf_op jit(solution)/shard_map/pallas_call | solution.py:234
  109.5 1.4 %shard_map.91 = (f32[128,512]{1,0:T(8,128)}, f32[128,512]{1,0:T(8,128)}) custom-call(s32[1]{0:T(128)} %bitcast.me_ref, s32[1,32]{1,0:T(1,128)S(1)} %bitcast.16, f32[128,512]{1,0:T(8,128)S(1)} %copy-done.2, f32[128,512]{1,0:T(8,128)S(1)} %copy-done.3, bf16[512,512]{1,0:T(8,128)(2,1)S(1)} %bitcast.13, bf16[512,512]{1,0:T(8,128)(2,1)S(1)} %collective-permute-done.7.sums_other_ref), custom_call_target="tpu_custom_call" | custom-call | tf_op jit(solution)/shard_map/pallas_call | solution.py:386
  (19 shorter events, 0.2 us)
Async XLA Ops:
  0.6 4.7 %copy-start.1 = (bf16[512,1024]{1,0:T(8,128)(2,1)S(1)}, bf16[512,1024]{1,0:T(8,128)(2,1)}, u32[]{:S(2)}) copy-start(bf16[512,1024]{1,0:T(8,128)(2,1)} %go_ref) | copy-start | bytes 3145732
  0.6 4.7 %copy-start.2 = (f32[128,512]{1,0:T(8,128)S(1)}, f32[128,512]{1,0:T(8,128)}, u32[]{:S(2)}) copy-start(f32[128,512]{1,0:T(8,128)} %first_ref.1) | copy-start | bytes 786436
  0.7 4.7 %copy-start.3 = (f32[128,512]{1,0:T(8,128)S(1)}, f32[128,512]{1,0:T(8,128)}, u32[]{:S(2)}) copy-start(f32[128,512]{1,0:T(8,128)} %second_ref.1) | copy-start | bytes 786436
  5.5 0.7 collective-permute-start
  6.2 21.3 %all-to-all-start = ((bf16[8,64,512]{2,1,0:T(8,128)(2,1)}), bf16[8,64,512]{2,1,0:T(8,128)(2,1)S(1)}, u32[]{:S(2)}, u32[]{:S(2)}) async-start(bf16[8,64,512]{2,1,0:T(8,128)(2,1)} %bitcast.17), calls=%async_computation | async-start | bytes 1048576 | tf_op jit(solution)/shard_map/all_to_all | solution.py:305
  15.2 0.7 collective-permute-start.1
  27.5 26.1 %copy-start.4 = (s32[32,1]{0,1:T(1,128)S(1)}, s32[32,1]{0,1:T(1,128)}, u32[]{:S(2)}) copy-start(s32[32,1]{0,1:T(1,128)} %param.9) | copy-start | bytes 388
  28.4 6.6 %collective-permute-start.2 = (bf16[128,512]{1,0:T(8,128)(2,1)S(1)}, bf16[128,512]{1,0:T(8,128)(2,1)S(1)}, u32[]{:S(2)}, u32[]{:S(2)}) collective-permute-start(bf16[128,512]{1,0:T(8,128)(2,1)S(1)} %get-tuple-element.77), channel_id=1, source_target_pairs={{8,24},{24,8},{40,56},{56,40},{72,88},{88,72},{104,120},{120,104},... | collective-permute-start | bytes 393224 | tf_op jit(solution)/shard_map/ppermute | solution.py:329
  31.5 15.3 %all-to-all-start.1 = ((bf16[8,64,512]{2,1,0:T(8,128)(2,1)}), bf16[8,64,512]{2,1,0:T(8,128)(2,1)S(1)}, u32[]{:S(2)}, u32[]{:S(2)}) async-start(bf16[8,64,512]{2,1,0:T(8,128)(2,1)} %bitcast.6), calls=%async_computation.1 | async-start | bytes 1048576 | tf_op jit(solution)/shard_map/all_to_all | solution.py:305
  35.1 3.9 %collective-permute-start.3 = (bf16[256,256]{1,0:T(8,128)(2,1)S(1)}, bf16[256,256]{1,0:T(8,128)(2,1)S(1)}, u32[]{:S(2)}, u32[]{:S(2)}) collective-permute-start(bf16[256,256]{1,0:T(8,128)(2,1)S(1)} %get-tuple-element.116), channel_id=1, source_target_pairs={{0,64},{8,72},{16,80},{24,88},{32,96},{40,104},{48,112},{56,120},{... | collective-permute-start | bytes 393224 | tf_op jit(solution)/shard_map/ppermute | solution.py:331
  39.0 7.8 %collective-permute-start.5 = (bf16[512,512]{1,0:T(8,128)(2,1)S(1)}, bf16[512,512]{1,0:T(8,128)(2,1)S(1)}, u32[]{:S(2)}, u32[]{:S(2)}) collective-permute-start(bf16[512,512]{1,0:T(8,128)(2,1)S(1)} %get-tuple-element.81), channel_id=1, source_target_pairs={{0,8},{8,0},{16,24},{24,16},{32,40},{40,32},{48,56},{56,48},{64,72... | collective-permute-start | bytes 1572872 | tf_op jit(solution)/shard_map/ppermute | solution.py:299
  44.9 1.9 %collective-permute-start.4 = (bf16[512,256]{1,0:T(8,128)(2,1)S(1)}, bf16[512,256]{1,0:T(8,128)(2,1)S(1)}, u32[]{:S(2)}, u32[]{:S(2)}) collective-permute-start(bf16[512,256]{1,0:T(8,128)(2,1)S(1)} %pad_maximum_fusion.1.near_ref), channel_id=1, source_target_pairs={{0,8},{8,0},{16,24},{24,16},{32,40},{40,32},{48,56},{56,48},{64,72... | collective-permute-start | bytes 786440 | tf_op jit(solution)/shard_map/ppermute | solution.py:299
  46.8 8.3 %collective-permute-start.6 = (bf16[512,512]{1,0:T(8,128)(2,1)S(1)}, bf16[512,512]{1,0:T(8,128)(2,1)S(1)}, u32[]{:S(2)}, u32[]{:S(2)}) collective-permute-start(bf16[512,512]{1,0:T(8,128)(2,1)S(1)} %bitcast.10), channel_id=1, source_target_pairs={{0,8},{8,0},{16,24},{24,16},{32,40},{40,32},{48,56},{56,48},{64,72... | collective-permute-start | bytes 1572872 | tf_op jit(solution)/shard_map/ppermute | solution.py:299
  88.3 19.1 %copy-start = (bf16[3584,512]{1,0:T(8,128)(2,1)S(1)}, bf16[3584,512]{1,0:T(8,128)(2,1)}, u32[]{:S(2)}) copy-start(bf16[3584,512]{1,0:T(8,128)(2,1)} %basis_ref.3) | copy-start | bytes 11010052
  103.7 5.7 %collective-permute-start.7 = (bf16[512,512]{1,0:T(8,128)(2,1)S(1)}, bf16[512,512]{1,0:T(8,128)(2,1)S(1)}, u32[]{:S(2)}, u32[]{:S(2)}) collective-permute-start(bf16[512,512]{1,0:T(8,128)(2,1)S(1)} %bitcast.12), channel_id=1, source_target_pairs={{0,8},{8,0},{16,24},{24,16},{32,40},{40,32},{48,56},{56,48},{64,72... | collective-permute-start | bytes 1572872 | tf_op jit(solution)/shard_map/ppermute | solution.py:299

commit v14 on v13

--- a/solution.py
+++ b/solution.py
@@ -318,13 +318,12 @@
     part, keep, send, got_x = lax.optimization_barrier((part, keep, send, got_x))
     part = over_planes(part)
     got_x = jnp.concatenate([got_x, lax.ppermute(send[:, early:], "dp", next_x[even])], axis=1)
-    part, keep, send, got_x, go_mine, go_theirs, me, owners = lax.optimization_barrier(
-        (part, keep, send, got_x, go_mine, go_theirs, me, owners)
+    part, keep, got_x, go_mine, go_theirs, me, owners = lax.optimization_barrier(
+        (part, keep, got_x, go_mine, go_theirs, me, owners)
     )
     part = part.reshape(planes, tok // planes, RANK)
     mine = jnp.sum(part.astype(f32), axis=0).astype(bf16)
     mine = jnp.broadcast_to(mine[None], part.shape).reshape(tok, RANK)
-    mine, send = lax.optimization_barrier((mine, send))
     coeffs = over_planes(mine)
     got_x = got_x + lax.ppermute(send, "dp", next_x[odd])
     near = jnp.concatenate([keep, got_x], axis=0)

time: 111 us -> 110 us (level)
  waiting for transfers between devices: 16.5 us -> 13.4 us
  starting transfers between devices: 34.8 us -> 36.5 us
    all_to_all x2, waiting for transfers between devices: 11.6 us -> 8.45 us  [over_planes(): return lax.all_to_all(x, 'mp', 0, 0, tiled=True)]
    ppermute x4, starting transfers between devices: 16.4 us -> 18.2 us  [other_core(): return lax.ppermute(x, 'dp', swap)]
  transfers between devices with their start and end apart: 10 -> 10, of which waited for: 4 -> 4; matrix products, arithmetic and copies ran while one was open for 0% -> 1% of each run, Pallas kernels for 3% -> 3%
where the time goes in v14:
time: 110 us
  blocking collectives  48.2 us (44%)
  starting transfers between devices  36.5 us (33%)
  waiting for transfers between devices  13.4 us (12%)
  Pallas kernels  9.76 us (9%)
    all_to_all x2, blocking collectives, over_chips(): lax.all_to_all(x, 'dp', 0, 0, axis_index_groups=same_core, tiled=True)  35.6 us
    ppermute x4, starting transfers between devices, other_core(): return lax.ppermute(x, 'dp', swap)  18.2 us
    all_to_all x1, blocking collectives, over_planes(): return lax.all_to_all(x, 'mp', 0, 0, tiled=True)  12.6 us
    all_to_all x2, starting transfers between devices, over_planes(): return lax.all_to_all(x, 'mp', 0, 0, tiled=True)  12.5 us
    all_to_all x2, waiting for transfers between devices, over_planes(): return lax.all_to_all(x, 'mp', 0, 0, tiled=True)  8.45 us
    pallas_call x1, Pallas kernels, coeffs_call(): pl.pallas_call(coeffs_kernel, in_specs=[pl.BlockSpec(memory_space=pl.ANY)...  4.61 us
    ppermute x1, starting transfers between devices, body(): got_x = got_x + lax.ppermute(send, 'dp', next_x[odd])  3.12 us
    ppermute x1, waiting for transfers between devices, body(): got_y = lax.ppermute(near[:, half:], 'dp', next_y)  2.52 us
  transfers between devices with their start and end apart: 10, of which 4 were waited for; matrix products, arithmetic and copies ran while one was open for 1% of the time, Pallas kernels for 3%

profile of v14, /device:TPU:1, one launch (start us, length us, event | category | flops | bytes accessed | tf_op | source)
XLA Modules:
  0.0 109.9 jit_solution(14276121885372672660)
XLA Ops:
  0.7 4.6 %shard_map.85 = bf16[512,512]{1,0:T(8,128)(2,1)} custom-call(bf16[512,3584]{1,0:T(8,128)(2,1)} %hidden_ref.1, bf16[3584,512]{1,0:T(8,128)(2,1)} %basis_ref.3), custom_call_target="tpu_custom_call" | custom-call | tf_op jit(solution)/shard_map/pallas_call | solution.py:78
  5.3 0.1 shard_map.86
  5.5 0.7 collective-permute-start
  6.1 0.0 collective-permute-done
  6.2 9.0 %all-to-all-start = ((bf16[8,64,512]{2,1,0:T(8,128)(2,1)}), bf16[8,64,512]{2,1,0:T(8,128)(2,1)S(1)}, u32[]{:S(2)}, u32[]{:S(2)}) async-start(bf16[8,64,512]{2,1,0:T(8,128)(2,1)} %bitcast.15), calls=%async_computation | async-start | bytes 1048576 | tf_op jit(solution)/shard_map/all_to_all | solution.py:305
  15.2 0.7 collective-permute-start.1
  15.9 3.1 %collective-permute-start.2 = (bf16[128,512]{1,0:T(8,128)(2,1)S(1)}, bf16[128,512]{1,0:T(8,128)(2,1)S(1)}, u32[]{:S(2)}, u32[]{:S(2)}) collective-permute-start(bf16[128,512]{1,0:T(8,128)(2,1)S(1)} %get-tuple-element.66), channel_id=1, source_target_pairs={{8,24},{24,8},{40,56},{56,40},{72,88},{88,72},{104,120},{120,104},... | collective-permute-start | bytes 393224 | tf_op jit(solution)/shard_map/ppermute | solution.py:328
  19.0 0.0 collective-permute-done.1
  19.0 8.4 %all-to-all-done = bf16[8,64,512]{2,1,0:T(8,128)(2,1)S(1)} async-done(((bf16[8,64,512]{2,1,0:T(8,128)(2,1)}), bf16[8,64,512]{2,1,0:T(8,128)(2,1)S(1)}, u32[]{:S(2)}, u32[]{:S(2)}) %all-to-all-start) | async-done | bytes 524320 | tf_op jit(solution)/shard_map/all_to_all | solution.py:305
  27.5 0.1 reduce_sum.12
  27.6 0.8 broadcast_in_dim.4
  28.4 3.5 %all-to-all-start.1 = ((bf16[8,64,512]{2,1,0:T(8,128)(2,1)}), bf16[8,64,512]{2,1,0:T(8,128)(2,1)S(1)}, u32[]{:S(2)}, u32[]{:S(2)}) async-start(bf16[8,64,512]{2,1,0:T(8,128)(2,1)} %broadcast_in_dim.4), calls=%async_computation.1 | async-start | bytes 1048576 | tf_op jit(solution)/shard_map/all_to_all | solution.py:305
  31.9 0.0 collective-permute-done.2
  32.0 1.4 %collective-permute-start.3 = (bf16[256,256]{1,0:T(8,128)(2,1)S(1)}, bf16[256,256]{1,0:T(8,128)(2,1)S(1)}, u32[]{:S(2)}, u32[]{:S(2)}) collective-permute-start(bf16[256,256]{1,0:T(8,128)(2,1)S(1)} %get-tuple-element.110), channel_id=1, source_target_pairs={{0,64},{8,72},{16,80},{24,88},{32,96},{40,104},{48,112},{56,120},{... | collective-permute-start | bytes 393224 | tf_op jit(solution)/shard_map/ppermute | solution.py:330
  33.4 2.5 %collective-permute-done.3 = bf16[256,256]{1,0:T(8,128)(2,1)S(1)} collective-permute-done((bf16[256,256]{1,0:T(8,128)(2,1)S(1)}, bf16[256,256]{1,0:T(8,128)(2,1)S(1)}, u32[]{:S(2)}, u32[]{:S(2)}) %collective-permute-start.3) | collective-permute-done | bytes 131104 | tf_op jit(solution)/shard_map/ppermute | solution.py:330
  35.9 8.3 %collective-permute-start.5 = (bf16[512,512]{1,0:T(8,128)(2,1)S(1)}, bf16[512,512]{1,0:T(8,128)(2,1)S(1)}, u32[]{:S(2)}, u32[]{:S(2)}) collective-permute-start(bf16[512,512]{1,0:T(8,128)(2,1)S(1)} %get-tuple-element.75), channel_id=1, source_target_pairs={{0,8},{8,0},{16,24},{24,16},{32,40},{40,32},{48,56},{56,48},{64,72... | collective-permute-start | bytes 1572872 | tf_op jit(solution)/shard_map/ppermute | solution.py:299
  44.2 0.1 collective-permute-start.4
  44.3 1.8 %collective-permute-done.4.far_ref = bf16[512,256]{1,0:T(8,128)(2,1)S(1)} collective-permute-done((bf16[512,256]{1,0:T(8,128)(2,1)S(1)}, bf16[512,256]{1,0:T(8,128)(2,1)S(1)}, u32[]{:S(2)}, u32[]{:S(2)}) %collective-permute-start.4) | collective-permute-done | bytes 262176 | tf_op jit(solution)/shard_map/ppermute | solution.py:299
  46.1 6.0 %collective-permute-start.6 = (bf16[512,512]{1,0:T(8,128)(2,1)S(1)}, bf16[512,512]{1,0:T(8,128)(2,1)S(1)}, u32[]{:S(2)}, u32[]{:S(2)}) collective-permute-start(bf16[512,512]{1,0:T(8,128)(2,1)S(1)} %bitcast.8), channel_id=1, source_target_pairs={{0,8},{8,0},{16,24},{24,16},{32,40},{40,32},{48,56},{56,48},{64,72... | collective-permute-start | bytes 1572872 | tf_op jit(solution)/shard_map/ppermute | solution.py:299
  52.2 0.9 shard_map.87
  53.1 0.6 collective-permute-done.6.co_other_ref
  53.7 0.5 shard_map.88
  54.2 20.4 %all_to_all.36.got_ref = bf16[16,48,512]{2,1,0:T(8,128)(2,1)S(1)} all-to-all(bf16[16,48,512]{2,1,0:T(8,128)(2,1)S(1)} %shard_map.88), channel_id=1, replica_groups={{0,16,32,48,64,80,96,112,128,144,160,176,192,208,224,240},{8,24,40,56,7..., dimensions={0} | all-to-all | bytes 1572864 | tf_op jit(solution)/shard_map/all_to_all | solution.py:302
  74.6 0.2 shard_map.89
  74.7 12.6 %all_to_all.37 = bf16[8,32,512]{2,1,0:T(8,128)(2,1)S(1)} all-to-all(bf16[8,32,512]{2,1,0:T(8,128)(2,1)S(1)} %get-tuple-element.93), channel_id=1, replica_groups=mesh['dp'=32,'mp'=8] {'mp'}, dimensions={0} | all-to-all | bytes 524288 | tf_op jit(solution)/shard_map/all_to_all | solution.py:305
  87.4 0.0 copy-start
  87.4 0.1 pad_maximum_fusion
  87.5 15.3 %all_to_all.38.last_ref = bf16[16,48,512]{2,1,0:T(8,128)(2,1)S(1)} all-to-all(bf16[16,48,512]{2,1,0:T(8,128)(2,1)S(1)} %pad_maximum_fusion), channel_id=1, replica_groups={{0,16,32,48,64,80,96,112,128,144,160,176,192,208,224,240},{8,24,40,56,7..., dimensions={0} | all-to-all | bytes 1572864 | tf_op jit(solution)/shard_map/all_to_all | solution.py:302
  102.8 3.7 %collective-permute-start.7 = (bf16[512,512]{1,0:T(8,128)(2,1)S(1)}, bf16[512,512]{1,0:T(8,128)(2,1)S(1)}, u32[]{:S(2)}, u32[]{:S(2)}) collective-permute-start(bf16[512,512]{1,0:T(8,128)(2,1)S(1)} %bitcast.10), channel_id=1, source_target_pairs={{0,8},{8,0},{16,24},{24,16},{32,40},{40,32},{48,56},{56,48},{64,72... | collective-permute-start | bytes 1572872 | tf_op jit(solution)/shard_map/ppermute | solution.py:299
  106.5 2.0 %shard_map.90 = bf16[3584,256]{1,0:T(8,128)(2,1)} custom-call(bf16[3584,512]{1,0:T(8,128)(2,1)S(1)} %copy-done, bf16[16,48,512]{2,1,0:T(8,128)(2,1)S(1)} %all_to_all.38.last_ref), custom_call_target="tpu_custom_call" | custom-call | tf_op jit(solution)/shard_map/pallas_call | solution.py:234
  108.5 0.0 collective-permute-done.7.sums_other_ref
  108.5 1.4 %shard_map.91 = (f32[128,512]{1,0:T(8,128)}, f32[128,512]{1,0:T(8,128)}) custom-call(s32[1]{0:T(128)} %bitcast.me_ref, s32[1,32]{1,0:T(1,128)S(1)} %bitcast.14, f32[128,512]{1,0:T(8,128)S(1)} %copy-done.2, f32[128,512]{1,0:T(8,128)S(1)} %copy-done.3, bf16[512,512]{1,0:T(8,128)(2,1)S(1)} %bitcast.11, bf16[512,512]{1,0:T(8,128)(2,1)S(1)} %collective-permute-done.7.sums_other_ref), custom_call_target="tpu_custom_call" | custom-call | tf_op jit(solution)/shard_map/pallas_call | solution.py:385
  (19 shorter events, 0.2 us)
Async XLA Ops:
  0.6 4.7 %copy-start.1 = (bf16[512,1024]{1,0:T(8,128)(2,1)S(1)}, bf16[512,1024]{1,0:T(8,128)(2,1)}, u32[]{:S(2)}) copy-start(bf16[512,1024]{1,0:T(8,128)(2,1)} %go_ref) | copy-start | bytes 3145732
  0.6 4.7 %copy-start.2 = (f32[128,512]{1,0:T(8,128)S(1)}, f32[128,512]{1,0:T(8,128)}, u32[]{:S(2)}) copy-start(f32[128,512]{1,0:T(8,128)} %first_ref.1) | copy-start | bytes 786436
  0.7 4.7 %copy-start.3 = (f32[128,512]{1,0:T(8,128)S(1)}, f32[128,512]{1,0:T(8,128)}, u32[]{:S(2)}) copy-start(f32[128,512]{1,0:T(8,128)} %second_ref.1) | copy-start | bytes 786436
  5.5 0.7 collective-permute-start
  6.2 21.3 %all-to-all-start = ((bf16[8,64,512]{2,1,0:T(8,128)(2,1)}), bf16[8,64,512]{2,1,0:T(8,128)(2,1)S(1)}, u32[]{:S(2)}, u32[]{:S(2)}) async-start(bf16[8,64,512]{2,1,0:T(8,128)(2,1)} %bitcast.15), calls=%async_computation | async-start | bytes 1048576 | tf_op jit(solution)/shard_map/all_to_all | solution.py:305
  15.2 3.8 %collective-permute-start.1 = (bf16[128,384]{1,0:T(8,128)(2,1)S(1)}, bf16[128,384]{1,0:T(8,128)(2,1)S(1)}, u32[]{:S(2)}, u32[]{:S(2)}) collective-permute-start(bf16[128,384]{1,0:T(8,128)(2,1)S(1)} %slice.16), channel_id=1, source_target_pairs={{0,16},{16,0},{32,48},{48,32},{64,80},{80,64},{96,112},{112,96},{1... | collective-permute-start | bytes 294920 | tf_op jit(solution)/shard_map/ppermute | solution.py:320
  15.9 16.0 %collective-permute-start.2 = (bf16[128,512]{1,0:T(8,128)(2,1)S(1)}, bf16[128,512]{1,0:T(8,128)(2,1)S(1)}, u32[]{:S(2)}, u32[]{:S(2)}) collective-permute-start(bf16[128,512]{1,0:T(8,128)(2,1)S(1)} %get-tuple-element.66), channel_id=1, source_target_pairs={{8,24},{24,8},{40,56},{56,40},{72,88},{88,72},{104,120},{120,104},... | collective-permute-start | bytes 393224 | tf_op jit(solution)/shard_map/ppermute | solution.py:328
  27.5 24.7 %copy-start.4 = (s32[32,1]{0,1:T(1,128)S(1)}, s32[32,1]{0,1:T(1,128)}, u32[]{:S(2)}) copy-start(s32[32,1]{0,1:T(1,128)} %param.9) | copy-start | bytes 388
  28.4 17.7 %all-to-all-start.1 = ((bf16[8,64,512]{2,1,0:T(8,128)(2,1)}), bf16[8,64,512]{2,1,0:T(8,128)(2,1)S(1)}, u32[]{:S(2)}, u32[]{:S(2)}) async-start(bf16[8,64,512]{2,1,0:T(8,128)(2,1)} %broadcast_in_dim.4), calls=%async_computation.1 | async-start | bytes 1048576 | tf_op jit(solution)/shard_map/all_to_all | solution.py:305
  32.0 3.9 %collective-permute-start.3 = (bf16[256,256]{1,0:T(8,128)(2,1)S(1)}, bf16[256,256]{1,0:T(8,128)(2,1)S(1)}, u32[]{:S(2)}, u32[]{:S(2)}) collective-permute-start(bf16[256,256]{1,0:T(8,128)(2,1)S(1)} %get-tuple-element.110), channel_id=1, source_target_pairs={{0,64},{8,72},{16,80},{24,88},{32,96},{40,104},{48,112},{56,120},{... | collective-permute-start | bytes 393224 | tf_op jit(solution)/shard_map/ppermute | solution.py:330
  35.9 10.2 %collective-permute-start.5 = (bf16[512,512]{1,0:T(8,128)(2,1)S(1)}, bf16[512,512]{1,0:T(8,128)(2,1)S(1)}, u32[]{:S(2)}, u32[]{:S(2)}) collective-permute-start(bf16[512,512]{1,0:T(8,128)(2,1)S(1)} %get-tuple-element.75), channel_id=1, source_target_pairs={{0,8},{8,0},{16,24},{24,16},{32,40},{40,32},{48,56},{56,48},{64,72... | collective-permute-start | bytes 1572872 | tf_op jit(solution)/shard_map/ppermute | solution.py:299
  44.2 1.9 %collective-permute-start.4 = (bf16[512,256]{1,0:T(8,128)(2,1)S(1)}, bf16[512,256]{1,0:T(8,128)(2,1)S(1)}, u32[]{:S(2)}, u32[]{:S(2)}) collective-permute-start(bf16[512,256]{1,0:T(8,128)(2,1)S(1)} %pad_maximum_fusion.1.near_ref), channel_id=1, source_target_pairs={{0,8},{8,0},{16,24},{24,16},{32,40},{40,32},{48,56},{56,48},{64,72... | collective-permute-start | bytes 786440 | tf_op jit(solution)/shard_map/ppermute | solution.py:299
  46.1 7.6 %collective-permute-start.6 = (bf16[512,512]{1,0:T(8,128)(2,1)S(1)}, bf16[512,512]{1,0:T(8,128)(2,1)S(1)}, u32[]{:S(2)}, u32[]{:S(2)}) collective-permute-start(bf16[512,512]{1,0:T(8,128)(2,1)S(1)} %bitcast.8), channel_id=1, source_target_pairs={{0,8},{8,0},{16,24},{24,16},{32,40},{40,32},{48,56},{56,48},{64,72... | collective-permute-start | bytes 1572872 | tf_op jit(solution)/shard_map/ppermute | solution.py:299
  87.4 19.1 %copy-start = (bf16[3584,512]{1,0:T(8,128)(2,1)S(1)}, bf16[3584,512]{1,0:T(8,128)(2,1)}, u32[]{:S(2)}) copy-start(bf16[3584,512]{1,0:T(8,128)(2,1)} %basis_ref.3) | copy-start | bytes 11010052
  102.8 5.7 %collective-permute-start.7 = (bf16[512,512]{1,0:T(8,128)(2,1)S(1)}, bf16[512,512]{1,0:T(8,128)(2,1)S(1)}, u32[]{:S(2)}, u32[]{:S(2)}) collective-permute-start(bf16[512,512]{1,0:T(8,128)(2,1)S(1)} %bitcast.10), channel_id=1, source_target_pairs={{0,8},{8,0},{16,24},{24,16},{32,40},{40,32},{48,56},{56,48},{64,72... | collective-permute-start | bytes 1572872 | tf_op jit(solution)/shard_map/ppermute | solution.py:299

commit v15 on v14

--- a/solution.py
+++ b/solution.py
@@ -315,23 +315,22 @@
     )
     go_mine, go_theirs, keep, send = sort_call(me, grad_out, first, second)
     got_x = lax.ppermute(send[:, :early], "dp", next_x[even])
-    part, keep, send, got_x = lax.optimization_barrier((part, keep, send, got_x))
+    part, keep, send, got_x, go_theirs = lax.optimization_barrier((part, keep, send, got_x, go_theirs))
     part = over_planes(part)
+    go_other = other_core(go_theirs)
     got_x = jnp.concatenate([got_x, lax.ppermute(send[:, early:], "dp", next_x[even])], axis=1)
-    part, keep, got_x, go_mine, go_theirs, me, owners = lax.optimization_barrier(
-        (part, keep, got_x, go_mine, go_theirs, me, owners)
+    got_x = got_x + lax.ppermute(send, "dp", next_x[odd])
+    part, keep, got_x, go_mine, go_other, me, owners = lax.optimization_barrier(
+        (part, keep, got_x, go_mine, go_other, me, owners)
     )
     part = part.reshape(planes, tok // planes, RANK)
     mine = jnp.sum(part.astype(f32), axis=0).astype(bf16)
     mine = jnp.broadcast_to(mine[None], part.shape).reshape(tok, RANK)
     coeffs = over_planes(mine)
-    got_x = got_x + lax.ppermute(send, "dp", next_x[odd])
     near = jnp.concatenate([keep, got_x], axis=0)
     got_y = lax.ppermute(near[:, half:], "dp", next_y)
     near = jnp.concatenate([near[:, :half], got_y], axis=0)
-    near, go_theirs = lax.optimization_barrier((near, go_theirs))
     far = other_core(near)
-    go_other = other_core(go_theirs)
     coeffs, near, far, go_mine, go_other, me, owners = lax.optimization_barrier(
         (coeffs, near, far, go_mine, go_other, me, owners)
     )

time: 110 us -> 112 us (1.018)
  starting transfers between devices: 36.5 us -> 40.7 us
  waiting for transfers between devices: 13.4 us -> 10.9 us
    all_to_all x2, waiting for transfers between devices: 8.45 us -> 4.21 us  [over_planes(): return lax.all_to_all(x, 'mp', 0, 0, tiled=True)]
    all_to_all x2, starting transfers between devices: 12.5 us -> 16 us  [over_planes(): return lax.all_to_all(x, 'mp', 0, 0, tiled=True)]
    ppermute x1, waiting for transfers between devices: 0.01 us -> 2.38 us  [body(): got_x = got_x + lax.ppermute(send, 'dp', next_x[odd])]
  transfers between devices with their start and end apart: 10 -> 10, of which waited for: 4 -> 5; matrix products, arithmetic and copies ran while one was open for 1% -> 0% of each run, Pallas kernels for 3% -> 3%
where the time goes in v15:
time: 112 us
  blocking collectives  48.2 us (43%)
  starting transfers between devices  40.7 us (36%)
  waiting for transfers between devices  10.9 us (10%)
  Pallas kernels  9.76 us (9%)
    all_to_all x2, blocking collectives, over_chips(): lax.all_to_all(x, 'dp', 0, 0, axis_index_groups=same_core, tiled=True)  35.7 us
    ppermute x4, starting transfers between devices, other_core(): return lax.ppermute(x, 'dp', swap)  18.9 us
    all_to_all x2, starting transfers between devices, over_planes(): return lax.all_to_all(x, 'mp', 0, 0, tiled=True)  16 us
    all_to_all x1, blocking collectives, over_planes(): return lax.all_to_all(x, 'mp', 0, 0, tiled=True)  12.6 us
    pallas_call x1, Pallas kernels, coeffs_call(): pl.pallas_call(coeffs_kernel, in_specs=[pl.BlockSpec(memory_space=pl.ANY)...  4.61 us
    all_to_all x2, waiting for transfers between devices, over_planes(): return lax.all_to_all(x, 'mp', 0, 0, tiled=True)  4.21 us
    ppermute x1, starting transfers between devices, body(): got_x = got_x + lax.ppermute(send, 'dp', next_x[odd])  3.11 us
    ppermute x1, waiting for transfers between devices, body(): got_y = lax.ppermute(near[:, half:], 'dp', next_y)  2.52 us
  transfers between devices with their start and end apart: 10, of which 5 were waited for; matrix products, arithmetic and copies ran while one was open for 0% of the time, Pallas kernels for 3%

profile of v15, /device:TPU:1, one launch (start us, length us, event | category | flops | bytes accessed | tf_op | source)
XLA Modules:
  0.0 111.6 jit_solution(8696994757751647898)
XLA Ops:
  0.7 4.6 %shard_map.85 = bf16[512,512]{1,0:T(8,128)(2,1)} custom-call(bf16[512,3584]{1,0:T(8,128)(2,1)} %hidden_ref.1, bf16[3584,512]{1,0:T(8,128)(2,1)} %basis_ref.3), custom_call_target="tpu_custom_call" | custom-call | tf_op jit(solution)/shard_map/pallas_call | solution.py:78
  5.3 0.1 shard_map.86
  5.5 0.7 collective-permute-start
  6.1 0.0 collective-permute-done
  6.2 9.0 %all-to-all-start = ((bf16[8,64,512]{2,1,0:T(8,128)(2,1)}), bf16[8,64,512]{2,1,0:T(8,128)(2,1)S(1)}, u32[]{:S(2)}, u32[]{:S(2)}) async-start(bf16[8,64,512]{2,1,0:T(8,128)(2,1)} %bitcast.15), calls=%async_computation | async-start | bytes 1048576 | tf_op jit(solution)/shard_map/all_to_all | solution.py:305
  15.2 6.1 %collective-permute-start.3 = (bf16[512,512]{1,0:T(8,128)(2,1)S(1)}, bf16[512,512]{1,0:T(8,128)(2,1)S(1)}, u32[]{:S(2)}, u32[]{:S(2)}) collective-permute-start(bf16[512,512]{1,0:T(8,128)(2,1)S(1)} %get-tuple-element.68), channel_id=1, source_target_pairs={{0,8},{8,0},{16,24},{24,16},{32,40},{40,32},{48,56},{56,48},{64,72... | collective-permute-start | bytes 1572872 | tf_op jit(solution)/shard_map/ppermute | solution.py:299
  21.3 3.1 %collective-permute-start.2 = (bf16[128,512]{1,0:T(8,128)(2,1)S(1)}, bf16[128,512]{1,0:T(8,128)(2,1)S(1)}, u32[]{:S(2)}, u32[]{:S(2)}) collective-permute-start(bf16[128,512]{1,0:T(8,128)(2,1)S(1)} %get-tuple-element.66), channel_id=1, source_target_pairs={{8,24},{24,8},{40,56},{56,40},{72,88},{88,72},{104,120},{120,104},... | collective-permute-start | bytes 393224 | tf_op jit(solution)/shard_map/ppermute | solution.py:322
  24.4 0.7 collective-permute-start.1
  25.1 2.4 %collective-permute-done.2 = bf16[128,512]{1,0:T(8,128)(2,1)S(1)} collective-permute-done((bf16[128,512]{1,0:T(8,128)(2,1)S(1)}, bf16[128,512]{1,0:T(8,128)(2,1)S(1)}, u32[]{:S(2)}, u32[]{:S(2)}) %collective-permute-start.2) | collective-permute-done | bytes 131104 | tf_op jit(solution)/shard_map/ppermute | solution.py:322
  27.5 0.0 collective-permute-done.3.other_ref
  27.5 0.0 copy-start.4
  27.5 0.1 reduce_sum.12
  27.6 0.8 broadcast_in_dim.4
  28.4 6.9 %all-to-all-start.1 = ((bf16[8,64,512]{2,1,0:T(8,128)(2,1)}), bf16[8,64,512]{2,1,0:T(8,128)(2,1)S(1)}, u32[]{:S(2)}, u32[]{:S(2)}) async-start(bf16[8,64,512]{2,1,0:T(8,128)(2,1)} %broadcast_in_dim.4), calls=%async_computation.1 | async-start | bytes 1048576 | tf_op jit(solution)/shard_map/all_to_all | solution.py:305
  35.4 1.4 %collective-permute-start.4 = (bf16[256,256]{1,0:T(8,128)(2,1)S(1)}, bf16[256,256]{1,0:T(8,128)(2,1)S(1)}, u32[]{:S(2)}, u32[]{:S(2)}) collective-permute-start(bf16[256,256]{1,0:T(8,128)(2,1)S(1)} %get-tuple-element.108), channel_id=1, source_target_pairs={{0,64},{8,72},{16,80},{24,88},{32,96},{40,104},{48,112},{56,120},{... | collective-permute-start | bytes 393224 | tf_op jit(solution)/shard_map/ppermute | solution.py:331
  36.8 2.5 %collective-permute-done.4 = bf16[256,256]{1,0:T(8,128)(2,1)S(1)} collective-permute-done((bf16[256,256]{1,0:T(8,128)(2,1)S(1)}, bf16[256,256]{1,0:T(8,128)(2,1)S(1)}, u32[]{:S(2)}, u32[]{:S(2)}) %collective-permute-start.4) | collective-permute-done | bytes 131104 | tf_op jit(solution)/shard_map/ppermute | solution.py:331
  39.4 4.8 %collective-permute-start.5 = (bf16[512,256]{1,0:T(8,128)(2,1)S(1)}, bf16[512,256]{1,0:T(8,128)(2,1)S(1)}, u32[]{:S(2)}, u32[]{:S(2)}) collective-permute-start(bf16[512,256]{1,0:T(8,128)(2,1)S(1)} %pad_maximum_fusion.1.near_ref), channel_id=1, source_target_pairs={{0,8},{8,0},{16,24},{24,16},{32,40},{40,32},{48,56},{56,48},{64,72... | collective-permute-start | bytes 786440 | tf_op jit(solution)/shard_map/ppermute | solution.py:299
  44.2 1.2 %collective-permute-done.5.far_ref = bf16[512,256]{1,0:T(8,128)(2,1)S(1)} collective-permute-done((bf16[512,256]{1,0:T(8,128)(2,1)S(1)}, bf16[512,256]{1,0:T(8,128)(2,1)S(1)}, u32[]{:S(2)}, u32[]{:S(2)}) %collective-permute-start.5) | collective-permute-done | bytes 262176 | tf_op jit(solution)/shard_map/ppermute | solution.py:299
  45.4 4.2 %all-to-all-done.1 = bf16[8,64,512]{2,1,0:T(8,128)(2,1)S(1)} async-done(((bf16[8,64,512]{2,1,0:T(8,128)(2,1)}), bf16[8,64,512]{2,1,0:T(8,128)(2,1)S(1)}, u32[]{:S(2)}, u32[]{:S(2)}) %all-to-all-start.1) | async-done | bytes 524320 | tf_op jit(solution)/shard_map/all_to_all | solution.py:305
  49.6 4.3 %collective-permute-start.6 = (bf16[512,512]{1,0:T(8,128)(2,1)S(1)}, bf16[512,512]{1,0:T(8,128)(2,1)S(1)}, u32[]{:S(2)}, u32[]{:S(2)}) collective-permute-start(bf16[512,512]{1,0:T(8,128)(2,1)S(1)} %bitcast.8), channel_id=1, source_target_pairs={{0,8},{8,0},{16,24},{24,16},{32,40},{40,32},{48,56},{56,48},{64,72... | collective-permute-start | bytes 1572872 | tf_op jit(solution)/shard_map/ppermute | solution.py:299
  53.8 0.9 shard_map.87
  54.8 0.6 collective-permute-done.6.co_other_ref
  55.4 0.5 shard_map.88
  55.8 20.4 %all_to_all.36.got_ref = bf16[16,48,512]{2,1,0:T(8,128)(2,1)S(1)} all-to-all(bf16[16,48,512]{2,1,0:T(8,128)(2,1)S(1)} %shard_map.88), channel_id=1, replica_groups={{0,16,32,48,64,80,96,112,128,144,160,176,192,208,224,240},{8,24,40,56,7..., dimensions={0} | all-to-all | bytes 1572864 | tf_op jit(solution)/shard_map/all_to_all | solution.py:302
  76.2 0.2 shard_map.89
  76.4 12.6 %all_to_all.37 = bf16[8,32,512]{2,1,0:T(8,128)(2,1)S(1)} all-to-all(bf16[8,32,512]{2,1,0:T(8,128)(2,1)S(1)} %get-tuple-element.91), channel_id=1, replica_groups=mesh['dp'=32,'mp'=8] {'mp'}, dimensions={0} | all-to-all | bytes 524288 | tf_op jit(solution)/shard_map/all_to_all | solution.py:305
  89.0 0.0 copy-start
  89.1 0.1 pad_maximum_fusion
  89.1 15.3 %all_to_all.38.last_ref = bf16[16,48,512]{2,1,0:T(8,128)(2,1)S(1)} all-to-all(bf16[16,48,512]{2,1,0:T(8,128)(2,1)S(1)} %pad_maximum_fusion), channel_id=1, replica_groups={{0,16,32,48,64,80,96,112,128,144,160,176,192,208,224,240},{8,24,40,56,7..., dimensions={0} | all-to-all | bytes 1572864 | tf_op jit(solution)/shard_map/all_to_all | solution.py:302
  104.4 3.7 %collective-permute-start.7 = (bf16[512,512]{1,0:T(8,128)(2,1)S(1)}, bf16[512,512]{1,0:T(8,128)(2,1)S(1)}, u32[]{:S(2)}, u32[]{:S(2)}) collective-permute-start(bf16[512,512]{1,0:T(8,128)(2,1)S(1)} %bitcast.10), channel_id=1, source_target_pairs={{0,8},{8,0},{16,24},{24,16},{32,40},{40,32},{48,56},{56,48},{64,72... | collective-permute-start | bytes 1572872 | tf_op jit(solution)/shard_map/ppermute | solution.py:299
  108.2 2.0 %shard_map.90 = bf16[3584,256]{1,0:T(8,128)(2,1)} custom-call(bf16[3584,512]{1,0:T(8,128)(2,1)S(1)} %copy-done, bf16[16,48,512]{2,1,0:T(8,128)(2,1)S(1)} %all_to_all.38.last_ref), custom_call_target="tpu_custom_call" | custom-call | tf_op jit(solution)/shard_map/pallas_call | solution.py:234
  110.2 1.4 %shard_map.91 = (f32[128,512]{1,0:T(8,128)}, f32[128,512]{1,0:T(8,128)}) custom-call(s32[1]{0:T(128)} %bitcast.me_ref, s32[1,32]{1,0:T(1,128)S(1)} %bitcast.14, f32[128,512]{1,0:T(8,128)S(1)} %copy-done.2, f32[128,512]{1,0:T(8,128)S(1)} %copy-done.3, bf16[512,512]{1,0:T(8,128)(2,1)S(1)} %bitcast.11, bf16[512,512]{1,0:T(8,128)(2,1)S(1)} %collective-permute-done.7.sums_other_ref), custom_call_target="tpu_custom_call" | custom-call | tf_op jit(solution)/shard_map/pallas_call | solution.py:384
  (20 shorter events, 0.2 us)
Async XLA Ops:
  0.6 4.7 %copy-start.1 = (bf16[512,1024]{1,0:T(8,128)(2,1)S(1)}, bf16[512,1024]{1,0:T(8,128)(2,1)}, u32[]{:S(2)}) copy-start(bf16[512,1024]{1,0:T(8,128)(2,1)} %go_ref) | copy-start | bytes 3145732
  0.6 4.7 %copy-start.2 = (f32[128,512]{1,0:T(8,128)S(1)}, f32[128,512]{1,0:T(8,128)}, u32[]{:S(2)}) copy-start(f32[128,512]{1,0:T(8,128)} %first_ref.1) | copy-start | bytes 786436
  0.7 4.7 %copy-start.3 = (f32[128,512]{1,0:T(8,128)S(1)}, f32[128,512]{1,0:T(8,128)}, u32[]{:S(2)}) copy-start(f32[128,512]{1,0:T(8,128)} %second_ref.1) | copy-start | bytes 786436
  5.5 0.7 collective-permute-start
  6.2 21.3 %all-to-all-start = ((bf16[8,64,512]{2,1,0:T(8,128)(2,1)}), bf16[8,64,512]{2,1,0:T(8,128)(2,1)S(1)}, u32[]{:S(2)}, u32[]{:S(2)}) async-start(bf16[8,64,512]{2,1,0:T(8,128)(2,1)} %bitcast.15), calls=%async_computation | async-start | bytes 1048576 | tf_op jit(solution)/shard_map/all_to_all | solution.py:305
  15.2 12.3 %collective-permute-start.3 = (bf16[512,512]{1,0:T(8,128)(2,1)S(1)}, bf16[512,512]{1,0:T(8,128)(2,1)S(1)}, u32[]{:S(2)}, u32[]{:S(2)}) collective-permute-start(bf16[512,512]{1,0:T(8,128)(2,1)S(1)} %get-tuple-element.68), channel_id=1, source_target_pairs={{0,8},{8,0},{16,24},{24,16},{32,40},{40,32},{48,56},{56,48},{64,72... | collective-permute-start | bytes 1572872 | tf_op jit(solution)/shard_map/ppermute | solution.py:299
  21.3 6.2 %collective-permute-start.2 = (bf16[128,512]{1,0:T(8,128)(2,1)S(1)}, bf16[128,512]{1,0:T(8,128)(2,1)S(1)}, u32[]{:S(2)}, u32[]{:S(2)}) collective-permute-start(bf16[128,512]{1,0:T(8,128)(2,1)S(1)} %get-tuple-element.66), channel_id=1, source_target_pairs={{8,24},{24,8},{40,56},{56,40},{72,88},{88,72},{104,120},{120,104},... | collective-permute-start | bytes 393224 | tf_op jit(solution)/shard_map/ppermute | solution.py:322
  24.4 0.7 collective-permute-start.1
  27.5 26.3 %copy-start.4 = (s32[32,1]{0,1:T(1,128)S(1)}, s32[32,1]{0,1:T(1,128)}, u32[]{:S(2)}) copy-start(s32[32,1]{0,1:T(1,128)} %param.9) | copy-start | bytes 388
  28.4 21.1 %all-to-all-start.1 = ((bf16[8,64,512]{2,1,0:T(8,128)(2,1)}), bf16[8,64,512]{2,1,0:T(8,128)(2,1)S(1)}, u32[]{:S(2)}, u32[]{:S(2)}) async-start(bf16[8,64,512]{2,1,0:T(8,128)(2,1)} %broadcast_in_dim.4), calls=%async_computation.1 | async-start | bytes 1048576 | tf_op jit(solution)/shard_map/all_to_all | solution.py:305
  35.4 3.9 %collective-permute-start.4 = (bf16[256,256]{1,0:T(8,128)(2,1)S(1)}, bf16[256,256]{1,0:T(8,128)(2,1)S(1)}, u32[]{:S(2)}, u32[]{:S(2)}) collective-permute-start(bf16[256,256]{1,0:T(8,128)(2,1)S(1)} %get-tuple-element.108), channel_id=1, source_target_pairs={{0,64},{8,72},{16,80},{24,88},{32,96},{40,104},{48,112},{56,120},{... | collective-permute-start | bytes 393224 | tf_op jit(solution)/shard_map/ppermute | solution.py:331
  39.4 6.0 %collective-permute-start.5 = (bf16[512,256]{1,0:T(8,128)(2,1)S(1)}, bf16[512,256]{1,0:T(8,128)(2,1)S(1)}, u32[]{:S(2)}, u32[]{:S(2)}) collective-permute-start(bf16[512,256]{1,0:T(8,128)(2,1)S(1)} %pad_maximum_fusion.1.near_ref), channel_id=1, source_target_pairs={{0,8},{8,0},{16,24},{24,16},{32,40},{40,32},{48,56},{56,48},{64,72... | collective-permute-start | bytes 786440 | tf_op jit(solution)/shard_map/ppermute | solution.py:299
  49.6 5.8 %collective-permute-start.6 = (bf16[512,512]{1,0:T(8,128)(2,1)S(1)}, bf16[512,512]{1,0:T(8,128)(2,1)S(1)}, u32[]{:S(2)}, u32[]{:S(2)}) collective-permute-start(bf16[512,512]{1,0:T(8,128)(2,1)S(1)} %bitcast.8), channel_id=1, source_target_pairs={{0,8},{8,0},{16,24},{24,16},{32,40},{40,32},{48,56},{56,48},{64,72... | collective-permute-start | bytes 1572872 | tf_op jit(solution)/shard_map/ppermute | solution.py:299
  89.0 19.1 %copy-start = (bf16[3584,512]{1,0:T(8,128)(2,1)S(1)}, bf16[3584,512]{1,0:T(8,128)(2,1)}, u32[]{:S(2)}) copy-start(bf16[3584,512]{1,0:T(8,128)(2,1)} %basis_ref.3) | copy-start | bytes 11010052
  104.4 5.7 %collective-permute-start.7 = (bf16[512,512]{1,0:T(8,128)(2,1)S(1)}, bf16[512,512]{1,0:T(8,128)(2,1)S(1)}, u32[]{:S(2)}, u32[]{:S(2)}) collective-permute-start(bf16[512,512]{1,0:T(8,128)(2,1)S(1)} %bitcast.10), channel_id=1, source_target_pairs={{0,8},{8,0},{16,24},{24,16},{32,40},{40,32},{48,56},{56,48},{64,72... | collective-permute-start | bytes 1572872 | tf_op jit(solution)/shard_map/ppermute | solution.py:299

commit v16 on v14

--- a/solution.py
+++ b/solution.py
@@ -127,6 +127,31 @@
         compiler_params=kernel_params(),
         cost_estimate=pl.CostEstimate(flops=2**28, bytes_accessed=2**24, transcendentals=0),
     )(me, go, first, second)
+
+
+def spread_kernel(part_ref, out_ref, total, sems):
+    total[...] = jnp.sum(part_ref[...].astype(f32), axis=0).astype(bf16)
+    copies = [
+        pltpu.make_async_copy(total, out_ref.at[m], sems.at[m]) for m in range(out_ref.shape[0])
+    ]
+    for copy in copies:
+        copy.start()
+    for copy in copies:
+        copy.wait()
+
+
+def spread_call(part):
+    return pl.pallas_call(
+        spread_kernel,
+        in_specs=[VMEM],
+        out_specs=pl.BlockSpec(memory_space=pl.ANY),
+        out_shape=jax.ShapeDtypeStruct(part.shape, bf16),
+        scratch_shapes=[
+            pltpu.VMEM(part.shape[1:], bf16),
+            pltpu.SemaphoreType.DMA((part.shape[0],)),
+        ],
+        compiler_params=kernel_params(),
+    )(part)
 
 
 OVER_TOKENS = (((0,), (0,)), ((), ()))
@@ -321,9 +346,7 @@
     part, keep, got_x, go_mine, go_theirs, me, owners = lax.optimization_barrier(
         (part, keep, got_x, go_mine, go_theirs, me, owners)
     )
-    part = part.reshape(planes, tok // planes, RANK)
-    mine = jnp.sum(part.astype(f32), axis=0).astype(bf16)
-    mine = jnp.broadcast_to(mine[None], part.shape).reshape(tok, RANK)
+    mine = spread_call(part.reshape(planes, tok // planes, RANK)).reshape(tok, RANK)
     coeffs = over_planes(mine)
     got_x = got_x + lax.ppermute(send, "dp", next_x[odd])
     near = jnp.concatenate([keep, got_x], axis=0)

time: 110 us -> 110 us (level)
  transfers between devices with their start and end apart: 10 -> 10, of which waited for: 4 -> 4; matrix products, arithmetic and copies ran while one was open for 1% -> 0% of each run, Pallas kernels for 3% -> 4%
where the time goes in v16:
time: 110 us
  blocking collectives  48.2 us (44%)
  starting transfers between devices  36.5 us (33%)
  waiting for transfers between devices  13.4 us (12%)
  Pallas kernels  10.7 us (10%)
    all_to_all x2, blocking collectives, over_chips(): lax.all_to_all(x, 'dp', 0, 0, axis_index_groups=same_core, tiled=True)  35.6 us
    ppermute x4, starting transfers between devices, other_core(): return lax.ppermute(x, 'dp', swap)  18.2 us
    all_to_all x1, blocking collectives, over_planes(): return lax.all_to_all(x, 'mp', 0, 0, tiled=True)  12.6 us
    all_to_all x2, starting transfers between devices, over_planes(): return lax.all_to_all(x, 'mp', 0, 0, tiled=True)  12.5 us
    all_to_all x2, waiting for transfers between devices, over_planes(): return lax.all_to_all(x, 'mp', 0, 0, tiled=True)  8.44 us
    pallas_call x1, Pallas kernels, coeffs_call(): pl.pallas_call(coeffs_kernel, in_specs=[pl.BlockSpec(memory_space=pl.ANY)...  4.61 us
    ppermute x1, starting transfers between devices, body(): got_x = got_x + lax.ppermute(send, 'dp', next_x[odd])  3.12 us
    ppermute x1, waiting for transfers between devices, body(): got_y = lax.ppermute(near[:, half:], 'dp', next_y)  2.52 us
  transfers between devices with their start and end apart: 10, of which 4 were waited for; matrix products, arithmetic and copies ran while one was open for 0% of the time, Pallas kernels for 4%

profile of v16, /device:TPU:1, one launch (start us, length us, event | category | flops | bytes accessed | tf_op | source)
XLA Modules:
  0.0 110.0 jit_solution(5612418671945283212)
XLA Ops:
  0.7 4.6 %shard_map.85 = bf16[512,512]{1,0:T(8,128)(2,1)} custom-call(bf16[512,3584]{1,0:T(8,128)(2,1)} %hidden_ref.1, bf16[3584,512]{1,0:T(8,128)(2,1)} %basis_ref.3), custom_call_target="tpu_custom_call" | custom-call | tf_op jit(solution)/shard_map/pallas_call | solution.py:78
  5.3 0.1 shard_map.86
  5.5 0.7 collective-permute-start
  6.2 0.0 collective-permute-done
  6.2 9.0 %all-to-all-start = ((bf16[8,64,512]{2,1,0:T(8,128)(2,1)}), bf16[8,64,512]{2,1,0:T(8,128)(2,1)S(1)}, u32[]{:S(2)}, u32[]{:S(2)}) async-start(bf16[8,64,512]{2,1,0:T(8,128)(2,1)} %bitcast.15), calls=%async_computation | async-start | bytes 1048576 | tf_op jit(solution)/shard_map/all_to_all | solution.py:330
  15.2 0.7 collective-permute-start.1
  15.9 3.1 %collective-permute-start.2 = (bf16[128,512]{1,0:T(8,128)(2,1)S(1)}, bf16[128,512]{1,0:T(8,128)(2,1)S(1)}, u32[]{:S(2)}, u32[]{:S(2)}) collective-permute-start(bf16[128,512]{1,0:T(8,128)(2,1)S(1)} %get-tuple-element.66), channel_id=1, source_target_pairs={{8,24},{24,8},{40,56},{56,40},{72,88},{88,72},{104,120},{120,104},... | collective-permute-start | bytes 393224 | tf_op jit(solution)/shard_map/ppermute | solution.py:351
  19.0 0.0 collective-permute-done.1
  19.0 0.0 copy-start.4
  19.1 8.4 %all-to-all-done = bf16[8,64,512]{2,1,0:T(8,128)(2,1)S(1)} async-done(((bf16[8,64,512]{2,1,0:T(8,128)(2,1)}), bf16[8,64,512]{2,1,0:T(8,128)(2,1)S(1)}, u32[]{:S(2)}, u32[]{:S(2)}) %all-to-all-start) | async-done | bytes 524320 | tf_op jit(solution)/shard_map/all_to_all | solution.py:330
  27.5 0.9 shard_map.87
  28.4 3.5 %all-to-all-start.1 = ((bf16[8,64,512]{2,1,0:T(8,128)(2,1)}), bf16[8,64,512]{2,1,0:T(8,128)(2,1)S(1)}, u32[]{:S(2)}, u32[]{:S(2)}) async-start(bf16[8,64,512]{2,1,0:T(8,128)(2,1)} %shard_map.87), calls=%async_computation.1 | async-start | bytes 1048576 | tf_op jit(solution)/shard_map/all_to_all | solution.py:330
  32.0 1.4 %collective-permute-start.3 = (bf16[256,256]{1,0:T(8,128)(2,1)S(1)}, bf16[256,256]{1,0:T(8,128)(2,1)S(1)}, u32[]{:S(2)}, u32[]{:S(2)}) collective-permute-start(bf16[256,256]{1,0:T(8,128)(2,1)S(1)} %get-tuple-element.110), channel_id=1, source_target_pairs={{0,64},{8,72},{16,80},{24,88},{32,96},{40,104},{48,112},{56,120},{... | collective-permute-start | bytes 393224 | tf_op jit(solution)/shard_map/ppermute | solution.py:353
  33.4 2.5 %collective-permute-done.3 = bf16[256,256]{1,0:T(8,128)(2,1)S(1)} collective-permute-done((bf16[256,256]{1,0:T(8,128)(2,1)S(1)}, bf16[256,256]{1,0:T(8,128)(2,1)S(1)}, u32[]{:S(2)}, u32[]{:S(2)}) %collective-permute-start.3) | collective-permute-done | bytes 131104 | tf_op jit(solution)/shard_map/ppermute | solution.py:353
  35.9 8.3 %collective-permute-start.5 = (bf16[512,512]{1,0:T(8,128)(2,1)S(1)}, bf16[512,512]{1,0:T(8,128)(2,1)S(1)}, u32[]{:S(2)}, u32[]{:S(2)}) collective-permute-start(bf16[512,512]{1,0:T(8,128)(2,1)S(1)} %get-tuple-element.75), channel_id=1, source_target_pairs={{0,8},{8,0},{16,24},{24,16},{32,40},{40,32},{48,56},{56,48},{64,72... | collective-permute-start | bytes 1572872 | tf_op jit(solution)/shard_map/ppermute | solution.py:324
  44.2 0.1 collective-permute-start.4
  44.3 1.8 %collective-permute-done.4.far_ref = bf16[512,256]{1,0:T(8,128)(2,1)S(1)} collective-permute-done((bf16[512,256]{1,0:T(8,128)(2,1)S(1)}, bf16[512,256]{1,0:T(8,128)(2,1)S(1)}, u32[]{:S(2)}, u32[]{:S(2)}) %collective-permute-start.4) | collective-permute-done | bytes 262176 | tf_op jit(solution)/shard_map/ppermute | solution.py:324
  46.2 0.0 collective-permute-done.5.other_ref
  46.2 0.0 all-to-all-done.1
  46.2 6.0 %collective-permute-start.6 = (bf16[512,512]{1,0:T(8,128)(2,1)S(1)}, bf16[512,512]{1,0:T(8,128)(2,1)S(1)}, u32[]{:S(2)}, u32[]{:S(2)}) collective-permute-start(bf16[512,512]{1,0:T(8,128)(2,1)S(1)} %bitcast.8), channel_id=1, source_target_pairs={{0,8},{8,0},{16,24},{24,16},{32,40},{40,32},{48,56},{56,48},{64,72... | collective-permute-start | bytes 1572872 | tf_op jit(solution)/shard_map/ppermute | solution.py:324
  52.2 0.9 shard_map.88
  53.1 0.6 collective-permute-done.6.co_other_ref
  53.7 0.5 shard_map.89
  54.2 20.4 %all_to_all.36.got_ref = bf16[16,48,512]{2,1,0:T(8,128)(2,1)S(1)} all-to-all(bf16[16,48,512]{2,1,0:T(8,128)(2,1)S(1)} %shard_map.89), channel_id=1, replica_groups={{0,16,32,48,64,80,96,112,128,144,160,176,192,208,224,240},{8,24,40,56,7..., dimensions={0} | all-to-all | bytes 1572864 | tf_op jit(solution)/shard_map/all_to_all | solution.py:327
  74.6 0.2 shard_map.90
  74.8 12.6 %all_to_all.37 = bf16[8,32,512]{2,1,0:T(8,128)(2,1)S(1)} all-to-all(bf16[8,32,512]{2,1,0:T(8,128)(2,1)S(1)} %get-tuple-element.93), channel_id=1, replica_groups=mesh['dp'=32,'mp'=8] {'mp'}, dimensions={0} | all-to-all | bytes 524288 | tf_op jit(solution)/shard_map/all_to_all | solution.py:330
  87.4 0.0 copy-start
  87.4 0.1 pad_maximum_fusion
  87.5 15.3 %all_to_all.38.last_ref = bf16[16,48,512]{2,1,0:T(8,128)(2,1)S(1)} all-to-all(bf16[16,48,512]{2,1,0:T(8,128)(2,1)S(1)} %pad_maximum_fusion), channel_id=1, replica_groups={{0,16,32,48,64,80,96,112,128,144,160,176,192,208,224,240},{8,24,40,56,7..., dimensions={0} | all-to-all | bytes 1572864 | tf_op jit(solution)/shard_map/all_to_all | solution.py:327
  102.8 3.7 %collective-permute-start.7 = (bf16[512,512]{1,0:T(8,128)(2,1)S(1)}, bf16[512,512]{1,0:T(8,128)(2,1)S(1)}, u32[]{:S(2)}, u32[]{:S(2)}) collective-permute-start(bf16[512,512]{1,0:T(8,128)(2,1)S(1)} %bitcast.10), channel_id=1, source_target_pairs={{0,8},{8,0},{16,24},{24,16},{32,40},{40,32},{48,56},{56,48},{64,72... | collective-permute-start | bytes 1572872 | tf_op jit(solution)/shard_map/ppermute | solution.py:324
  106.5 2.0 %shard_map.91 = bf16[3584,256]{1,0:T(8,128)(2,1)} custom-call(bf16[3584,512]{1,0:T(8,128)(2,1)S(1)} %copy-done, bf16[16,48,512]{2,1,0:T(8,128)(2,1)S(1)} %all_to_all.38.last_ref), custom_call_target="tpu_custom_call" | custom-call | tf_op jit(solution)/shard_map/pallas_call | solution.py:259
  108.6 1.4 %shard_map.92 = (f32[128,512]{1,0:T(8,128)}, f32[128,512]{1,0:T(8,128)}) custom-call(s32[1]{0:T(128)} %bitcast.me_ref, s32[1,32]{1,0:T(1,128)S(1)} %bitcast.14, f32[128,512]{1,0:T(8,128)S(1)} %copy-done.2, f32[128,512]{1,0:T(8,128)S(1)} %copy-done.3, bf16[512,512]{1,0:T(8,128)(2,1)S(1)} %bitcast.11, bf16[512,512]{1,0:T(8,128)(2,1)S(1)} %collective-permute-done.7.sums_other_ref), custom_call_target="tpu_custom_call" | custom-call | tf_op jit(solution)/shard_map/pallas_call | solution.py:408
  (18 shorter events, 0.2 us)
Async XLA Ops:
  0.6 4.7 %copy-start.1 = (bf16[512,1024]{1,0:T(8,128)(2,1)S(1)}, bf16[512,1024]{1,0:T(8,128)(2,1)}, u32[]{:S(2)}) copy-start(bf16[512,1024]{1,0:T(8,128)(2,1)} %go_ref) | copy-start | bytes 3145732
  0.6 4.7 %copy-start.2 = (f32[128,512]{1,0:T(8,128)S(1)}, f32[128,512]{1,0:T(8,128)}, u32[]{:S(2)}) copy-start(f32[128,512]{1,0:T(8,128)} %first_ref.1) | copy-start | bytes 786436
  0.7 4.7 %copy-start.3 = (f32[128,512]{1,0:T(8,128)S(1)}, f32[128,512]{1,0:T(8,128)}, u32[]{:S(2)}) copy-start(f32[128,512]{1,0:T(8,128)} %second_ref.1) | copy-start | bytes 786436
  5.5 0.7 collective-permute-start
  6.2 21.3 %all-to-all-start = ((bf16[8,64,512]{2,1,0:T(8,128)(2,1)}), bf16[8,64,512]{2,1,0:T(8,128)(2,1)S(1)}, u32[]{:S(2)}, u32[]{:S(2)}) async-start(bf16[8,64,512]{2,1,0:T(8,128)(2,1)} %bitcast.15), calls=%async_computation | async-start | bytes 1048576 | tf_op jit(solution)/shard_map/all_to_all | solution.py:330
  15.2 3.8 %collective-permute-start.1 = (bf16[128,384]{1,0:T(8,128)(2,1)S(1)}, bf16[128,384]{1,0:T(8,128)(2,1)S(1)}, u32[]{:S(2)}, u32[]{:S(2)}) collective-permute-start(bf16[128,384]{1,0:T(8,128)(2,1)S(1)} %slice.16), channel_id=1, source_target_pairs={{0,16},{16,0},{32,48},{48,32},{64,80},{80,64},{96,112},{112,96},{1... | collective-permute-start | bytes 294920 | tf_op jit(solution)/shard_map/ppermute | solution.py:345
  15.9 16.1 %collective-permute-start.2 = (bf16[128,512]{1,0:T(8,128)(2,1)S(1)}, bf16[128,512]{1,0:T(8,128)(2,1)S(1)}, u32[]{:S(2)}, u32[]{:S(2)}) collective-permute-start(bf16[128,512]{1,0:T(8,128)(2,1)S(1)} %get-tuple-element.66), channel_id=1, source_target_pairs={{8,24},{24,8},{40,56},{56,40},{72,88},{88,72},{104,120},{120,104},... | collective-permute-start | bytes 393224 | tf_op jit(solution)/shard_map/ppermute | solution.py:351
  19.0 33.2 %copy-start.4 = (s32[32,1]{0,1:T(1,128)S(1)}, s32[32,1]{0,1:T(1,128)}, u32[]{:S(2)}) copy-start(s32[32,1]{0,1:T(1,128)} %param.9) | copy-start | bytes 388
  28.4 17.7 %all-to-all-start.1 = ((bf16[8,64,512]{2,1,0:T(8,128)(2,1)}), bf16[8,64,512]{2,1,0:T(8,128)(2,1)S(1)}, u32[]{:S(2)}, u32[]{:S(2)}) async-start(bf16[8,64,512]{2,1,0:T(8,128)(2,1)} %shard_map.87), calls=%async_computation.1 | async-start | bytes 1048576 | tf_op jit(solution)/shard_map/all_to_all | solution.py:330
  32.0 3.9 %collective-permute-start.3 = (bf16[256,256]{1,0:T(8,128)(2,1)S(1)}, bf16[256,256]{1,0:T(8,128)(2,1)S(1)}, u32[]{:S(2)}, u32[]{:S(2)}) collective-permute-start(bf16[256,256]{1,0:T(8,128)(2,1)S(1)} %get-tuple-element.110), channel_id=1, source_target_pairs={{0,64},{8,72},{16,80},{24,88},{32,96},{40,104},{48,112},{56,120},{... | collective-permute-start | bytes 393224 | tf_op jit(solution)/shard_map/ppermute | solution.py:353
  35.9 10.2 %collective-permute-start.5 = (bf16[512,512]{1,0:T(8,128)(2,1)S(1)}, bf16[512,512]{1,0:T(8,128)(2,1)S(1)}, u32[]{:S(2)}, u32[]{:S(2)}) collective-permute-start(bf16[512,512]{1,0:T(8,128)(2,1)S(1)} %get-tuple-element.75), channel_id=1, source_target_pairs={{0,8},{8,0},{16,24},{24,16},{32,40},{40,32},{48,56},{56,48},{64,72... | collective-permute-start | bytes 1572872 | tf_op jit(solution)/shard_map/ppermute | solution.py:324
  44.2 1.9 %collective-permute-start.4 = (bf16[512,256]{1,0:T(8,128)(2,1)S(1)}, bf16[512,256]{1,0:T(8,128)(2,1)S(1)}, u32[]{:S(2)}, u32[]{:S(2)}) collective-permute-start(bf16[512,256]{1,0:T(8,128)(2,1)S(1)} %pad_maximum_fusion.1.near_ref), channel_id=1, source_target_pairs={{0,8},{8,0},{16,24},{24,16},{32,40},{40,32},{48,56},{56,48},{64,72... | collective-permute-start | bytes 786440 | tf_op jit(solution)/shard_map/ppermute | solution.py:324
  46.2 7.6 %collective-permute-start.6 = (bf16[512,512]{1,0:T(8,128)(2,1)S(1)}, bf16[512,512]{1,0:T(8,128)(2,1)S(1)}, u32[]{:S(2)}, u32[]{:S(2)}) collective-permute-start(bf16[512,512]{1,0:T(8,128)(2,1)S(1)} %bitcast.8), channel_id=1, source_target_pairs={{0,8},{8,0},{16,24},{24,16},{32,40},{40,32},{48,56},{56,48},{64,72... | collective-permute-start | bytes 1572872 | tf_op jit(solution)/shard_map/ppermute | solution.py:324
  87.4 19.1 %copy-start = (bf16[3584,512]{1,0:T(8,128)(2,1)S(1)}, bf16[3584,512]{1,0:T(8,128)(2,1)}, u32[]{:S(2)}) copy-start(bf16[3584,512]{1,0:T(8,128)(2,1)} %basis_ref.3) | copy-start | bytes 11010052
  102.8 5.7 %collective-permute-start.7 = (bf16[512,512]{1,0:T(8,128)(2,1)S(1)}, bf16[512,512]{1,0:T(8,128)(2,1)S(1)}, u32[]{:S(2)}, u32[]{:S(2)}) collective-permute-start(bf16[512,512]{1,0:T(8,128)(2,1)S(1)} %bitcast.10), channel_id=1, source_target_pairs={{0,8},{8,0},{16,24},{24,16},{32,40},{40,32},{48,56},{56,48},{64,72... | collective-permute-start | bytes 1572872 | tf_op jit(solution)/shard_map/ppermute | solution.py:324
